TPU v7x, 32 devices: a whole 2x2x4 slice. The times are simulated.
32 devices in a mesh: groups: 2 (over y), frame: 8 (over z, x), row: 2 (over core).
Axes of the slice: x: 2, y: 2, z: 4, core: 2. Of those that a mesh axis runs over, the one named last changes fastest.
Arguments:
- latents: bfloat16 [16, 1024, 256], P(('groups', 'frame'), 'row'), parts along dimension 0, may hold values from -8 to 8
- ref_frames: int32 [16, 2], P(('groups', 'frame')), parts along dimension 0, may hold values from 0 to 7, as said below
- windows: int32 [16], P(('groups', 'frame')), parts along dimension 0, may hold values from 1 to 2, as said below
- quant_level: int32 [16], P(('groups', 'frame')), parts along dimension 0, may hold values from 0 to 63
- quant_scale: float32 [64, 256], replicated, may hold values from 0.5 to 2
- shared_proj: bfloat16 [256, 256], replicated, may hold values from -0.375 to 0.375
- value_proj: bfloat16 [256, 256], replicated, may hold values from -0.375 to 0.375
- output_proj: bfloat16 [256, 256], replicated, may hold values from -0.75 to 0.75
- conv_taps: bfloat16 [3, 256, 256], replicated, may hold values from -0.21875 to 0.21875
- cotangent: bfloat16 [16, 1024, 256], P(('groups', 'frame'), 'row'), parts along dimension 0, may hold values from -6 to 6
Outputs:
- coded_latent: bfloat16 [16, 1024, 256], P(('groups', 'frame'), 'row'), parts along dimension 0
- grad_latents: bfloat16 [16, 1024, 256], P(('groups', 'frame'), 'row'), parts along dimension 0
- grad_shared: float32 [512, 256], P('groups'), parts along dimension 0
- grad_values: float32 [512, 256], P('groups'), parts along dimension 0
- grad_output: float32 [512, 256], P('groups'), parts along dimension 0
- grad_taps: float32 [6, 256, 256], P('groups'), parts along dimension 0
There are 2 independent parts, one for each index of `groups`. A program takes and returns all parts, laid end to end along the dimension named above; an argument that names none is the same for every part. Nothing has to cross between parts.
Inputs may be any that keep to these rules, and one draw needn't show every extreme that they name: ref_frames[f, s] differs from f by a power of two no larger than 2 ** 2, and that largest distance occurs. `windows`: some frame has a window of 2 rows.
All inputs are finite; a program needn't handle non-finite values.
Results may differ from a plain program's by a relative error of at most 0.0045.
The roundings to bfloat16 on the way count: a program that leaves them out, or rounds other values in their place, can miss the bound.
Values may be sent and summed in bfloat16 or wider, within the bound.
No kernel may reach another device: no remote copies, remote signals or barrier semaphores. Data moves between devices by JAX's collectives and lax.ppermute only.
A program may use at most 128 MiB of HBM per device.

v0:
```python
import math

import jax
import jax.numpy as jnp
from jax import lax
from jax.sharding import PartitionSpec as P

HEADS = 8
DH = 32
COLS = 64
QROWS = 8
WMAX = 2
LEVELS = 3


SCORE_GAIN = 1.5
LAST_DIMS = (((1,), (1,)), ((), ()))
FIRST_DIMS = (((0,), (0,)), ((), ()))


def shifted_2(array, axis, by):
    devices = lax.axis_size(axis)
    pairs = [(i, i + by) for i in range(devices) if 0 <= i + by < devices]
    return lax.ppermute(array, axis, pairs)


def from_partner(value, axis, stride):
    mask = 2**stride
    pairs = [(source, source ^ mask) for source in range(lax.axis_size(axis))]
    return lax.ppermute(value, axis, pairs)


def with_halo(array, sides, width):
    for axis, dim in sides:
        devices, length = (lax.axis_size(axis), array.shape[dim])
        up = [(i, (i + 1) % devices) for i in range(devices - 1)]
        down = [(j, i) for i, j in up]
        last = lax.slice_in_dim(array, length - width, length, axis=dim)
        first = lax.slice_in_dim(array, 0, width, axis=dim)
        before = lax.ppermute(last, axis, up)
        after = lax.ppermute(first, axis, down)
        array = jnp.concatenate([before, array, after], axis=dim)
    return array


def split_heads(block):
    return jnp.transpose(block.reshape(block.shape[0], HEADS, DH), (1, 0, 2))


def merge_heads(block):
    return jnp.transpose(block, (1, 0, 2)).reshape(block.shape[1], HEADS * DH)


def head_weights(query_head, key_head, allowed):
    scores = jnp.dot(query_head, key_head.T, preferred_element_type=jnp.float32) * (
        SCORE_GAIN / math.sqrt(DH)
    )
    scores = jnp.where(allowed, scores, -jnp.inf)
    row_max = jnp.max(scores, axis=1, keepdims=True)
    exp_terms = jnp.where(allowed, jnp.exp(scores - row_max), 0.0)
    return exp_terms / jnp.sum(exp_terms, axis=1, keepdims=True)


def block_forward(query, keys, values, allowed):

    def one_head(head_parts):
        query_head, key_head, value_head = head_parts
        weights = head_weights(query_head, key_head, allowed)
        return jnp.dot(weights.astype(jnp.bfloat16), value_head, preferred_element_type=jnp.float32)

    result = lax.map(one_head, (split_heads(query), split_heads(keys), split_heads(values)))
    return merge_heads(result).astype(jnp.bfloat16)


def block_backward(query, keys, values, allowed, upstream):

    def one_head(head_parts):
        query_head, key_head, value_head, grad_head = head_parts
        weights = head_weights(query_head, key_head, allowed)
        prob = weights.astype(jnp.bfloat16)
        grad_prob = jnp.dot(grad_head, value_head.T, preferred_element_type=jnp.float32)
        value_grad = jnp.dot(prob.T, grad_head, preferred_element_type=jnp.float32)
        row_inner = jnp.sum(weights * grad_prob, axis=1, keepdims=True)
        grad_score = (weights * (grad_prob - row_inner) * (SCORE_GAIN / math.sqrt(DH))).astype(
            jnp.bfloat16
        )
        query_grad = jnp.dot(grad_score, key_head, preferred_element_type=jnp.float32)
        key_grad = jnp.dot(grad_score.T, query_head, preferred_element_type=jnp.float32)
        return (query_grad, key_grad, value_grad)

    query_grad, key_grad, value_grad = lax.map(
        one_head,
        (split_heads(query), split_heads(keys), split_heads(values), split_heads(upstream)),
    )
    return (merge_heads(query_grad), merge_heads(key_grad), merge_heads(value_grad))


def allowed_mask(begin_row, window, total_rows):
    key_span = QROWS + 2 * WMAX
    query_rows = begin_row + jnp.repeat(jnp.arange(QROWS, dtype=jnp.int32), COLS)
    key_rows = jnp.tile(
        jnp.repeat(begin_row - WMAX + jnp.arange(key_span, dtype=jnp.int32), COLS), 2
    )
    nearby = jnp.abs(query_rows[:, None] - key_rows[None, :]) <= window
    inside = (key_rows >= 0) & (key_rows < total_rows)
    return nearby & inside[None, :]


def add_window(summed, addend):
    return summed + addend


def against(left_side, weight):
    return lax.dot_general(left_side, weight, LAST_DIMS, preferred_element_type=jnp.float32)


def cross_rows(left_side, right_side):
    return lax.dot_general(left_side, right_side, FIRST_DIMS, preferred_element_type=jnp.float32)


def exact_against(left_side, weight):
    return lax.dot_general(
        left_side,
        weight.astype(jnp.float32),
        LAST_DIMS,
        precision=lax.Precision.HIGHEST,
        preferred_element_type=jnp.float32,
    )


def exact_cross(left_side, right_side):
    return lax.dot_general(
        left_side.astype(jnp.float32),
        right_side,
        FIRST_DIMS,
        precision=lax.Precision.HIGHEST,
        preferred_element_type=jnp.float32,
    )


def fetch_slots(payload, frame_id, own_refs, offsets):
    slot_data = jnp.zeros((2,) + payload.shape, payload.dtype)
    for offset in offsets:
        arrived = shifted_2(payload, "frame", offset)
        matched = (own_refs == frame_id - offset).reshape((2,) + (1,) * payload.ndim)
        slot_data = jnp.where(matched, arrived[None], slot_data)
    return slot_data


def return_slots(partials, frame_id, own_refs, offsets):
    summed = jnp.zeros(partials.shape[1:], jnp.float32)
    for offset in offsets:
        matched = (own_refs == frame_id - offset).reshape((2,) + (1,) * (partials.ndim - 1))
        outgoing = jnp.sum(jnp.where(matched, partials, 0.0), axis=0)
        summed = summed + shifted_2(outgoing, "frame", -offset)
    return summed


def fold_rims(extended, row_id, rows_dev):
    upper_rim = extended[:, :WMAX]
    middle = extended[:, WMAX : WMAX + rows_dev]
    lower_rim = extended[:, WMAX + rows_dev :]
    outgoing = jnp.where(row_id == 0, lower_rim, upper_rim)
    incoming = from_partner(outgoing.astype(jnp.bfloat16), "row", 0).astype(outgoing.dtype)
    filler = jnp.zeros((extended.shape[0], rows_dev - WMAX) + extended.shape[2:], extended.dtype)
    add_first = jnp.where(row_id == 0, 0.0, incoming)
    add_last = jnp.where(row_id == 0, incoming, 0.0)
    return (
        middle
        + jnp.concatenate([add_first, filler], axis=1)
        + jnp.concatenate([filler, add_last], axis=1)
    )


def local(
    latents,
    ref_frames,
    windows,
    quant_level,
    quant_scale,
    shared_proj,
    value_proj,
    output_proj,
    conv_taps,
    cotangent,
):
    width = latents.shape[2]
    rows_dev = latents.shape[1] // COLS
    total_rows = rows_dev * lax.axis_size("row")
    frame_id = lax.axis_index("frame")
    row_id = lax.axis_index("row")
    first_row = row_id * rows_dev
    own_refs = ref_frames[0]
    window = windows[0]
    key_span = QROWS + 2 * WMAX
    ext_rows = rows_dev + 2 * WMAX
    block_ids = jnp.arange(rows_dev // QROWS, dtype=jnp.int32)
    offsets = [direction * (1 << bit_level) for bit_level in range(LEVELS) for direction in (1, -1)]
    grid_shape = (rows_dev, COLS, width)
    tokens = latents[0]
    queries = jnp.dot(tokens, shared_proj, preferred_element_type=jnp.float32).astype(jnp.bfloat16)
    payload = tokens.reshape(grid_shape)
    extended = with_halo(payload, (("row", 0),), WMAX)
    slot_data = fetch_slots(extended, frame_id, own_refs, offsets)
    slot_flat = slot_data.reshape(-1, width)
    slot_keys = (
        jnp.dot(slot_flat, shared_proj, preferred_element_type=jnp.float32)
        .astype(jnp.bfloat16)
        .reshape(2, ext_rows, COLS, width)
    )
    slot_vals = (
        jnp.dot(slot_flat, value_proj, preferred_element_type=jnp.float32)
        .astype(jnp.bfloat16)
        .reshape(2, ext_rows, COLS, width)
    )
    query_grid = queries.reshape(grid_shape)

    def block_parts(block):
        begin_row = block * QROWS
        query = query_grid.reshape(-1, width)
        key_block = slot_keys.reshape(-1, width)
        value_block = slot_vals.reshape(-1, width)
        allowed = allowed_mask(first_row + begin_row, window, total_rows)
        return (query, key_block, value_block, allowed)

    def forward_block(block):
        query, key_block, value_block, allowed = block_parts(block)
        return block_forward(query, key_block, value_block, allowed)

    mixed_rows = lax.map(forward_block, block_ids).reshape(-1, width)
    residual = tokens.astype(jnp.float32) + jnp.dot(
        mixed_rows, output_proj, preferred_element_type=jnp.float32
    )
    hidden = residual.astype(jnp.bfloat16).reshape(grid_shape)
    hidden_ext = with_halo(hidden, (("row", 0),), 1)
    context = jnp.zeros_like(residual)
    for tap_shift in (-1, 0, 1):
        shifted = hidden_ext[1 + tap_shift : 1 + tap_shift + rows_dev].reshape(-1, width)
        context = context + jnp.dot(
            shifted, conv_taps[tap_shift + 1], preferred_element_type=jnp.float32
        )
    level_ids = jnp.arange(quant_scale.shape[0], dtype=jnp.int32)
    gain_row = jnp.sum(jnp.where((level_ids == quant_level[0])[:, None], quant_scale, 0.0), axis=0)
    coded_latent = ((residual + context) * gain_row[None, :]).astype(jnp.bfloat16)
    grad_z = cotangent[0].astype(jnp.float32) * gain_row[None, :]
    grad_zb = grad_z.astype(jnp.bfloat16)
    grad_ext = with_halo(grad_zb.reshape(grid_shape), (("row", 0),), 1)
    grad_resid = grad_z
    for tap_shift in (-1, 0, 1):
        shifted = grad_ext[1 - tap_shift : 1 - tap_shift + rows_dev].reshape(-1, width)
        grad_resid = grad_resid + against(shifted, conv_taps[tap_shift + 1])
    grad_rb = grad_resid.astype(jnp.bfloat16)
    grad_mixed = against(grad_rb, output_proj).astype(jnp.bfloat16).reshape(grid_shape)

    def backward_block(inner_sums, block):
        query_grad, key_grad, value_grad = inner_sums
        query, key_block, value_block, allowed = block_parts(block)
        begin_row = block * QROWS
        upstream = grad_mixed.reshape(-1, width)
        block_query, block_key, block_value = block_backward(
            query, key_block, value_block, allowed, upstream
        )
        query_grad = block_query.reshape(QROWS, COLS, width)
        key_grad = add_window(key_grad, block_key.reshape(2, key_span, COLS, width))
        value_grad = add_window(value_grad, block_value.reshape(2, key_span, COLS, width))
        return ((query_grad, key_grad, value_grad), None)

    initial = (
        jnp.zeros(grid_shape, jnp.float32),
        jnp.zeros((2, ext_rows, COLS, width), jnp.float32),
        jnp.zeros((2, ext_rows, COLS, width), jnp.float32),
    )
    (query_grad, key_grad, value_grad), _ = lax.scan(backward_block, initial, block_ids)
    query_grad = query_grad.reshape(-1, width)
    flat_keys = key_grad.reshape(-1, width)
    flat_vals = value_grad.reshape(-1, width)
    partials = (
        exact_against(flat_keys, shared_proj) + exact_against(flat_vals, value_proj)
    ).reshape(2, ext_rows, COLS, width)
    returned = fold_rims(
        return_slots(partials, frame_id, own_refs, offsets)[None], row_id, rows_dev
    )[0]
    returned = returned.reshape(-1, returned.shape[-1])
    grad_latents = grad_resid + exact_against(query_grad, shared_proj) + returned
    grad_shared = exact_cross(tokens, query_grad) + exact_cross(slot_flat, flat_keys)
    grad_values = exact_cross(slot_flat, flat_vals)
    grad_output = cross_rows(mixed_rows, grad_rb)
    grad_taps = jnp.stack(
        [
            cross_rows(
                hidden_ext[1 + tap_shift : 1 + tap_shift + rows_dev].reshape(-1, width), grad_zb
            )
            for tap_shift in (-1, 0, 1)
        ]
    )
    grad_shared, grad_values, grad_output, grad_taps = lax.psum(
        (grad_shared, grad_values, grad_output, grad_taps), ("frame", "row")
    )
    norm_scale = 1.0 / math.sqrt(lax.axis_size("frame") * total_rows * COLS)
    return (
        coded_latent.reshape(1, -1, width),
        grad_latents.astype(jnp.bfloat16).reshape(1, -1, width),
        grad_shared * norm_scale,
        grad_values * norm_scale,
        grad_output * norm_scale,
        grad_taps * norm_scale,
    )


def solution(mesh):
    placed = (
        P(("groups", "frame"), "row", None),
        P(("groups", "frame"), None),
        P(("groups", "frame")),
        P(("groups", "frame")),
        P(),
        P(),
        P(),
        P(),
        P(),
        P(("groups", "frame"), "row", None),
    )
    return jax.shard_map(
        local,
        mesh=mesh,
        in_specs=placed,
        out_specs=(
            P(("groups", "frame"), "row", None),
            P(("groups", "frame"), "row", None),
            P("groups", None),
            P("groups", None),
            P("groups", None),
            P("groups", None, None),
        ),
        check_vma=False,
    )
```

profile of v0, /device:TPU:0, one launch (start us, length us, event | category | flops | bytes accessed | tf_op | source)
XLA Modules:
  0.0 488.4 jit_solution(7931116638724330434)
XLA Ops:
  29.3 5.6 %collective-permute-start.7 = (bf16[12,64,256]{2,1,0:T(8,128)(2,1)}, bf16[12,64,256]{2,1,0:T(8,128)(2,1)}, u32[]{:S(2)}, u32[]{:S(2)}) collective-permute-start(bf16[12,64,256]{2,1,0:T(8,128)(2,1)} %pad_maximum_fusion.1), channel_id=1, source_target_pairs={{0,2},{2,4},{4,6},{6,8},{8,10},{10,12},{12,14},{1,3},{3,5},{5,7},{... | collective-permute-start | bytes 1179656 | tf_op jit(solution)/shard_map/ppermute | solution.py:24
  41.8 5.6 %collective-permute-start.5 = (bf16[12,64,256]{2,1,0:T(8,128)(2,1)}, bf16[12,64,256]{2,1,0:T(8,128)(2,1)}, u32[]{:S(2)}, u32[]{:S(2)}) collective-permute-start(bf16[12,64,256]{2,1,0:T(8,128)(2,1)} %pad_maximum_fusion.1), channel_id=1, source_target_pairs={{0,4},{2,6},{4,8},{6,10},{8,12},{10,14},{1,5},{3,7},{5,9},{7,11},{... | collective-permute-start | bytes 1179656 | tf_op jit(solution)/shard_map/ppermute | solution.py:24
  48.6 5.6 %collective-permute-start.3 = (bf16[12,64,256]{2,1,0:T(8,128)(2,1)}, bf16[12,64,256]{2,1,0:T(8,128)(2,1)}, u32[]{:S(2)}, u32[]{:S(2)}) collective-permute-start(bf16[12,64,256]{2,1,0:T(8,128)(2,1)} %pad_maximum_fusion.1), channel_id=1, source_target_pairs={{0,8},{2,10},{4,12},{6,14},{1,9},{3,11},{5,13},{7,15},{16,24},{18,... | collective-permute-start | bytes 1179656 | tf_op jit(solution)/shard_map/ppermute | solution.py:24
  59.2 3.8 collective-permute-done.4
  64.7 16.2 %collective-permute-done.2 = bf16[12,64,256]{2,1,0:T(8,128)(2,1)} collective-permute-done((bf16[12,64,256]{2,1,0:T(8,128)(2,1)}, bf16[12,64,256]{2,1,0:T(8,128)(2,1)}, u32[]{:S(2)}, u32[]{:S(2)}) %collective-permute-start.2) | collective-permute-done | bytes 393248 | tf_op jit(solution)/shard_map/ppermute | solution.py:24
  86.4 3.7 copy.18
  92.9 73.0 %while.46 = (s32[]{:T(128)}, bf16[8,512,32]{1,2,0:T(8,128)(2,1)}, bf16[8,512,32]{2,1,0:T(8,128)(2,1)}, bf16[8,1536,32]{2,1,0:T(8,128)(2,1)}, bf16[8,1536,32]{2,1...) while((s32[]{:T(128)}, bf16[8,512,32]{1,2,0:T(8,128)(2,1)}, ...), condition=%wide.region_3.4_spmd.clone.clone, body=%wide.region_0.3_spmd.clone.sunk.clone | while | flops 117963776 | bytes 10462825 | solution.py:71
  98.1 3.9 fusion.159
  107.3 3.9 fusion.159
  116.4 3.9 fusion.159
  125.5 3.9 fusion.159
  134.6 3.9 fusion.159
  143.7 3.9 fusion.159
  152.8 3.9 fusion.159
  161.9 3.9 fusion.159
  169.9 145.0 %while.47 = (s32[]{:T(128)}, f32[8,512,32]{1,2,0:T(8,128)S(1)}, f32[8,1536,32]{1,2,0:T(8,128)}, f32[8,1536,32]{1,2,0:T(8,128)S(1)}, bf16[8,512,32]{2,1,0:T(8,128...) while((s32[]{:T(128)}, f32[8,512,32]{1,2,0:T(8,128)S(1)}, ...), condition=%wide.region_9.10_spmd.clone.clone, body=%wide.region_5.9_spmd.clone.sunk.clone | while | flops 284686848 | bytes 28981892 | solution.py:91
  178.3 3.5 multiply_reduce_fusion.3
  196.4 3.5 multiply_reduce_fusion.3
  232.7 3.5 multiply_reduce_fusion.3
  250.8 3.5 multiply_reduce_fusion.3
  342.0 6.4 %collective-permute-done.13 = f32[12,64,256]{2,1,0:T(8,128)S(1)} collective-permute-done((f32[12,64,256]{2,1,0:T(8,128)S(1)}, f32[12,64,256]{2,1,0:T(8,128)S(1)}, u32[]{:S(2)}, u32[]{:S(2)}) %collective-permute-start.13) | collective-permute-done | bytes 786464 | tf_op jit(solution)/shard_map/ppermute | solution.py:24
  354.4 20.1 %collective-permute-done.16 = f32[12,64,256]{2,1,0:T(8,128)} collective-permute-done((f32[12,64,256]{2,1,0:T(8,128)}, f32[12,64,256]{2,1,0:T(8,128)}, u32[]{:S(2)}, u32[]{:S(2)}) %collective-permute-start.16) | collective-permute-done | bytes 786464 | tf_op jit(solution)/shard_map/ppermute | solution.py:24
  374.5 11.0 %collective-permute-done.14 = f32[12,64,256]{2,1,0:T(8,128)} collective-permute-done((f32[12,64,256]{2,1,0:T(8,128)}, f32[12,64,256]{2,1,0:T(8,128)}, u32[]{:S(2)}, u32[]{:S(2)}) %collective-permute-start.14) | collective-permute-done | bytes 786464 | tf_op jit(solution)/shard_map/ppermute | solution.py:24
  388.1 85.4 %all-reduce.5.cloned.1.call-done = (f32[256,256]{0,1:T(8,128)}, f32[256,256]{0,1:T(8,128)}, f32[256,256]{0,1:T(8,128)}, f32[3,256,256]{2,1,0:T(8,128)}) async-done(((f32[256,256]{0,1:T(8,128)}, f32[256,256]{0,1:T(8,128)}, f32[256,256]{0,1:T(8,128)}, f32[3,256,256]{2,1,0:T(8,128)}), (f32[256,256]{0,1:T(8,128)}, f32[256,256]{0,1:T(8,128)}, f32[256,256]{0,1:T(8,128)}, ...) | async-done | bytes 1572880 | tf_op jit(solution)/shard_map/psum | solution.py:296
  (225 shorter events, 264.2 us)
Async XLA Ops:
  7.2 21.3 %copy-start.3 = (bf16[1,512,256]{2,1,0:T(8,128)(2,1)S(1)}, bf16[1,512,256]{2,1,0:T(8,128)(2,1)}, u32[]{:S(2)}) copy-start(bf16[1,512,256]{2,1,0:T(8,128)(2,1)} %param.14) | copy-start | bytes 786436
  7.2 466.3 %all-reduce.5.cloned.1.call-start = ((), (), s32[]{:S(2)}) async-start(), calls=%async_computation | async-start | bytes 3145728 | tf_op jit(solution)/shard_map/psum | solution.py:296
  8.2 31.1 %copy-start.1 = (bf16[1,512,256]{2,1,0:T(8,128)(2,1)S(1)}, bf16[1,512,256]{2,1,0:T(8,128)(2,1)}, u32[]{:S(2)}) copy-start(bf16[1,512,256]{2,1,0:T(8,128)(2,1)} %param.23) | copy-start | bytes 786436
  8.2 20.3 %collective-permute-start.1 = (bf16[2,64,256]{2,1,0:T(8,128)(2,1)S(1)}, bf16[2,64,256]{2,1,0:T(8,128)(2,1)S(1)}, u32[]{:S(2)}, u32[]{:S(2)}) collective-permute-start(bf16[2,64,256]{2,1,0:T(8,128)(2,1)S(1)} %bitcast.292), channel_id=1, source_target_pairs={{1,0},{3,2},{5,4},{7,6},{9,8},{11,10},{13,12},{15,14},{17,16},{19,... | collective-permute-start | bytes 196616 | tf_op jit(solution)/shard_map/ppermute | solution.py:41
  9.6 18.9 %collective-permute-start = (bf16[2,64,256]{2,1,0:T(8,128)(2,1)S(1)}, bf16[2,64,256]{2,1,0:T(8,128)(2,1)S(1)}, u32[]{:S(2)}, u32[]{:S(2)}) collective-permute-start(bf16[2,64,256]{2,1,0:T(8,128)(2,1)S(1)} %bitcast.291), channel_id=1, source_target_pairs={{0,1},{2,3},{4,5},{6,7},{8,9},{10,11},{12,13},{14,15},{16,17},{18,... | collective-permute-start | bytes 196616 | tf_op jit(solution)/shard_map/ppermute | solution.py:40
  16.6 21.9 %collective-permute-start.11 = (bf16[1,64,256]{2,1,0:T(8,128)(2,1)}, bf16[1,64,256]{2,1,0:T(8,128)(2,1)}, u32[]{:S(2)}, u32[]{:S(2)}) collective-permute-start(bf16[1,64,256]{2,1,0:T(8,128)(2,1)} %get-tuple-element.261), channel_id=1, source_target_pairs={{0,1},{2,3},{4,5},{6,7},{8,9},{10,11},{12,13},{14,15},{16,17},{18,... | collective-permute-start | bytes 98312 | tf_op jit(solution)/shard_map/ppermute | solution.py:40
  18.5 20.0 %collective-permute-start.10 = (bf16[1,64,256]{2,1,0:T(8,128)(2,1)}, bf16[1,64,256]{2,1,0:T(8,128)(2,1)}, u32[]{:S(2)}, u32[]{:S(2)}) collective-permute-start(bf16[1,64,256]{2,1,0:T(8,128)(2,1)} %get-tuple-element.262), channel_id=1, source_target_pairs={{1,0},{3,2},{5,4},{7,6},{9,8},{11,10},{13,12},{15,14},{17,16},{19,... | collective-permute-start | bytes 98312 | tf_op jit(solution)/shard_map/ppermute | solution.py:41
  29.3 24.9 %collective-permute-start.7 = (bf16[12,64,256]{2,1,0:T(8,128)(2,1)}, bf16[12,64,256]{2,1,0:T(8,128)(2,1)}, u32[]{:S(2)}, u32[]{:S(2)}) collective-permute-start(bf16[12,64,256]{2,1,0:T(8,128)(2,1)} %pad_maximum_fusion.1), channel_id=1, source_target_pairs={{0,2},{2,4},{4,6},{6,8},{8,10},{10,12},{12,14},{1,3},{3,5},{5,7},{... | collective-permute-start | bytes 1179656 | tf_op jit(solution)/shard_map/ppermute | solution.py:24
  40.5 18.7 %collective-permute-start.6 = (bf16[12,64,256]{2,1,0:T(8,128)(2,1)}, bf16[12,64,256]{2,1,0:T(8,128)(2,1)}, u32[]{:S(2)}, u32[]{:S(2)}) collective-permute-start(bf16[12,64,256]{2,1,0:T(8,128)(2,1)} %pad_maximum_fusion.1), channel_id=1, source_target_pairs={{2,0},{4,2},{6,4},{8,6},{10,8},{12,10},{14,12},{3,1},{5,3},{7,5},{... | collective-permute-start | bytes 1179656 | tf_op jit(solution)/shard_map/ppermute | solution.py:24
  41.8 17.4 %collective-permute-start.5 = (bf16[12,64,256]{2,1,0:T(8,128)(2,1)}, bf16[12,64,256]{2,1,0:T(8,128)(2,1)}, u32[]{:S(2)}, u32[]{:S(2)}) collective-permute-start(bf16[12,64,256]{2,1,0:T(8,128)(2,1)} %pad_maximum_fusion.1), channel_id=1, source_target_pairs={{0,4},{2,6},{4,8},{6,10},{8,12},{10,14},{1,5},{3,7},{5,9},{7,11},{... | collective-permute-start | bytes 1179656 | tf_op jit(solution)/shard_map/ppermute | solution.py:24
  47.4 15.7 %collective-permute-start.4 = (bf16[12,64,256]{2,1,0:T(8,128)(2,1)}, bf16[12,64,256]{2,1,0:T(8,128)(2,1)}, u32[]{:S(2)}, u32[]{:S(2)}) collective-permute-start(bf16[12,64,256]{2,1,0:T(8,128)(2,1)} %pad_maximum_fusion.1), channel_id=1, source_target_pairs={{4,0},{6,2},{8,4},{10,6},{12,8},{14,10},{5,1},{7,3},{9,5},{11,7},{... | collective-permute-start | bytes 1179656 | tf_op jit(solution)/shard_map/ppermute | solution.py:24
  48.6 16.1 %collective-permute-start.3 = (bf16[12,64,256]{2,1,0:T(8,128)(2,1)}, bf16[12,64,256]{2,1,0:T(8,128)(2,1)}, u32[]{:S(2)}, u32[]{:S(2)}) collective-permute-start(bf16[12,64,256]{2,1,0:T(8,128)(2,1)} %pad_maximum_fusion.1), channel_id=1, source_target_pairs={{0,8},{2,10},{4,12},{6,14},{1,9},{3,11},{5,13},{7,15},{16,24},{18,... | collective-permute-start | bytes 1179656 | tf_op jit(solution)/shard_map/ppermute | solution.py:24
  54.3 26.6 %collective-permute-start.2 = (bf16[12,64,256]{2,1,0:T(8,128)(2,1)}, bf16[12,64,256]{2,1,0:T(8,128)(2,1)}, u32[]{:S(2)}, u32[]{:S(2)}) collective-permute-start(bf16[12,64,256]{2,1,0:T(8,128)(2,1)} %pad_maximum_fusion.1), channel_id=1, source_target_pairs={{8,0},{10,2},{12,4},{14,6},{9,1},{11,3},{13,5},{15,7},{24,16},{26,... | collective-permute-start | bytes 1179656 | tf_op jit(solution)/shard_map/ppermute | solution.py:24
  92.9 77.0 %copy-start.4 = (f32[8,512,32]{1,2,0:T(8,128)S(1)}, f32[8,512,32]{1,2,0:T(8,128)}, u32[]{:S(2)}) copy-start(f32[8,512,32]{1,2,0:T(8,128)} %custom-call.2) | copy-start | bytes 1572868
  323.2 15.2 %collective-permute-start.8 = (bf16[1,64,256]{2,1,0:T(8,128)(2,1)S(1)}, bf16[1,64,256]{2,1,0:T(8,128)(2,1)S(1)}, u32[]{:S(2)}, u32[]{:S(2)}) collective-permute-start(bf16[1,64,256]{2,1,0:T(8,128)(2,1)S(1)} %get-tuple-element.265), channel_id=1, source_target_pairs={{0,1},{2,3},{4,5},{6,7},{8,9},{10,11},{12,13},{14,15},{16,17},{18,... | collective-permute-start | bytes 98312 | tf_op jit(solution)/shard_map/ppermute | solution.py:40
  325.3 15.3 %collective-permute-start.9 = (bf16[1,64,256]{2,1,0:T(8,128)(2,1)S(1)}, bf16[1,64,256]{2,1,0:T(8,128)(2,1)S(1)}, u32[]{:S(2)}, u32[]{:S(2)}) collective-permute-start(bf16[1,64,256]{2,1,0:T(8,128)(2,1)S(1)} %get-tuple-element.266), channel_id=1, source_target_pairs={{1,0},{3,2},{5,4},{7,6},{9,8},{11,10},{13,12},{15,14},{17,16},{19,... | collective-permute-start | bytes 98312 | tf_op jit(solution)/shard_map/ppermute | solution.py:41
  329.4 19.0 %collective-permute-start.13 = (f32[12,64,256]{2,1,0:T(8,128)S(1)}, f32[12,64,256]{2,1,0:T(8,128)S(1)}, u32[]{:S(2)}, u32[]{:S(2)}) collective-permute-start(f32[12,64,256]{2,1,0:T(8,128)S(1)} %get-tuple-element.201), channel_id=1, source_target_pairs={{0,2},{2,4},{4,6},{6,8},{8,10},{10,12},{12,14},{1,3},{3,5},{5,7},{... | collective-permute-start | bytes 2359304 | tf_op jit(solution)/shard_map/ppermute | solution.py:24
  333.9 20.5 %collective-permute-start.17 = (f32[12,64,256]{2,1,0:T(8,128)}, f32[12,64,256]{2,1,0:T(8,128)}, u32[]{:S(2)}, u32[]{:S(2)}) collective-permute-start(f32[12,64,256]{2,1,0:T(8,128)} %get-tuple-element.202), channel_id=1, source_target_pairs={{0,8},{2,10},{4,12},{6,14},{1,9},{3,11},{5,13},{7,15},{16,24},{18,... | collective-permute-start | bytes 2359304 | tf_op jit(solution)/shard_map/ppermute | solution.py:24
  337.1 37.4 %collective-permute-start.16 = (f32[12,64,256]{2,1,0:T(8,128)}, f32[12,64,256]{2,1,0:T(8,128)}, u32[]{:S(2)}, u32[]{:S(2)}) collective-permute-start(f32[12,64,256]{2,1,0:T(8,128)} %get-tuple-element.203), channel_id=1, source_target_pairs={{8,0},{10,2},{12,4},{14,6},{9,1},{11,3},{13,5},{15,7},{24,16},{26,... | collective-permute-start | bytes 2359304 | tf_op jit(solution)/shard_map/ppermute | solution.py:24
  338.4 36.1 %collective-permute-start.15 = (f32[12,64,256]{2,1,0:T(8,128)}, f32[12,64,256]{2,1,0:T(8,128)}, u32[]{:S(2)}, u32[]{:S(2)}) collective-permute-start(f32[12,64,256]{2,1,0:T(8,128)} %get-tuple-element.204), channel_id=1, source_target_pairs={{0,4},{2,6},{4,8},{6,10},{8,12},{10,14},{1,5},{3,7},{5,9},{7,11},{... | collective-permute-start | bytes 2359304 | tf_op jit(solution)/shard_map/ppermute | solution.py:24
  340.6 44.8 %collective-permute-start.14 = (f32[12,64,256]{2,1,0:T(8,128)}, f32[12,64,256]{2,1,0:T(8,128)}, u32[]{:S(2)}, u32[]{:S(2)}) collective-permute-start(f32[12,64,256]{2,1,0:T(8,128)} %get-tuple-element.205), channel_id=1, source_target_pairs={{4,0},{6,2},{8,4},{10,6},{12,8},{14,10},{5,1},{7,3},{9,5},{11,7},{... | collective-permute-start | bytes 2359304 | tf_op jit(solution)/shard_map/ppermute | solution.py:24
  348.4 37.0 %collective-permute-start.12 = (f32[12,64,256]{2,1,0:T(8,128)}, f32[12,64,256]{2,1,0:T(8,128)}, u32[]{:S(2)}, u32[]{:S(2)}) collective-permute-start(f32[12,64,256]{2,1,0:T(8,128)} %get-tuple-element.206), channel_id=1, source_target_pairs={{2,0},{4,2},{6,4},{8,6},{10,8},{12,10},{14,12},{3,1},{5,3},{7,5},{... | collective-permute-start | bytes 2359304 | tf_op jit(solution)/shard_map/ppermute | solution.py:24
  351.3 34.2 %copy-start.11 = (f32[12,64,256]{2,1,0:T(8,128)S(1)}, f32[12,64,256]{2,1,0:T(8,128)}, u32[]{:S(2)}) copy-start(f32[12,64,256]{2,1,0:T(8,128)} %copy-done.10) | copy-start | bytes 2359300
  388.0 92.2 %collective-permute-start.18 = (bf16[1,2,64,256]{3,2,1,0:T(8,128)(2,1)S(1)}, bf16[1,2,64,256]{3,2,1,0:T(8,128)(2,1)S(1)}, u32[]{:S(2)}, u32[]{:S(2)}) collective-permute-start(bf16[1,2,64,256]{3,2,1,0:T(8,128)(2,1)S(1)} %fusion.70), channel_id=1, source_target_pairs={{0,1},{1,0},{2,3},{3,2},{4,5},{5,4},{6,7},{7,6},{8,9},{9,8},{10,11... | collective-permute-start | bytes 196616 | tf_op jit(solution)/shard_map/ppermute | solution.py:30
  (22 other events, 128.0 us)
Sparse Core Ops, SparseCore 0:
  351.4 121.9 all-reduce.4
where the time goes:
time: 492 us; the launch traced here: 488 us
  matrix products  189 us (38%)
  waiting for transfers between devices  145 us (29%)
  other arithmetic  77 us (16%)
  starting transfers between devices  42.7 us (9%)
  local copies, waits for them, and re-layouts  19.4 us (4%)
  between operations  15.3 us (3%)
    psum x1, waiting for transfers between devices, local(): lax.psum((grad_shared, grad_values, grad_output, grad_taps), ('frame', 'r...  85.4 us
    ppermute x12, waiting for transfers between devices, shifted_2(): return lax.ppermute(array, axis, pairs)  59.2 us
    dot_general x16, matrix products, head_weights(): jnp.dot(query_head, key_head.T, preferred_element_type=jnp.float32)  49.3 us
    reduce_sum x16, other arithmetic, head_weights(): return exp_terms / jnp.sum(exp_terms, axis=1, keepdims=True)  33.9 us
    dot_general x8, matrix products, one_head(): jnp.dot(weights.astype(jnp.bfloat16), value_head, preferred_element_type=...  31.4 us
    ppermute x12, starting transfers between devices, shifted_2(): return lax.ppermute(array, axis, pairs)  31.4 us
    dot_general x8, matrix products, one_head(): jnp.dot(grad_head, value_head.T, preferred_element_type=jnp.float32)  28.1 us
    dot_general x8, matrix products, one_head(): value_grad = jnp.dot(prob.T, grad_head, preferred_element_type=jnp.float32)  25.4 us
  transfers between devices with their start and end apart: 20, of which 7 were waited for; matrix products, arithmetic and copies ran while one was open for 8% of the time, Pallas kernels for 0%

commit v1 on v0

v1 whole, which is shorter than its diff:
```python
import functools
import math

import jax
import jax.numpy as jnp
from jax import lax
from jax.experimental import pallas as pl
from jax.experimental.pallas import tpu as pltpu
from jax.sharding import PartitionSpec as P

HEADS = 8
DH = 32
COLS = 64
WMAX = 2
BROWS = 2

SCALE = 1.5 / math.sqrt(DH)
MASKED = -1e30
F32 = jnp.float32
BF16 = jnp.bfloat16
NN = (((1,), (0,)), ((), ()))
NT = (((1,), (1,)), ((), ()))


def dot(left, right, dims=NN):
    return lax.dot_general(left, right, dims, preferred_element_type=F32)


def halves_of(value):
    high = value.astype(BF16)
    return high, (value - high.astype(F32)).astype(BF16)


def left_split_dot(left, right, dims=NN):
    high, low = halves_of(left)
    return dot(high, right, dims) + dot(low, right, dims)


def right_split_dot(left, right, dims=NN):
    high, low = halves_of(right)
    return dot(left, high, dims) + dot(left, low, dims)


def shifted(array, by):
    devices = lax.axis_size("frame")
    pairs = [(i, i + by) for i in range(devices) if 0 <= i + by < devices]
    return lax.ppermute(array, "frame", pairs)


def swapped(array, axis, mask):
    pairs = [(i, i ^ mask) for i in range(lax.axis_size(axis))]
    return lax.ppermute(array, axis, pairs)


def whole_call(body, outs, args, smem=(), scratch=(), grid=None, flops=0, moved=0, name=None):
    specs = [
        pl.BlockSpec(memory_space=pltpu.SMEM if i in smem else pltpu.VMEM)
        for i in range(len(args))
    ]
    more = {} if grid is None else {"grid": grid}
    return pl.pallas_call(
        body,
        out_shape=[jax.ShapeDtypeStruct(shape, dtype) for shape, dtype in outs],
        in_specs=specs,
        out_specs=[pl.BlockSpec(memory_space=pltpu.VMEM)] * len(outs),
        scratch_shapes=list(scratch),
        compiler_params=pltpu.CompilerParams(vmem_limit_bytes=48 * 1024 * 1024),
        cost_estimate=pl.CostEstimate(flops=flops, bytes_accessed=moved, transcendentals=0),
        name=name,
        **more,
    )(*args)


def before_kernel(
    meta, cot, gain, edge, tokens, taps, shared, outp,
    resid_out, rb_out, ext_out, up_out, upt_out, query_out, queryt_out,
):
    row_id = meta[2]
    count = cot.shape[0]
    grad_z = cot[...].astype(F32) * gain[...]
    got = edge[...]
    none = jnp.zeros_like(got)
    ext_out[:COLS] = jnp.where(row_id == 0, none, got)
    ext_out[COLS : COLS + count] = grad_z.astype(BF16)
    ext_out[COLS + count :] = jnp.where(row_id == 0, got, none)
    total = grad_z
    for tap in range(3):
        begin = (2 - tap) * COLS
        total = total + dot(ext_out[begin : begin + count], taps[tap], NT)
    resid_out[...] = total
    rounded = total.astype(BF16)
    rb_out[...] = rounded
    upstream = dot(rounded, outp[...], NT).astype(BF16)
    up_out[...] = upstream
    upt_out[...] = upstream.T
    query = dot(tokens[...], shared[...]).astype(BF16)
    query_out[...] = query
    queryt_out[...] = query.T


def attention_kernel(
    meta, slots, halo, query, queryt, up, upt, tokens, rb, ext, resid_grad, shared, value, outp,
    mid_out, edge_out, hidden_out, resid_out, base_out, weights_out,
    key_all, val_all, key_blk, val_blk, bias, mixed_all, dq_all, dkt, dvt,
):
    step = pl.program_id(0)
    window, row_id, total_rows = meta[1], meta[2], meta[3]
    width = query.shape[1]
    count = query.shape[0]
    rim = WMAX * COLS
    ext_count = count + 2 * rim
    block = BROWS * COLS
    span = block + 2 * rim

    @pl.when(step == 0)
    def _():
        for slot in range(2):
            for weight, full in ((shared, key_all), (value, val_all)):
                full[slot, rim : rim + count] = dot(slots[slot], weight[...]).astype(BF16)
                far = dot(halo[slot], weight[...]).astype(BF16)
                none = jnp.zeros_like(far)
                full[slot, :rim] = jnp.where(row_id == 0, none, far)
                full[slot, rim + count :] = jnp.where(row_id == 0, far, none)
        dkt[...] = jnp.zeros_like(dkt)
        dvt[...] = jnp.zeros_like(dvt)

    begin = pl.multiple_of(step * block, block)
    for slot in range(2):
        key_blk[slot * span : (slot + 1) * span] = key_all[slot, pl.ds(begin, span)]
        val_blk[slot * span : (slot + 1) * span] = val_all[slot, pl.ds(begin, span)]
    first_row = row_id * (count // COLS) + step * BROWS
    query_row = first_row + lax.broadcasted_iota(jnp.int32, (block, span), 0) // COLS
    key_row = first_row - WMAX + lax.broadcasted_iota(jnp.int32, (block, span), 1) // COLS
    near = jnp.abs(query_row - key_row) <= window
    allowed = near & (key_row >= 0) & (key_row < total_rows)
    one_bias = jnp.where(allowed, 0.0, MASKED)
    bias[:, :span] = one_bias
    bias[:, span:] = one_bias

    query_b = query[pl.ds(begin, block), :]
    up_b = up[pl.ds(begin, block), :]
    lane_head = lax.broadcasted_iota(jnp.int32, (1, width), 1) // DH
    mixed = jnp.zeros((block, width), F32)
    grad_q = jnp.zeros((block, width), F32)
    for head in range(HEADS):
        mask = (lane_head == head).astype(F32)
        mask_b = mask.astype(BF16)
        scores = dot(query_b * mask_b, key_blk[...], NT) * SCALE + bias[...]
        top = jnp.max(scores, axis=1, keepdims=True)
        terms = jnp.exp(scores - top)
        weights = terms * (1.0 / jnp.sum(terms, axis=1, keepdims=True))
        prob = weights.astype(BF16)
        mixed = mixed + dot(prob, val_blk[...]) * mask
        grad_prob = dot(up_b * mask_b, val_blk[...], NT)
        weighted = weights * grad_prob
        inner = jnp.sum(weighted, axis=1, keepdims=True)
        grad_score = ((weights * (grad_prob - inner)) * SCALE).astype(BF16)
        grad_q = grad_q + dot(grad_score, key_blk[...]) * mask
        lanes = slice(head * DH, (head + 1) * DH)
        up_h = upt[lanes, pl.ds(begin, block)]
        query_h = queryt[lanes, pl.ds(begin, block)]
        dv = dot(up_h, prob)
        dk = dot(query_h, grad_score)
        for slot in range(2):
            dvt[slot, lanes, pl.ds(begin, span)] += dv[:, slot * span : (slot + 1) * span]
            dkt[slot, lanes, pl.ds(begin, span)] += dk[:, slot * span : (slot + 1) * span]
    mixed_all[pl.ds(begin, block), :] = mixed.astype(BF16)
    dq_all[pl.ds(begin, block), :] = grad_q

    @pl.when(step == pl.num_programs(0) - 1)
    def _():
        mixed_full = mixed_all[...]
        residual = tokens[...].astype(F32) + dot(mixed_full, outp[...])
        resid_out[...] = residual
        hidden = residual.astype(BF16)
        hidden_out[...] = hidden
        weights_out[2] = dot(mixed_full.T, rb[...])
        hidden_t = hidden.T
        for tap in range(3):
            start = (2 - tap) * COLS
            weights_out[3 + tap] = dot(hidden_t, ext[start : start + count])
        grad_q_full = dq_all[...]
        base_out[...] = resid_grad[...] + left_split_dot(grad_q_full, shared[...], NT)
        shared_grad = right_split_dot(tokens[...].T, grad_q_full)
        shared_t = jnp.zeros((width, width), F32)
        value_t = jnp.zeros((width, width), F32)
        for slot in range(2):
            key_high, key_low = halves_of(dkt[slot])
            val_high, val_low = halves_of(dvt[slot])
            part = (
                dot(shared[...], key_high)
                + dot(shared[...], key_low)
                + dot(value[...], val_high)
                + dot(value[...], val_low)
            )
            mid_out[slot] = part[:, rim : rim + count]
            edge_out[slot] = jnp.where(
                row_id == 0, part[:, rim + count :], part[:, :rim]
            ).astype(BF16)
            middle = slice(rim, rim + count)
            for high_low in (key_high, key_low):
                rims = jnp.where(
                    row_id == 0,
                    high_low[:, rim + count :].astype(F32),
                    high_low[:, :rim].astype(F32),
                ).astype(BF16)
                shared_t += dot(high_low[:, middle], slots[slot]) + dot(rims, halo[slot])
            for high_low in (val_high, val_low):
                rims = jnp.where(
                    row_id == 0,
                    high_low[:, rim + count :].astype(F32),
                    high_low[:, :rim].astype(F32),
                ).astype(BF16)
                value_t += dot(high_low[:, middle], slots[slot]) + dot(rims, halo[slot])
        weights_out[0] = shared_grad + shared_t.T
        weights_out[1] = value_t.T


def coded_kernel(meta, hidden, halo, residual, gain, taps, coded_out, ext):
    row_id = meta[2]
    count = hidden.shape[0]
    got = halo[...]
    none = jnp.zeros_like(got)
    ext[:COLS] = jnp.where(row_id == 0, none, got)
    ext[COLS : COLS + count] = hidden[...]
    ext[COLS + count :] = jnp.where(row_id == 0, got, none)
    total = jnp.zeros((count, hidden.shape[1]), F32)
    for tap in range(3):
        begin = tap * COLS
        total = total + dot(ext[begin : begin + count], taps[tap])
    coded_out[...] = ((residual[...] + total) * gain[...]).astype(BF16)


def final_kernel(base, first, second, third, grad_out):
    returned = first[...].astype(F32) + second[...].astype(F32) + third[...].astype(F32)
    grad_out[...] = (base[...] + returned.T).astype(BF16)


def summed_over(value, stages, direct):
    row_of = {axis: lax.axis_index(axis) for axis in ("frame", "row")}
    for axis, mask in stages:
        bit = (row_of[axis] & mask) != 0
        half = value.shape[0] // 2
        low, high = value[:half], value[half:]
        got = swapped(jnp.where(bit, low, high).astype(BF16), axis, mask)
        value = jnp.where(bit, high, low) + got.astype(F32)
    own = value.astype(BF16)
    level = [own] + [swapped(own, "frame", mask) for mask in direct]
    level = [part.astype(F32) for part in level]
    while len(level) > 1:
        level = [level[i] + level[i + 1] for i in range(0, len(level), 2)]
    value = level[0].astype(BF16)
    for axis, mask in stages[::-1]:
        bit = (row_of[axis] & mask) != 0
        got = swapped(value, axis, mask)
        value = jnp.concatenate([jnp.where(bit, got, value), jnp.where(bit, value, got)], 0)
    return value


def local(
    latents, ref_frames, windows, quant_level, quant_scale,
    shared_proj, value_proj, output_proj, conv_taps, cotangent,
):
    width = latents.shape[2]
    count = latents.shape[1]
    rows_dev = count // COLS
    frames = lax.axis_size("frame")
    total_rows = rows_dev * lax.axis_size("row")
    frame_id = lax.axis_index("frame")
    row_id = lax.axis_index("row")
    refs = ref_frames[0]
    odd = (frame_id & 1) == 1
    rim = WMAX * COLS
    tokens = latents[0]
    meta = jnp.stack(
        [frame_id, windows[0], row_id, jnp.int32(total_rows)]
    ).astype(jnp.int32)
    gain = lax.dynamic_slice_in_dim(quant_scale, quant_level[0], 1, 0)

    from_before = shifted(tokens, 2)
    from_after = shifted(tokens, -2)
    from_pair = swapped(tokens, "frame", 1)

    cot = cotangent[0]
    cot_edge = jnp.where(row_id == 0, cot[count - COLS :], cot[:COLS])
    grad_edge = swapped((cot_edge.astype(F32) * gain).astype(BF16), "row", 1)
    grad_resid, grad_rb, grad_ext, up, upt, query, queryt = whole_call(
        before_kernel,
        [
            ((count, width), F32),
            ((count, width), BF16),
            ((count + 2 * COLS, width), BF16),
            ((count, width), BF16),
            ((width, count), BF16),
            ((count, width), BF16),
            ((width, count), BF16),
        ],
        (meta, cot, gain, grad_edge, tokens, conv_taps, shared_proj, output_proj),
        smem=(0,),
        flops=2 * 5 * count * width * width,
        moved=4 * count * width * 6,
        name="gradient_path",
    )

    from_before_2 = shifted(from_before, 2)
    from_after_2 = shifted(from_after, -2)
    from_cross = swapped(jnp.where(odd, from_before, from_after), "frame", 1)
    pair_step = jnp.where(odd, -1, 1)
    distance = (refs - frame_id)[:, None, None]
    slots = jnp.where(distance == pair_step, from_pair[None], from_cross[None])
    for step, source in (
        (-2, from_before), (2, from_after), (-4, from_before_2), (4, from_after_2)
    ):
        slots = jnp.where(distance == step, source[None], slots)
    halo = swapped(jnp.where(row_id == 0, slots[:, count - rim :], slots[:, :rim]), "row", 1)

    block = BROWS * COLS
    span = block + 2 * rim
    ext_count = count + 2 * rim
    mid, edge, hidden, residual, base, weight_grads = whole_call(
        attention_kernel,
        [
            ((2, width, count), F32),
            ((2, width, rim), BF16),
            ((count, width), BF16),
            ((count, width), F32),
            ((count, width), F32),
            ((6, width, width), F32),
        ],
        (
            meta, slots, halo, query, queryt, up, upt, tokens, grad_rb, grad_ext, grad_resid,
            shared_proj, value_proj, output_proj,
        ),
        smem=(0,),
        scratch=[
            pltpu.VMEM((2, ext_count, width), BF16),
            pltpu.VMEM((2, ext_count, width), BF16),
            pltpu.VMEM((2 * span, width), BF16),
            pltpu.VMEM((2 * span, width), BF16),
            pltpu.VMEM((block, 2 * span), F32),
            pltpu.VMEM((count, width), BF16),
            pltpu.VMEM((count, width), F32),
            pltpu.VMEM((2, width, ext_count), F32),
            pltpu.VMEM((2, width, ext_count), F32),
        ],
        grid=(count // block,),
        flops=6 * 2 * count * 2 * span * width * HEADS,
        moved=count * width * 60,
        name="attention",
    )

    hidden_edge = jnp.where(row_id == 0, hidden[count - COLS :], hidden[:COLS])
    hidden_halo = swapped(hidden_edge, "row", 1)
    edge_got = swapped(edge, "row", 1).astype(F32)
    none = jnp.zeros((2, width, count - rim), F32)
    mid = mid + jnp.where(
        row_id == 0,
        jnp.concatenate([none, edge_got], 2),
        jnp.concatenate([edge_got, none], 2),
    )

    def part_for(step):
        return jnp.sum(jnp.where(distance == step, mid, 0.0), axis=0)

    back = shifted(part_for(-4).astype(BF16), -2)
    ahead = shifted(part_for(4).astype(BF16), 2)
    across = swapped(part_for(-pair_step).astype(BF16), "frame", 1).astype(F32)
    third = swapped(part_for(pair_step).astype(BF16), "frame", 1)
    first = shifted(
        (part_for(-2) + back.astype(F32) + jnp.where(odd, across, 0.0)).astype(BF16), -2
    )
    second = shifted(
        (part_for(2) + ahead.astype(F32) + jnp.where(odd, 0.0, across)).astype(BF16), 2
    )

    stages = [("row", 1), ("frame", 1)]
    mask = 2
    while mask * 4 < frames:
        stages.append(("frame", mask))
        mask *= 2
    direct = [mask, 2 * mask, 3 * mask]
    sums = summed_over(weight_grads.reshape(-1, width), stages, direct).astype(F32)
    sums = sums * (1.0 / math.sqrt(frames * total_rows * COLS))
    sums = sums.reshape(6, width, width)

    (coded,) = whole_call(
        coded_kernel,
        [((count, width), BF16)],
        (meta, hidden, hidden_halo, residual, gain, conv_taps),
        smem=(0,),
        scratch=[pltpu.VMEM((count + 2 * COLS, width), BF16)],
        flops=2 * 3 * count * width * width,
        moved=count * width * 8,
        name="context",
    )
    (grad_latents,) = whole_call(
        final_kernel,
        [((count, width), BF16)],
        (base, first, second, third),
        flops=count * width * 4,
        moved=count * width * 12,
        name="latent_gradient",
    )
    return (
        coded[None],
        grad_latents[None],
        sums[0],
        sums[1],
        sums[2],
        sums[3:],
    )


def solution(mesh):
    placed = (
        P(("groups", "frame"), "row", None),
        P(("groups", "frame"), None),
        P(("groups", "frame")),
        P(("groups", "frame")),
        P(),
        P(),
        P(),
        P(),
        P(),
        P(("groups", "frame"), "row", None),
    )
    return jax.shard_map(
        local,
        mesh=mesh,
        in_specs=placed,
        out_specs=(
            P(("groups", "frame"), "row", None),
            P(("groups", "frame"), "row", None),
            P("groups", None),
            P("groups", None),
            P("groups", None),
            P("groups", None, None),
        ),
        check_vma=False,
    )
```

time: 492 us -> 133 us (0.27)
  matrix products: 189 us -> 0 us
  waiting for transfers between devices: 145 us -> 46.2 us
  other arithmetic: 77 us -> 7.2 us
  Pallas kernels: 0 us -> 37.5 us
  between operations: 15.3 us -> 2.33 us
  local copies, waits for them, and re-layouts: 19.4 us -> 6.85 us
  starting transfers between devices: 42.7 us -> 32.2 us
    dot_general x77 -> x0, matrix products: 189 us -> none  [the longest x16 49.3 us: head_weights(): jnp.dot(query_head, key_head.T, preferred_element_type=jnp.float32)]
    psum x1 -> x0, waiting for transfers between devices: 85.4 us -> none  [local(): lax.psum((grad_shared, grad_values, grad_output, grad_taps), ('frame', 'r...]
    pallas_call x0 -> x4, Pallas kernels: none -> 37.5 us  [whole_call(): pl.pallas_call(body, out_shape=[jax.ShapeDtypeStruct(shape, dtype) for sh...]
    reduce_sum x18 -> x1, other arithmetic: 37.4 us -> 0.57 us  [part_for(): return jnp.sum(jnp.where(distance == step, mid, 0.0), axis=0)]
    convert_element_type x11 -> x7, other arithmetic: 23.4 us -> 2.67 us  [the longest x2 1.48 us: summed_over(): got = swapped(jnp.where(bit, low, high).astype(BF16), axis, mask)]
    ppermute x19 -> x23, waiting for transfers between devices: 59.2 us -> 46.2 us  [the longest x15 28.3 us: swapped(): return lax.ppermute(array, axis, pairs)]
    ppermute x19 -> x23, starting transfers between devices: 42.6 us -> 32.2 us  [the longest x8 18 us: shifted(): return lax.ppermute(array, 'frame', pairs)]
    another operation x6 -> x0, local copies, waits for them, and re-layouts: 9.24 us -> none  [the longest x4 9.16 us: split_heads(): return jnp.transpose(block.reshape(block.shape[0], HEADS, DH), (1, 0, 2))]
  transfers between devices with their start and end apart: 20 -> 23, of which waited for: 7 -> 13; matrix products, arithmetic and copies ran while one was open for 8% -> 3% of each run, Pallas kernels for 0% -> 3%
where the time goes in v1:
time: 133 us; the launch traced here: 132 us
  waiting for transfers between devices  46.2 us (35%)
  Pallas kernels  37.5 us (28%)
  starting transfers between devices  32.2 us (24%)
  other arithmetic  7.2 us (5%)
  local copies, waits for them, and re-layouts  6.85 us (5%)
  between operations  2.33 us (2%)
    pallas_call x4, Pallas kernels, whole_call(): pl.pallas_call(body, out_shape=[jax.ShapeDtypeStruct(shape, dtype) for sh...  37.5 us
    ppermute x15, waiting for transfers between devices, swapped(): return lax.ppermute(array, axis, pairs)  28.3 us
    ppermute x8, starting transfers between devices, shifted(): return lax.ppermute(array, 'frame', pairs)  18 us
    ppermute x8, waiting for transfers between devices, shifted(): return lax.ppermute(array, 'frame', pairs)  17.9 us
    ppermute x15, starting transfers between devices, swapped(): return lax.ppermute(array, axis, pairs)  14.2 us
    unnamed x26, local copies, waits for them, and re-layouts  5.01 us
  transfers between devices with their start and end apart: 23, of which 13 were waited for; matrix products, arithmetic and copies ran while one was open for 3% of the time, Pallas kernels for 3%

profile of v1, /device:TPU:0, one launch (start us, length us, event | category | flops | bytes accessed | tf_op | source)
XLA Modules:
  0.0 132.3 jit_solution(5881296356588016169)
XLA Ops:
  0.6 3.0 %collective-permute-start.4 = (bf16[512,256]{1,0:T(8,128)(2,1)}, bf16[512,256]{1,0:T(8,128)(2,1)S(1)}, u32[]{:S(2)}, u32[]{:S(2)}) collective-permute-start(bf16[512,256]{1,0:T(8,128)(2,1)} %bitcast.32), channel_id=1, source_target_pairs={{0,2},{2,0},{4,6},{6,4},{8,10},{10,8},{12,14},{14,12},{1,3},{3,1},... | collective-permute-start | bytes 786440 | tf_op jit(solution)/shard_map/ppermute | solution.py:52
  3.7 3.5 %collective-permute-start.2 = (bf16[512,256]{1,0:T(8,128)(2,1)}, bf16[512,256]{1,0:T(8,128)(2,1)S(1)}, u32[]{:S(2)}, u32[]{:S(2)}) collective-permute-start(bf16[512,256]{1,0:T(8,128)(2,1)} %bitcast.33), channel_id=1, source_target_pairs={{0,4},{2,6},{4,8},{6,10},{8,12},{10,14},{1,5},{3,7},{5,9},{7,11},{... | collective-permute-start | bytes 786440 | tf_op jit(solution)/shard_map/ppermute | solution.py:47
  10.1 2.6 %collective-permute-done.2 = bf16[512,256]{1,0:T(8,128)(2,1)S(1)} collective-permute-done((bf16[512,256]{1,0:T(8,128)(2,1)}, bf16[512,256]{1,0:T(8,128)(2,1)S(1)}, u32[]{:S(2)}, u32[]{:S(2)}) %collective-permute-start.2) | collective-permute-done | bytes 262176 | tf_op jit(solution)/shard_map/ppermute | solution.py:47
  12.7 4.0 %collective-permute-done = bf16[512,256]{1,0:T(8,128)(2,1)S(1)} collective-permute-done((bf16[512,256]{1,0:T(8,128)(2,1)}, bf16[512,256]{1,0:T(8,128)(2,1)S(1)}, u32[]{:S(2)}, u32[]{:S(2)}) %collective-permute-start) | collective-permute-done | bytes 262176 | tf_op jit(solution)/shard_map/ppermute | solution.py:47
  17.4 3.5 %collective-permute-start.3 = (bf16[512,256]{1,0:T(8,128)(2,1)S(1)}, bf16[512,256]{1,0:T(8,128)(2,1)S(1)}, u32[]{:S(2)}, u32[]{:S(2)}) collective-permute-start(bf16[512,256]{1,0:T(8,128)(2,1)S(1)} %collective-permute-done.2), channel_id=1, source_target_pairs={{0,4},{2,6},{4,8},{6,10},{8,12},{10,14},{1,5},{3,7},{5,9},{7,11},{... | collective-permute-start | bytes 786440 | tf_op jit(solution)/shard_map/ppermute | solution.py:47
  24.7 4.4 %collective-permute-done.1 = bf16[512,256]{1,0:T(8,128)(2,1)S(1)} collective-permute-done((bf16[512,256]{1,0:T(8,128)(2,1)S(1)}, bf16[512,256]{1,0:T(8,128)(2,1)S(1)}, u32[]{:S(2)}, u32[]{:S(2)}) %collective-permute-start.1) | collective-permute-done | bytes 262176 | tf_op jit(solution)/shard_map/ppermute | solution.py:47
  29.6 1.4 %gradient_path.1 = (f32[512,256]{1,0:T(8,128)S(1)}, bf16[512,256]{1,0:T(8,128)(2,1)S(1)}, bf16[640,256]{1,0:T(8,128)(2,1)S(1)}, bf16[512,256]{1,0:T(8,128)(2,1)S...) custom-call(s32[4]{0:T(128)S(1)} %pad_add_fusion.meta, ...), custom_call_target="tpu_custom_call" | custom-call | flops 335544320 | bytes 3145728 | tf_op jit(solution)/shard_map/gradient_path/pallas_call | solution.py:61
  35.3 33.6 %attention.1 = (f32[2,256,512]{2,1,0:T(8,128)S(1)}, bf16[2,256,128]{2,1,0:T(8,128)(2,1)S(1)}, bf16[512,256]{1,0:T(8,128)(2,1)S(1)}, f32[512,256]{1,0:T(8,128)S(1...) custom-call(s32[4]{0:T(128)S(1)} %pad_add_fusion.meta, bf16[2,512,256]{2,1,0:T(8,128)(2,1)S(1)} %select_select_fusion.slots, ...), custom_call_target="tpu_custom_call" | custom-call | flops 9663676416 | bytes 7864320 | tf_op jit(solution)/shard_map/attention/pallas_call | solution.py:61
  69.6 1.4 %select_convert_fusion = bf16[3,256,256]{2,1,0:T(8,128)(2,1)S(1)} fusion(f32[6,256,256]{2,1,0:T(8,128)} %get-tuple-element.31, pred[]{:T(512)S(6)} %ne.8), kind=kLoop, calls=%fused_computation.9 | loop fusion | flops 196608 | bytes 1179649 | tf_op jit(solution)/shard_map/convert_element_type | solution.py:245
  71.6 1.5 %slice_select_fusion = f32[3,256,256]{2,1,0:T(8,128)S(1)} fusion(f32[6,256,256]{2,1,0:T(8,128)} %get-tuple-element.31, pred[]{:T(512)S(6)} %ne.8), kind=kLoop, calls=%fused_computation.10 | loop fusion | flops 196608 | bytes 2359297 | tf_op jit(solution)/shard_map/jit(_where)/select_n | solution.py:246
  74.2 1.6 %collective-permute-start.17 = (bf16[384,256]{1,0:T(8,128)(2,1)S(1)}, bf16[384,256]{1,0:T(8,128)(2,1)S(1)}, u32[]{:S(2)}, u32[]{:S(2)}) collective-permute-start(bf16[384,256]{1,0:T(8,128)(2,1)S(1)} %select_convert_fusion.1), channel_id=1, source_target_pairs={{0,2},{2,0},{4,6},{6,4},{8,10},{10,8},{12,14},{14,12},{1,3},{3,1},... | collective-permute-start | bytes 589832 | tf_op jit(solution)/shard_map/ppermute | solution.py:52
  75.8 5.7 %collective-permute-done.17 = bf16[384,256]{1,0:T(8,128)(2,1)S(1)} collective-permute-done((bf16[384,256]{1,0:T(8,128)(2,1)S(1)}, bf16[384,256]{1,0:T(8,128)(2,1)S(1)}, u32[]{:S(2)}, u32[]{:S(2)}) %collective-permute-start.17) | collective-permute-done | bytes 196640 | tf_op jit(solution)/shard_map/ppermute | solution.py:52
  81.6 3.0 %collective-permute-start.19 = (bf16[384,256]{1,0:T(8,128)(2,1)S(1)}, bf16[384,256]{1,0:T(8,128)(2,1)S(1)}, u32[]{:S(2)}, u32[]{:S(2)}) collective-permute-start(bf16[384,256]{1,0:T(8,128)(2,1)S(1)} %add_convert_fusion.1), channel_id=1, source_target_pairs={{0,8},{2,10},{4,12},{6,14},{8,0},{10,2},{12,4},{14,6},{1,9},{3,11}... | collective-permute-start | bytes 589832 | tf_op jit(solution)/shard_map/ppermute | solution.py:52
  84.6 1.4 %collective-permute-start.18 = (bf16[384,256]{1,0:T(8,128)(2,1)S(1)}, bf16[384,256]{1,0:T(8,128)(2,1)S(1)}, u32[]{:S(2)}, u32[]{:S(2)}) collective-permute-start(bf16[384,256]{1,0:T(8,128)(2,1)S(1)} %add_convert_fusion.1), channel_id=1, source_target_pairs={{0,4},{2,6},{4,0},{6,2},{8,12},{10,14},{12,8},{14,10},{1,5},{3,7},... | collective-permute-start | bytes 589832 | tf_op jit(solution)/shard_map/ppermute | solution.py:52
  86.0 1.3 %collective-permute-done.9 = bf16[2,256,128]{2,1,0:T(8,128)(2,1)S(1)} collective-permute-done((bf16[2,256,128]{2,1,0:T(8,128)(2,1)S(1)}, bf16[2,256,128]{2,1,0:T(8,128)(2,1)S(1)}, u32[]{:S(2)}, u32[]{:S(2)}) %collective-permute-start.9) | collective-permute-done | bytes 131104 | tf_op jit(solution)/shard_map/ppermute | solution.py:52
  87.4 4.0 %collective-permute-done.20 = bf16[384,256]{1,0:T(8,128)(2,1)S(1)} collective-permute-done((bf16[384,256]{1,0:T(8,128)(2,1)S(1)}, bf16[384,256]{1,0:T(8,128)(2,1)S(1)}, u32[]{:S(2)}, u32[]{:S(2)}) %collective-permute-start.20) | collective-permute-done | bytes 196640 | tf_op jit(solution)/shard_map/ppermute | solution.py:52
  91.3 10.2 %collective-permute-done.19 = bf16[384,256]{1,0:T(8,128)(2,1)S(1)} collective-permute-done((bf16[384,256]{1,0:T(8,128)(2,1)S(1)}, bf16[384,256]{1,0:T(8,128)(2,1)S(1)}, u32[]{:S(2)}, u32[]{:S(2)}) %collective-permute-start.19) | collective-permute-done | bytes 196640 | tf_op jit(solution)/shard_map/ppermute | solution.py:52
  101.7 1.6 %collective-permute-start.21 = (bf16[384,256]{1,0:T(8,128)(2,1)S(1)}, bf16[384,256]{1,0:T(8,128)(2,1)S(1)}, u32[]{:S(2)}, u32[]{:S(2)}) collective-permute-start(bf16[384,256]{1,0:T(8,128)(2,1)S(1)} %add_convert_fusion), channel_id=1, source_target_pairs={{0,2},{2,0},{4,6},{6,4},{8,10},{10,8},{12,14},{14,12},{1,3},{3,1},... | collective-permute-start | bytes 589832 | tf_op jit(solution)/shard_map/ppermute | solution.py:52
  105.7 1.6 %collective-permute-start.11 = (bf16[256,512]{1,0:T(8,128)(2,1)S(1)}, bf16[256,512]{1,0:T(8,128)(2,1)S(1)}, u32[]{:S(2)}, u32[]{:S(2)}) collective-permute-start(bf16[256,512]{1,0:T(8,128)(2,1)S(1)} %get-tuple-element.34), channel_id=1, source_target_pairs={{0,2},{2,0},{4,6},{6,4},{8,10},{10,8},{12,14},{14,12},{1,3},{3,1},... | collective-permute-start | bytes 786440 | tf_op jit(solution)/shard_map/ppermute | solution.py:52
  107.3 4.5 %collective-permute-start.13 = (bf16[256,512]{1,0:T(8,128)(2,1)S(1)}, bf16[256,512]{1,0:T(8,128)(2,1)S(1)}, u32[]{:S(2)}, u32[]{:S(2)}) collective-permute-start(bf16[256,512]{1,0:T(8,128)(2,1)S(1)} %get-tuple-element.36), channel_id=1, source_target_pairs={{0,4},{2,6},{4,8},{6,10},{8,12},{10,14},{1,5},{3,7},{5,9},{7,11},{... | collective-permute-start | bytes 786440 | tf_op jit(solution)/shard_map/ppermute | solution.py:47
  113.1 5.8 %collective-permute-done.11 = bf16[256,512]{1,0:T(8,128)(2,1)S(1)} collective-permute-done((bf16[256,512]{1,0:T(8,128)(2,1)S(1)}, bf16[256,512]{1,0:T(8,128)(2,1)S(1)}, u32[]{:S(2)}, u32[]{:S(2)}) %collective-permute-start.11) | collective-permute-done | bytes 262176 | tf_op jit(solution)/shard_map/ppermute | solution.py:52
  119.2 1.3 collective-permute-start.14
  123.1 1.6 %context.1 = bf16[512,256]{1,0:T(8,128)(2,1)} custom-call(s32[4]{0:T(128)S(1)} %pad_add_fusion.meta, bf16[512,256]{1,0:T(8,128)(2,1)S(1)} %get-tuple-element.26.hidden, bf16[64,256]{1,0:T(8,128)(2,1)S(1)} %collective-permute-done.8.halo, f32[512,256]{1,0:T(8,128)S(1)} %get-tuple-element.27.residual, f32[1,256]{1,0:T(1,128)S(1)} %constant_dynamic-slice_fusion.gain, ...), custom_call_target="tpu_custom_call" | custom-call | flops 201326592 | bytes 1048576 | tf_op jit(solution)/shard_map/context/pallas_call | solution.py:61
  125.1 4.1 %collective-permute-done.12.first = bf16[256,512]{1,0:T(8,128)(2,1)S(1)} collective-permute-done((bf16[256,512]{1,0:T(8,128)(2,1)S(1)}, bf16[256,512]{1,0:T(8,128)(2,1)S(1)}, u32[]{:S(2)}, u32[]{:S(2)}) %collective-permute-start.12) | collective-permute-done | bytes 262176 | tf_op jit(solution)/shard_map/ppermute | solution.py:47
  (76 shorter events, 23.3 us)
Async XLA Ops:
  0.6 22.8 %collective-permute-start.4 = (bf16[512,256]{1,0:T(8,128)(2,1)}, bf16[512,256]{1,0:T(8,128)(2,1)S(1)}, u32[]{:S(2)}, u32[]{:S(2)}) collective-permute-start(bf16[512,256]{1,0:T(8,128)(2,1)} %bitcast.32), channel_id=1, source_target_pairs={{0,2},{2,0},{4,6},{6,4},{8,10},{10,8},{12,14},{14,12},{1,3},{3,1},... | collective-permute-start | bytes 786440 | tf_op jit(solution)/shard_map/ppermute | solution.py:52
  3.7 9.1 %collective-permute-start.2 = (bf16[512,256]{1,0:T(8,128)(2,1)}, bf16[512,256]{1,0:T(8,128)(2,1)S(1)}, u32[]{:S(2)}, u32[]{:S(2)}) collective-permute-start(bf16[512,256]{1,0:T(8,128)(2,1)} %bitcast.33), channel_id=1, source_target_pairs={{0,4},{2,6},{4,8},{6,10},{8,12},{10,14},{1,5},{3,7},{5,9},{7,11},{... | collective-permute-start | bytes 786440 | tf_op jit(solution)/shard_map/ppermute | solution.py:47
  7.1 9.6 %collective-permute-start = (bf16[512,256]{1,0:T(8,128)(2,1)}, bf16[512,256]{1,0:T(8,128)(2,1)S(1)}, u32[]{:S(2)}, u32[]{:S(2)}) collective-permute-start(bf16[512,256]{1,0:T(8,128)(2,1)} %bitcast.34), channel_id=1, source_target_pairs={{4,0},{6,2},{8,4},{10,6},{12,8},{14,10},{5,1},{7,3},{9,5},{11,7},{... | collective-permute-start | bytes 786440 | tf_op jit(solution)/shard_map/ppermute | solution.py:47
  9.9 19.6 %collective-permute-start.7 = (bf16[64,256]{1,0:T(8,128)(2,1)S(1)}, bf16[64,256]{1,0:T(8,128)(2,1)S(1)}, u32[]{:S(2)}, u32[]{:S(2)}) collective-permute-start(bf16[64,256]{1,0:T(8,128)(2,1)S(1)} %fusion.4), channel_id=1, source_target_pairs={{0,1},{1,0},{2,3},{3,2},{4,5},{5,4},{6,7},{7,6},{8,9},{9,8},{10,11... | collective-permute-start | bytes 98312 | tf_op jit(solution)/shard_map/ppermute | solution.py:52
  10.0 19.5 %copy-start.1 = (bf16[3,256,256]{2,1,0:T(8,128)(2,1)S(1)}, bf16[3,256,256]{2,1,0:T(8,128)(2,1)}, u32[]{:S(2)}) copy-start(bf16[3,256,256]{2,1,0:T(8,128)(2,1)} %taps.3) | copy-start | bytes 1179652
  16.8 7.9 %collective-permute-start.5 = (bf16[512,256]{1,0:T(8,128)(2,1)S(1)}, bf16[512,256]{1,0:T(8,128)(2,1)S(1)}, u32[]{:S(2)}, u32[]{:S(2)}) collective-permute-start(bf16[512,256]{1,0:T(8,128)(2,1)S(1)} %broadcast_select_fusion.2), channel_id=1, source_target_pairs={{0,2},{2,0},{4,6},{6,4},{8,10},{10,8},{12,14},{14,12},{1,3},{3,1},... | collective-permute-start | bytes 786440 | tf_op jit(solution)/shard_map/ppermute | solution.py:52
  17.4 7.3 %collective-permute-start.3 = (bf16[512,256]{1,0:T(8,128)(2,1)S(1)}, bf16[512,256]{1,0:T(8,128)(2,1)S(1)}, u32[]{:S(2)}, u32[]{:S(2)}) collective-permute-start(bf16[512,256]{1,0:T(8,128)(2,1)S(1)} %collective-permute-done.2), channel_id=1, source_target_pairs={{0,4},{2,6},{4,8},{6,10},{8,12},{10,14},{1,5},{3,7},{5,9},{7,11},{... | collective-permute-start | bytes 786440 | tf_op jit(solution)/shard_map/ppermute | solution.py:47
  20.9 8.3 %collective-permute-start.1 = (bf16[512,256]{1,0:T(8,128)(2,1)S(1)}, bf16[512,256]{1,0:T(8,128)(2,1)S(1)}, u32[]{:S(2)}, u32[]{:S(2)}) collective-permute-start(bf16[512,256]{1,0:T(8,128)(2,1)S(1)} %collective-permute-done), channel_id=1, source_target_pairs={{4,0},{6,2},{8,4},{10,6},{12,8},{14,10},{5,1},{7,3},{9,5},{11,7},{... | collective-permute-start | bytes 786440 | tf_op jit(solution)/shard_map/ppermute | solution.py:47
  29.4 1.6 %collective-permute-start.6 = (bf16[2,128,256]{2,1,0:T(8,128)(2,1)S(1)}, bf16[2,128,256]{2,1,0:T(8,128)(2,1)S(1)}, u32[]{:S(2)}, u32[]{:S(2)}) collective-permute-start(bf16[2,128,256]{2,1,0:T(8,128)(2,1)S(1)} %slice_select_fusion.1), channel_id=1, source_target_pairs={{0,1},{1,0},{2,3},{3,2},{4,5},{5,4},{6,7},{7,6},{8,9},{9,8},{10,11... | collective-permute-start | bytes 393224 | tf_op jit(solution)/shard_map/ppermute | solution.py:52
  71.0 2.0 %collective-permute-start.16 = (bf16[768,256]{1,0:T(8,128)(2,1)S(1)}, bf16[768,256]{1,0:T(8,128)(2,1)}, u32[]{:S(2)}, u32[]{:S(2)}) collective-permute-start(bf16[768,256]{1,0:T(8,128)(2,1)S(1)} %bitcast.38), channel_id=1, source_target_pairs={{0,1},{1,0},{2,3},{3,2},{4,5},{5,4},{6,7},{7,6},{8,9},{9,8},{10,11... | collective-permute-start | bytes 1179656 | tf_op jit(solution)/shard_map/ppermute | solution.py:52
  74.2 7.2 %collective-permute-start.17 = (bf16[384,256]{1,0:T(8,128)(2,1)S(1)}, bf16[384,256]{1,0:T(8,128)(2,1)S(1)}, u32[]{:S(2)}, u32[]{:S(2)}) collective-permute-start(bf16[384,256]{1,0:T(8,128)(2,1)S(1)} %select_convert_fusion.1), channel_id=1, source_target_pairs={{0,2},{2,0},{4,6},{6,4},{8,10},{10,8},{12,14},{14,12},{1,3},{3,1},... | collective-permute-start | bytes 589832 | tf_op jit(solution)/shard_map/ppermute | solution.py:52
  81.5 9.8 %collective-permute-start.20 = (bf16[384,256]{1,0:T(8,128)(2,1)S(1)}, bf16[384,256]{1,0:T(8,128)(2,1)S(1)}, u32[]{:S(2)}, u32[]{:S(2)}) collective-permute-start(bf16[384,256]{1,0:T(8,128)(2,1)S(1)} %add_convert_fusion.1), channel_id=1, source_target_pairs={{0,12},{2,14},{4,8},{6,10},{8,4},{10,6},{12,0},{14,2},{1,13},{3,15... | collective-permute-start | bytes 589832 | tf_op jit(solution)/shard_map/ppermute | solution.py:52
  81.6 20.0 %collective-permute-start.19 = (bf16[384,256]{1,0:T(8,128)(2,1)S(1)}, bf16[384,256]{1,0:T(8,128)(2,1)S(1)}, u32[]{:S(2)}, u32[]{:S(2)}) collective-permute-start(bf16[384,256]{1,0:T(8,128)(2,1)S(1)} %add_convert_fusion.1), channel_id=1, source_target_pairs={{0,8},{2,10},{4,12},{6,14},{8,0},{10,2},{12,4},{14,6},{1,9},{3,11}... | collective-permute-start | bytes 589832 | tf_op jit(solution)/shard_map/ppermute | solution.py:52
  84.6 17.0 %collective-permute-start.18 = (bf16[384,256]{1,0:T(8,128)(2,1)S(1)}, bf16[384,256]{1,0:T(8,128)(2,1)S(1)}, u32[]{:S(2)}, u32[]{:S(2)}) collective-permute-start(bf16[384,256]{1,0:T(8,128)(2,1)S(1)} %add_convert_fusion.1), channel_id=1, source_target_pairs={{0,4},{2,6},{4,0},{6,2},{8,12},{10,14},{12,8},{14,10},{1,5},{3,7},... | collective-permute-start | bytes 589832 | tf_op jit(solution)/shard_map/ppermute | solution.py:52
  86.0 1.3 %collective-permute-start.9 = (bf16[2,256,128]{2,1,0:T(8,128)(2,1)S(1)}, bf16[2,256,128]{2,1,0:T(8,128)(2,1)S(1)}, u32[]{:S(2)}, u32[]{:S(2)}) collective-permute-start(bf16[2,256,128]{2,1,0:T(8,128)(2,1)S(1)} %copy-done.10), channel_id=1, source_target_pairs={{0,1},{1,0},{2,3},{3,2},{4,5},{5,4},{6,7},{7,6},{8,9},{9,8},{10,11... | collective-permute-start | bytes 393224 | tf_op jit(solution)/shard_map/ppermute | solution.py:52
  101.7 10.1 %collective-permute-start.21 = (bf16[384,256]{1,0:T(8,128)(2,1)S(1)}, bf16[384,256]{1,0:T(8,128)(2,1)S(1)}, u32[]{:S(2)}, u32[]{:S(2)}) collective-permute-start(bf16[384,256]{1,0:T(8,128)(2,1)S(1)} %add_convert_fusion), channel_id=1, source_target_pairs={{0,2},{2,0},{4,6},{6,4},{8,10},{10,8},{12,14},{14,12},{1,3},{3,1},... | collective-permute-start | bytes 589832 | tf_op jit(solution)/shard_map/ppermute | solution.py:52
  103.8 20.9 %collective-permute-start.15 = (bf16[256,512]{1,0:T(8,128)(2,1)S(1)}, bf16[256,512]{1,0:T(8,128)(2,1)S(1)}, u32[]{:S(2)}, u32[]{:S(2)}) collective-permute-start(bf16[256,512]{1,0:T(8,128)(2,1)S(1)} %get-tuple-element.32), channel_id=1, source_target_pairs={{0,2},{2,0},{4,6},{6,4},{8,10},{10,8},{12,14},{14,12},{1,3},{3,1},... | collective-permute-start | bytes 786440 | tf_op jit(solution)/shard_map/ppermute | solution.py:52
  104.4 8.7 %collective-permute-start.10 = (bf16[256,512]{1,0:T(8,128)(2,1)S(1)}, bf16[256,512]{1,0:T(8,128)(2,1)S(1)}, u32[]{:S(2)}, u32[]{:S(2)}) collective-permute-start(bf16[256,512]{1,0:T(8,128)(2,1)S(1)} %get-tuple-element.33), channel_id=1, source_target_pairs={{4,0},{6,2},{8,4},{10,6},{12,8},{14,10},{5,1},{7,3},{9,5},{11,7},{... | collective-permute-start | bytes 786440 | tf_op jit(solution)/shard_map/ppermute | solution.py:47
  105.7 13.2 %collective-permute-start.11 = (bf16[256,512]{1,0:T(8,128)(2,1)S(1)}, bf16[256,512]{1,0:T(8,128)(2,1)S(1)}, u32[]{:S(2)}, u32[]{:S(2)}) collective-permute-start(bf16[256,512]{1,0:T(8,128)(2,1)S(1)} %get-tuple-element.34), channel_id=1, source_target_pairs={{0,2},{2,0},{4,6},{6,4},{8,10},{10,8},{12,14},{14,12},{1,3},{3,1},... | collective-permute-start | bytes 786440 | tf_op jit(solution)/shard_map/ppermute | solution.py:52
  107.3 11.7 %collective-permute-start.13 = (bf16[256,512]{1,0:T(8,128)(2,1)S(1)}, bf16[256,512]{1,0:T(8,128)(2,1)S(1)}, u32[]{:S(2)}, u32[]{:S(2)}) collective-permute-start(bf16[256,512]{1,0:T(8,128)(2,1)S(1)} %get-tuple-element.36), channel_id=1, source_target_pairs={{0,4},{2,6},{4,8},{6,10},{8,12},{10,14},{1,5},{3,7},{5,9},{7,11},{... | collective-permute-start | bytes 786440 | tf_op jit(solution)/shard_map/ppermute | solution.py:47
  111.9 18.2 %collective-permute-start.22 = (bf16[768,256]{1,0:T(8,128)(2,1)S(1)}, bf16[768,256]{1,0:T(8,128)(2,1)S(1)}, u32[]{:S(2)}, u32[]{:S(2)}) collective-permute-start(bf16[768,256]{1,0:T(8,128)(2,1)S(1)} %pad_maximum_fusion), channel_id=1, source_target_pairs={{0,1},{1,0},{2,3},{3,2},{4,5},{5,4},{6,7},{7,6},{8,9},{9,8},{10,11... | collective-permute-start | bytes 1179656 | tf_op jit(solution)/shard_map/ppermute | solution.py:52
  119.2 5.9 %collective-permute-start.14 = (bf16[256,512]{1,0:T(8,128)(2,1)S(1)}, bf16[256,512]{1,0:T(8,128)(2,1)S(1)}, u32[]{:S(2)}, u32[]{:S(2)}) collective-permute-start(bf16[256,512]{1,0:T(8,128)(2,1)S(1)} %get-tuple-element.47), channel_id=1, source_target_pairs={{0,4},{2,6},{4,8},{6,10},{8,12},{10,14},{1,5},{3,7},{5,9},{7,11},{... | collective-permute-start | bytes 786440 | tf_op jit(solution)/shard_map/ppermute | solution.py:47
  120.5 8.7 %collective-permute-start.12 = (bf16[256,512]{1,0:T(8,128)(2,1)S(1)}, bf16[256,512]{1,0:T(8,128)(2,1)S(1)}, u32[]{:S(2)}, u32[]{:S(2)}) collective-permute-start(bf16[256,512]{1,0:T(8,128)(2,1)S(1)} %get-tuple-element.48), channel_id=1, source_target_pairs={{4,0},{6,2},{8,4},{10,6},{12,8},{14,10},{5,1},{7,3},{9,5},{11,7},{... | collective-permute-start | bytes 786440 | tf_op jit(solution)/shard_map/ppermute | solution.py:47
  121.8 1.3 collective-permute-start.8
  (12 other events, 104.4 us)

commit v2 on v1

v2 whole, which is shorter than its diff:
```python
import functools
import math

import jax
import jax.numpy as jnp
from jax import lax
from jax.experimental import pallas as pl
from jax.experimental.pallas import tpu as pltpu
from jax.sharding import PartitionSpec as P

HEADS = 8
DH = 32
COLS = 64
WMAX = 2
BROWS = 2

SCALE = 1.5 / math.sqrt(DH)
MASKED = -1e30
LOG2E = 1.4426950408889634
F32 = jnp.float32
BF16 = jnp.bfloat16
NN = (((1,), (0,)), ((), ()))
NT = (((1,), (1,)), ((), ()))


def dot(left, right, dims=NN):
    return lax.dot_general(left, right, dims, preferred_element_type=F32)


def halves_of(value):
    high = value.astype(BF16)
    return high, (value - high.astype(F32)).astype(BF16)


def left_split_dot(left, right, dims=NN):
    high, low = halves_of(left)
    return dot(high, right, dims) + dot(low, right, dims)


def right_split_dot(left, right, dims=NN):
    high, low = halves_of(right)
    return dot(left, high, dims) + dot(left, low, dims)


def swapped(array, axis, mask):
    pairs = [(i, i ^ mask) for i in range(lax.axis_size(axis))]
    return lax.ppermute(array, axis, pairs)


def along(array, parity):
    devices = lax.axis_size("frame")
    pairs = [(i, i + 2) for i in range(devices) if (i & 2) == parity and i + 2 < devices]
    return lax.ppermute(array, "frame", pairs + [(j, i) for i, j in pairs])


def whole_call(
    body, outs, args, smem=(), scratch=(), grid=None, flops=0, moved=0, name=None, vmem=16
):
    specs = [
        pl.BlockSpec(memory_space=pltpu.SMEM if i in smem else pltpu.VMEM)
        for i in range(len(args))
    ]
    more = {} if grid is None else {"grid": grid}
    return pl.pallas_call(
        body,
        out_shape=[jax.ShapeDtypeStruct(shape, dtype) for shape, dtype in outs],
        in_specs=specs,
        out_specs=[pl.BlockSpec(memory_space=pltpu.VMEM)] * len(outs),
        scratch_shapes=list(scratch),
        compiler_params=pltpu.CompilerParams(vmem_limit_bytes=vmem * 1024 * 1024),
        cost_estimate=pl.CostEstimate(flops=flops, bytes_accessed=moved, transcendentals=0),
        name=name,
        **more,
    )(*args)


def before_kernel(
    meta, cot, gain, edge, tokens, taps, shared, outp,
    resid_out, rb_out, ext_out, up_out, upt_out, query_out, queryt_out,
):
    row_id = meta[2]
    count = cot.shape[0]
    grad_z = cot[...].astype(F32) * gain[...]
    got = edge[...]
    none = jnp.zeros_like(got)
    ext_out[:COLS] = jnp.where(row_id == 0, none, got)
    ext_out[COLS : COLS + count] = grad_z.astype(BF16)
    ext_out[COLS + count :] = jnp.where(row_id == 0, got, none)
    total = grad_z
    for tap in range(3):
        begin = (2 - tap) * COLS
        total = total + dot(ext_out[begin : begin + count], taps[tap], NT)
    resid_out[...] = total
    rounded = total.astype(BF16)
    rb_out[...] = rounded
    upstream = dot(rounded, outp[...], NT).astype(BF16)
    up_out[...] = upstream
    upt_out[...] = upstream.T
    query = dot(tokens[...], shared[...]).astype(BF16)
    query_out[...] = query
    queryt_out[...] = query.T


def attention_kernel(
    meta, slots, halo, query, queryt, up, upt, tokens, rb, ext, resid_grad, shared, value, outp,
    mid_out, send_out, keep_out, hidden_out, resid_out, base_out,
    key_all, val_all, key_blk, val_blk, keyt_blk, valt_blk, bias, mixed_all, dq_all, dkt, dvt, sums,
):
    step = pl.program_id(0)
    window, row_id, total_rows = meta[1], meta[2], meta[3]
    width = query.shape[1]
    count = query.shape[0]
    rim = WMAX * COLS
    block = BROWS * COLS
    span = block + 2 * rim

    @pl.when(step == 0)
    def _():
        for slot in range(2):
            for weight, full in ((shared, key_all), (value, val_all)):
                full[slot, rim : rim + count] = dot(slots[slot], weight[...]).astype(BF16)
                far = dot(halo[slot], weight[...]).astype(BF16)
                none = jnp.zeros_like(far)
                full[slot, :rim] = jnp.where(row_id == 0, none, far)
                full[slot, rim + count :] = jnp.where(row_id == 0, far, none)
        dkt[...] = jnp.zeros_like(dkt)
        dvt[...] = jnp.zeros_like(dvt)

    begin = pl.multiple_of(step * block, block)
    for slot in range(2):
        key_blk[slot * span : (slot + 1) * span] = key_all[slot, pl.ds(begin, span)]
        val_blk[slot * span : (slot + 1) * span] = val_all[slot, pl.ds(begin, span)]
    keyt_blk[...] = key_blk[...].T
    valt_blk[...] = val_blk[...].T
    first_row = row_id * (count // COLS) + step * BROWS
    query_row = first_row + lax.broadcasted_iota(jnp.int32, (block, span), 0) // COLS
    key_row = first_row - WMAX + lax.broadcasted_iota(jnp.int32, (block, span), 1) // COLS
    near = jnp.abs(query_row - key_row) <= window
    allowed = near & (key_row >= 0) & (key_row < total_rows)
    one_bias = jnp.where(allowed, 0.0, MASKED)
    bias[:, :span] = one_bias
    bias[:, span:] = one_bias

    def all_heads(rows):
        return jnp.concatenate([rows * mask.astype(BF16) for mask in masks], 0)

    def own_lanes(stacked):
        total = jnp.zeros((block, width), F32)
        for head, mask in enumerate(masks):
            total = total + stacked[head * block : (head + 1) * block] * mask
        return total

    lane_head = lax.broadcasted_iota(jnp.int32, (1, width), 1) // DH
    masks = [(lane_head == head).astype(F32) for head in range(HEADS)]
    cube = (HEADS, block, 2 * span)
    flat = (HEADS * block, 2 * span)
    scores = dot(all_heads(query[pl.ds(begin, block), :]), keyt_blk[...]).reshape(cube)
    scores = scores + bias[...][None]
    top = jnp.max(scores, axis=2, keepdims=True)
    terms = jnp.exp2((scores - top) * (SCALE * LOG2E))
    weights = terms * (1.0 / jnp.sum(terms, axis=2, keepdims=True))
    prob = weights.astype(BF16)
    mixed_all[pl.ds(begin, block), :] = own_lanes(
        dot(prob.reshape(flat), val_blk[...])
    ).astype(BF16)
    grad_prob = dot(all_heads(up[pl.ds(begin, block), :]), valt_blk[...]).reshape(cube)
    inner = jnp.sum(weights * grad_prob, axis=2, keepdims=True)
    grad_score = ((weights * (grad_prob - inner)) * SCALE).astype(BF16)
    dq_all[pl.ds(begin, block), :] = own_lanes(dot(grad_score.reshape(flat), key_blk[...]))
    for head in range(HEADS):
        lanes = slice(head * DH, (head + 1) * DH)
        dv = dot(upt[lanes, pl.ds(begin, block)], prob[head])
        dk = dot(queryt[lanes, pl.ds(begin, block)], grad_score[head])
        for slot in range(2):
            dvt[slot, lanes, pl.ds(begin, span)] += dv[:, slot * span : (slot + 1) * span]
            dkt[slot, lanes, pl.ds(begin, span)] += dk[:, slot * span : (slot + 1) * span]

    @pl.when(step == pl.num_programs(0) - 1)
    def _():
        def far_rim(array):
            upper, lower = array[:, :rim], array[:, rim + count :]
            return jnp.where(row_id == 0, lower, upper)

        half = 3 * width
        middle = slice(rim, rim + count)
        grad_q = dq_all[...]
        shared_t = jnp.zeros((width, width), F32)
        value_t = jnp.zeros((width, width), F32)
        for slot in range(2):
            part = jnp.zeros((width, count + 2 * rim), F32)
            for piece in halves_of(dkt[slot]):
                part = part + dot(shared[...], piece)
                rims = far_rim(piece)
                shared_t += dot(piece[:, middle], slots[slot]) + dot(rims, halo[slot])
            for piece in halves_of(dvt[slot]):
                part = part + dot(value[...], piece)
                rims = far_rim(piece)
                value_t += dot(piece[:, middle], slots[slot]) + dot(rims, halo[slot])
            mid_out[slot] = part[:, middle]
            send_out[half:, slot * rim : (slot + 1) * rim] = far_rim(part).astype(BF16)
        base_out[...] = resid_grad[...] + left_split_dot(grad_q, shared[...], NT)
        sums[:width] = right_split_dot(tokens[...].T, grad_q) + shared_t.T
        sums[width : 2 * width] = value_t.T
        mixed_full = mixed_all[...]
        residual = tokens[...].astype(F32) + dot(mixed_full, outp[...])
        resid_out[...] = residual
        hidden = residual.astype(BF16)
        hidden_out[...] = hidden
        sums[2 * width : half] = dot(mixed_full.T, rb[...])
        hidden_t = hidden.T
        for tap in range(3):
            start = (2 - tap) * COLS
            sums[half + tap * width : half + (tap + 1) * width] = dot(
                hidden_t, ext[start : start + count]
            )
        keep_out[...] = sums[pl.ds(pl.multiple_of(row_id * half, half), half)]
        send_out[:half] = sums[pl.ds(pl.multiple_of((1 - row_id) * half, half), half)].astype(BF16)


def spread_kernel(
    meta, mid, keep, got,
    pair_out, across_out, first_out, second_out, third_out, first_keep, second_keep, own_out,
):
    frame_id, row_id = meta[0], meta[2]
    steps = [meta[4] - frame_id, meta[5] - frame_id]
    width, count = mid.shape[1], mid.shape[2]
    rim = WMAX * COLS
    half = keep.shape[0]
    piece = half // 4
    parts = []
    for slot in range(2):
        rims = got[half:, slot * rim : (slot + 1) * rim].astype(F32)
        none = jnp.zeros_like(rims)
        part = mid[slot]
        first = part[:, :rim] + jnp.where(row_id == 0, none, rims)
        last = part[:, count - rim :] + jnp.where(row_id == 0, rims, none)
        parts.append(jnp.concatenate([first, part[:, rim : count - rim], last], 1))

    def part_for(step):
        chosen = jnp.zeros((width, count), F32)
        for slot in range(2):
            chosen = chosen + jnp.where(steps[slot] == step, parts[slot], 0.0)
        return chosen

    pair_step = jnp.where((frame_id & 1) == 0, 1, -1)
    link_step = jnp.where((frame_id & 2) == 0, 1, -1)
    pair_out[...] = part_for(pair_step).astype(BF16)
    across_out[:width] = part_for(-pair_step).astype(BF16)
    first_out[:width] = part_for(4 * link_step).astype(BF16)
    second_out[...] = part_for(-4 * link_step).astype(BF16)
    first_keep[...] = part_for(2 * link_step)
    second_keep[...] = part_for(-2 * link_step)
    me = frame_id & 3

    def rows_of(index):
        rows = pl.ds(pl.multiple_of(index * piece, piece), piece)
        return keep[rows] + got[rows].astype(F32)

    own_out[...] = rows_of(me)
    for mask, out, begin in ((1, across_out, width), (2, first_out, width), (3, third_out, 0)):
        rows = rows_of(me ^ mask).astype(BF16)
        out[begin:, :width] = rows[: piece // 2]
        out[begin:, width:] = rows[piece // 2 :]


def coded_kernel(meta, hidden, halo, residual, gain, taps, coded_out, ext):
    row_id = meta[2]
    count = hidden.shape[0]
    got = halo[...]
    none = jnp.zeros_like(got)
    ext[:COLS] = jnp.where(row_id == 0, none, got)
    ext[COLS : COLS + count] = hidden[...]
    ext[COLS + count :] = jnp.where(row_id == 0, got, none)
    total = jnp.zeros((count, hidden.shape[1]), F32)
    for tap in range(3):
        begin = tap * COLS
        total = total + dot(ext[begin : begin + count], taps[tap])
    coded_out[...] = ((residual[...] + total) * gain[...]).astype(BF16)


def final_kernel(base, first, second, third, grad_out):
    returned = first[...].astype(F32) + second[...].astype(F32) + third[...].astype(F32)
    grad_out[...] = (base[...] + returned.T).astype(BF16)


def weights_kernel(meta, own, other, shared_out, value_out, output_out, taps_out, *, norm):
    row_id = meta[2]
    width = shared_out.shape[1]
    low = jnp.where(row_id == 0, own[...].astype(F32), other[...].astype(F32)) * norm
    high = jnp.where(row_id == 0, other[...].astype(F32), own[...].astype(F32)) * norm
    shared_out[...] = low[:width]
    value_out[...] = low[width : 2 * width]
    output_out[...] = low[2 * width :]
    for tap in range(3):
        taps_out[tap] = high[tap * width : (tap + 1) * width]


def local(
    latents, ref_frames, windows, quant_level, quant_scale,
    shared_proj, value_proj, output_proj, conv_taps, cotangent,
):
    width = latents.shape[2]
    count = latents.shape[1]
    rows_dev = count // COLS
    frames = lax.axis_size("frame")
    total_rows = rows_dev * lax.axis_size("row")
    frame_id = lax.axis_index("frame")
    row_id = lax.axis_index("row")
    refs = ref_frames[0]
    odd = (frame_id & 1) == 1
    rim = WMAX * COLS
    tokens = latents[0]
    low_link = (frame_id & 2) == 0
    meta = jnp.concatenate(
        [jnp.stack([frame_id, windows[0], row_id, jnp.int32(total_rows)]).astype(jnp.int32), refs]
    )
    gain = lax.dynamic_slice_in_dim(quant_scale, quant_level[0], 1, 0)

    from_pair = swapped(tokens, "frame", 1)
    from_first = along(tokens, 0)
    from_second = along(tokens, 2)
    from_before = jnp.where(low_link, from_second, from_first)
    from_after = jnp.where(low_link, from_first, from_second)

    cot = cotangent[0]
    cot_edge = jnp.where(row_id == 0, cot[count - COLS :], cot[:COLS])
    grad_edge = swapped((cot_edge.astype(F32) * gain).astype(BF16), "row", 1)
    grad_resid, grad_rb, grad_ext, up, upt, query, queryt = whole_call(
        before_kernel,
        [
            ((count, width), F32),
            ((count, width), BF16),
            ((count + 2 * COLS, width), BF16),
            ((count, width), BF16),
            ((width, count), BF16),
            ((count, width), BF16),
            ((width, count), BF16),
        ],
        (meta, cot, gain, grad_edge, tokens, conv_taps, shared_proj, output_proj),
        smem=(0,),
        flops=2 * 5 * count * width * width,
        moved=4 * count * width * 6,
        name="gradient_path",
    )

    far_first = along(from_second, 0)
    far_second = along(from_first, 2)
    from_cross = swapped(jnp.where(odd, from_before, from_after), "frame", 1)
    from_before_2 = jnp.where(low_link, far_second, far_first)
    from_after_2 = jnp.where(low_link, far_first, far_second)
    pair_step = jnp.where(odd, -1, 1)
    distance = (refs - frame_id)[:, None, None]
    slots = jnp.where(distance == pair_step, from_pair[None], from_cross[None])
    for step, source in (
        (-2, from_before), (2, from_after), (-4, from_before_2), (4, from_after_2)
    ):
        slots = jnp.where(distance == step, source[None], slots)
    halo = swapped(jnp.where(row_id == 0, slots[:, count - rim :], slots[:, :rim]), "row", 1)

    block = BROWS * COLS
    span = block + 2 * rim
    ext_count = count + 2 * rim
    half = 3 * width
    mid, send, keep, hidden, residual, base = whole_call(
        attention_kernel,
        [
            ((2, width, count), F32),
            ((half + width, width), BF16),
            ((half, width), F32),
            ((count, width), BF16),
            ((count, width), F32),
            ((count, width), F32),
        ],
        (
            meta, slots, halo, query, queryt, up, upt, tokens, grad_rb, grad_ext, grad_resid,
            shared_proj, value_proj, output_proj,
        ),
        smem=(0,),
        scratch=[
            pltpu.VMEM((2, ext_count, width), BF16),
            pltpu.VMEM((2, ext_count, width), BF16),
            pltpu.VMEM((2 * span, width), BF16),
            pltpu.VMEM((2 * span, width), BF16),
            pltpu.VMEM((width, 2 * span), BF16),
            pltpu.VMEM((width, 2 * span), BF16),
            pltpu.VMEM((block, 2 * span), F32),
            pltpu.VMEM((count, width), BF16),
            pltpu.VMEM((count, width), F32),
            pltpu.VMEM((2, width, ext_count), F32),
            pltpu.VMEM((2, width, ext_count), F32),
            pltpu.VMEM((2 * half, width), F32),
        ],
        grid=(count // block,),
        flops=6 * 2 * count * 2 * span * width * HEADS,
        moved=count * width * 60,
        name="attention",
        vmem=28,
    )

    got = swapped(send, "row", 1)
    hidden_edge = jnp.where(row_id == 0, hidden[count - COLS :], hidden[:COLS])
    hidden_halo = swapped(hidden_edge, "row", 1)
    piece = half // 4
    packed = piece // 2
    pair, across, first, second, third, first_keep, second_keep, own = whole_call(
        spread_kernel,
        [
            ((width, count), BF16),
            ((width + packed, count), BF16),
            ((width + packed, count), BF16),
            ((width, count), BF16),
            ((packed, count), BF16),
            ((width, count), F32),
            ((width, count), F32),
            ((piece, width), F32),
        ],
        (meta, mid, keep, got),
        smem=(0,),
        flops=count * width * 12,
        moved=count * width * 30,
        name="spread",
    )

    across = swapped(across, "frame", 1)
    first = along(first, 0)
    second = along(second, 2)
    third = swapped(third, "frame", 3)

    def unpacked(array):
        return jnp.concatenate([array[:, :width], array[:, width:]], 0).astype(F32)

    total = (own + unpacked(across[width:])) + (unpacked(first[width:]) + unpacked(third))
    mask = 4
    while mask < frames:
        total = total.astype(BF16)
        total = total.astype(F32) + swapped(total, "frame", mask).astype(F32)
        mask *= 2
    own = total.astype(BF16)

    back_pair = swapped(pair, "frame", 1)
    crossing = across[:width].astype(F32)
    with_first = odd != low_link
    back_first = along(
        (first_keep + second.astype(F32) + jnp.where(with_first, crossing, 0.0)).astype(BF16), 0
    )
    back_second = along(
        (second_keep + first[:width].astype(F32) + jnp.where(with_first, 0.0, crossing)).astype(
            BF16
        ),
        2,
    )

    me = frame_id & 3
    pieces = jnp.zeros((4, piece, width), BF16)
    pieces = lax.dynamic_update_index_in_dim(pieces, own, me, 0)
    for mask in (1, 2, 3):
        pieces = lax.dynamic_update_index_in_dim(
            pieces, swapped(own, "frame", mask), me ^ mask, 0
        )
    pieces = pieces.reshape(half, width)
    other = swapped(pieces, "row", 1)
    shared_grad, value_grad, output_grad, taps_grad = whole_call(
        functools.partial(
            weights_kernel, norm=1.0 / math.sqrt(frames * total_rows * COLS)
        ),
        [
            ((width, width), F32),
            ((width, width), F32),
            ((width, width), F32),
            ((3, width, width), F32),
        ],
        (meta, pieces, other),
        smem=(0,),
        flops=6 * width * width,
        moved=6 * width * width * 6,
        name="weight_gradients",
    )

    (coded,) = whole_call(
        coded_kernel,
        [((count, width), BF16)],
        (meta, hidden, hidden_halo, residual, gain, conv_taps),
        smem=(0,),
        scratch=[pltpu.VMEM((count + 2 * COLS, width), BF16)],
        flops=2 * 3 * count * width * width,
        moved=count * width * 8,
        name="context",
    )
    (grad_latents,) = whole_call(
        final_kernel,
        [((count, width), BF16)],
        (base, back_first, back_second, back_pair),
        flops=count * width * 4,
        moved=count * width * 12,
        name="latent_gradient",
    )
    return (
        coded[None],
        grad_latents[None],
        shared_grad,
        value_grad,
        output_grad,
        taps_grad,
    )


def solution(mesh):
    placed = (
        P(("groups", "frame"), "row", None),
        P(("groups", "frame"), None),
        P(("groups", "frame")),
        P(("groups", "frame")),
        P(),
        P(),
        P(),
        P(),
        P(),
        P(("groups", "frame"), "row", None),
    )
    return jax.shard_map(
        local,
        mesh=mesh,
        in_specs=placed,
        out_specs=(
            P(("groups", "frame"), "row", None),
            P(("groups", "frame"), "row", None),
            P("groups", None),
            P("groups", None),
            P("groups", None),
            P("groups", None, None),
        ),
        check_vma=False,
    )
```

time: 133 us -> 97.2 us (0.73)
  Pallas kernels: 37.5 us -> 23.6 us
  waiting for transfers between devices: 46.2 us -> 33.1 us
  other arithmetic: 7.2 us -> 3.18 us
  local copies, waits for them, and re-layouts: 6.85 us -> 3.92 us
  starting transfers between devices: 32.2 us -> 30.2 us
    pallas_call x4 -> x6, Pallas kernels: 37.5 us -> 23.6 us  [whole_call(): pl.pallas_call(body, out_shape=[jax.ShapeDtypeStruct(shape, dtype) for sh...]
    ppermute x8, waiting for transfers between devices: 17.9 us -> 7.99 us  [along(): return lax.ppermute(array, 'frame', pairs + [(j, i) for i, j in pairs])]
    ppermute x15 -> x14, waiting for transfers between devices: 28.3 us -> 25.1 us  [swapped(): return lax.ppermute(array, axis, pairs)]
    ppermute x8, starting transfers between devices: 18 us -> 15.8 us  [along(): return lax.ppermute(array, 'frame', pairs + [(j, i) for i, j in pairs])]
    unnamed x26 -> x28, local copies, waits for them, and re-layouts: 5.01 us -> 2.86 us
    slice x2 -> x3, local copies, waits for them, and re-layouts: 1.82 us -> 0.02 us  [unpacked(): return jnp.concatenate([array[:, :width], array[:, width:]], 0).astype(F32)]
    select_n x3 -> x1, other arithmetic: 1.64 us -> 0.04 us  [local(): from_after_2 = jnp.where(low_link, far_first, far_second)]
    dynamic_update_slice x0 -> x1, other arithmetic: none -> 1.56 us  [local(): pieces = lax.dynamic_update_index_in_dim(pieces, own, me, 0)]
  transfers between devices with their start and end apart: 23 -> 22, of which waited for: 13 -> 11; matrix products, arithmetic and copies ran while one was open for 3% -> 2% of each run, Pallas kernels for 3% -> 4%
where the time goes in v2:
time: 97.2 us; the launch traced here: 96.2 us
  waiting for transfers between devices  33.1 us (34%)
  starting transfers between devices  30.2 us (31%)
  Pallas kernels  23.6 us (24%)
  local copies, waits for them, and re-layouts  3.92 us (4%)
  other arithmetic  3.18 us (3%)
  between operations  2.25 us (2%)
    ppermute x14, waiting for transfers between devices, swapped(): return lax.ppermute(array, axis, pairs)  25.1 us
    pallas_call x6, Pallas kernels, whole_call(): pl.pallas_call(body, out_shape=[jax.ShapeDtypeStruct(shape, dtype) for sh...  23.6 us
    ppermute x8, starting transfers between devices, along(): return lax.ppermute(array, 'frame', pairs + [(j, i) for i, j in pairs])  15.8 us
    ppermute x14, starting transfers between devices, swapped(): return lax.ppermute(array, axis, pairs)  14.4 us
    ppermute x8, waiting for transfers between devices, along(): return lax.ppermute(array, 'frame', pairs + [(j, i) for i, j in pairs])  7.99 us
    unnamed x28, local copies, waits for them, and re-layouts  2.86 us
  transfers between devices with their start and end apart: 22, of which 11 were waited for; matrix products, arithmetic and copies ran while one was open for 2% of the time, Pallas kernels for 4%

profile of v2, /device:TPU:0, one launch (start us, length us, event | category | flops | bytes accessed | tf_op | source)
XLA Modules:
  0.0 96.2 jit_solution(1489431719416977708)
XLA Ops:
  1.5 5.9 %collective-permute-start.2 = (bf16[512,256]{1,0:T(8,128)(2,1)}, bf16[512,256]{1,0:T(8,128)(2,1)S(1)}, u32[]{:S(2)}, u32[]{:S(2)}) collective-permute-start(bf16[512,256]{1,0:T(8,128)(2,1)} %bitcast.31), channel_id=1, source_target_pairs={{0,4},{2,6},{8,12},{10,14},{4,0},{6,2},{12,8},{14,10},{1,5},{3,7},... | collective-permute-start | bytes 786440 | tf_op jit(solution)/shard_map/ppermute | solution.py:53
  7.4 1.5 %collective-permute-start.4 = (bf16[512,256]{1,0:T(8,128)(2,1)}, bf16[512,256]{1,0:T(8,128)(2,1)S(1)}, u32[]{:S(2)}, u32[]{:S(2)}) collective-permute-start(bf16[512,256]{1,0:T(8,128)(2,1)} %bitcast.32), channel_id=1, source_target_pairs={{0,2},{2,0},{4,6},{6,4},{8,10},{10,8},{12,14},{14,12},{1,3},{3,1},... | collective-permute-start | bytes 786440 | tf_op jit(solution)/shard_map/ppermute | solution.py:47
  10.2 3.8 %collective-permute-start.1 = (bf16[512,256]{1,0:T(8,128)(2,1)S(1)}, bf16[512,256]{1,0:T(8,128)(2,1)S(1)}, u32[]{:S(2)}, u32[]{:S(2)}) collective-permute-start(bf16[512,256]{1,0:T(8,128)(2,1)S(1)} %collective-permute-done), channel_id=1, source_target_pairs={{0,4},{2,6},{8,12},{10,14},{4,0},{6,2},{12,8},{14,10},{1,5},{3,7},... | collective-permute-start | bytes 786440 | tf_op jit(solution)/shard_map/ppermute | solution.py:53
  14.7 1.6 %collective-permute-start.5 = (bf16[512,256]{1,0:T(8,128)(2,1)S(1)}, bf16[512,256]{1,0:T(8,128)(2,1)S(1)}, u32[]{:S(2)}, u32[]{:S(2)}) collective-permute-start(bf16[512,256]{1,0:T(8,128)(2,1)S(1)} %get-tuple-element.58), channel_id=1, source_target_pairs={{0,2},{2,0},{4,6},{6,4},{8,10},{10,8},{12,14},{14,12},{1,3},{3,1},... | collective-permute-start | bytes 786440 | tf_op jit(solution)/shard_map/ppermute | solution.py:47
  16.3 3.1 %collective-permute-done.1 = bf16[512,256]{1,0:T(8,128)(2,1)S(1)} collective-permute-done((bf16[512,256]{1,0:T(8,128)(2,1)S(1)}, bf16[512,256]{1,0:T(8,128)(2,1)S(1)}, u32[]{:S(2)}, u32[]{:S(2)}) %collective-permute-start.1) | collective-permute-done | bytes 262176 | tf_op jit(solution)/shard_map/ppermute | solution.py:53
  19.4 2.2 %collective-permute-done.5 = bf16[512,256]{1,0:T(8,128)(2,1)S(1)} collective-permute-done((bf16[512,256]{1,0:T(8,128)(2,1)S(1)}, bf16[512,256]{1,0:T(8,128)(2,1)S(1)}, u32[]{:S(2)}, u32[]{:S(2)}) %collective-permute-start.5) | collective-permute-done | bytes 262176 | tf_op jit(solution)/shard_map/ppermute | solution.py:47
  23.9 1.4 %gradient_path.1 = (f32[512,256]{1,0:T(8,128)S(1)}, bf16[512,256]{1,0:T(8,128)(2,1)S(1)}, bf16[640,256]{1,0:T(8,128)(2,1)S(1)}, bf16[512,256]{1,0:T(8,128)(2,1)S...) custom-call(s32[6]{0:T(128)S(1)} %concatenate.12.meta, ...), custom_call_target="tpu_custom_call" | custom-call | flops 335544320 | bytes 3145728 | tf_op jit(solution)/shard_map/gradient_path/pallas_call | solution.py:64
  25.3 16.9 %attention.1 = (f32[2,256,512]{2,1,0:T(8,128)S(1)}, bf16[1024,256]{1,0:T(8,128)(2,1)S(1)}, f32[768,256]{1,0:T(8,128)S(1)}, bf16[512,256]{1,0:T(8,128)(2,1)S(1)},...) custom-call(s32[6]{0:T(128)S(1)} %concatenate.12.meta, bf16[2,512,256]{2,1,0:T(8,128)(2,1)S(1)} %select_select_fusion.slots, ...), custom_call_target="tpu_custom_call" | custom-call | flops 9663676416 | bytes 7864320 | tf_op jit(solution)/shard_map/attention/pallas_call | solution.py:64
  42.5 1.8 %collective-permute-done.9.got = bf16[1024,256]{1,0:T(8,128)(2,1)S(1)} collective-permute-done((bf16[1024,256]{1,0:T(8,128)(2,1)S(1)}, bf16[1024,256]{1,0:T(8,128)(2,1)S(1)}, u32[]{:S(2)}, u32[]{:S(2)}) %collective-permute-start.9) | collective-permute-done | bytes 524320 | tf_op jit(solution)/shard_map/ppermute | solution.py:47
  45.3 2.9 %collective-permute-start.13 = (bf16[352,512]{1,0:T(8,128)(2,1)S(1)}, bf16[352,512]{1,0:T(8,128)(2,1)S(1)}, u32[]{:S(2)}, u32[]{:S(2)}) collective-permute-start(bf16[352,512]{1,0:T(8,128)(2,1)S(1)} %get-tuple-element.48), channel_id=1, source_target_pairs={{0,4},{2,6},{8,12},{10,14},{4,0},{6,2},{12,8},{14,10},{1,5},{3,7},... | collective-permute-start | bytes 1081352 | tf_op jit(solution)/shard_map/ppermute | solution.py:53
  48.2 1.0 %collective-permute-start.16 = (bf16[96,512]{1,0:T(8,128)(2,1)S(1)}, bf16[96,512]{1,0:T(8,128)(2,1)S(1)}, u32[]{:S(2)}, u32[]{:S(2)}) collective-permute-start(bf16[96,512]{1,0:T(8,128)(2,1)S(1)} %get-tuple-element.51), channel_id=1, source_target_pairs={{0,6},{2,4},{4,2},{6,0},{8,14},{10,12},{12,10},{14,8},{1,7},{3,5},... | collective-permute-start | bytes 294920 | tf_op jit(solution)/shard_map/ppermute | solution.py:47
  49.7 10.3 %collective-permute-done.16 = bf16[96,512]{1,0:T(8,128)(2,1)S(1)} collective-permute-done((bf16[96,512]{1,0:T(8,128)(2,1)S(1)}, bf16[96,512]{1,0:T(8,128)(2,1)S(1)}, u32[]{:S(2)}, u32[]{:S(2)}) %collective-permute-start.16) | collective-permute-done | bytes 98336 | tf_op jit(solution)/shard_map/ppermute | solution.py:47
  60.1 1.4 %collective-permute-done.11 = bf16[352,512]{1,0:T(8,128)(2,1)S(1)} collective-permute-done((bf16[352,512]{1,0:T(8,128)(2,1)S(1)}, bf16[352,512]{1,0:T(8,128)(2,1)S(1)}, u32[]{:S(2)}, u32[]{:S(2)}) %collective-permute-start.11) | collective-permute-done | bytes 360480 | tf_op jit(solution)/shard_map/ppermute | solution.py:47
  62.3 2.7 %collective-permute-start.17 = (bf16[192,256]{1,0:T(8,128)(2,1)S(1)}, bf16[192,256]{1,0:T(8,128)(2,1)}, u32[]{:S(2)}, u32[]{:S(2)}) collective-permute-start(bf16[192,256]{1,0:T(8,128)(2,1)S(1)} %add_convert_fusion.1), channel_id=1, source_target_pairs={{0,8},{2,10},{4,12},{6,14},{8,0},{10,2},{12,4},{14,6},{1,9},{3,11}... | collective-permute-start | bytes 294920 | tf_op jit(solution)/shard_map/ppermute | solution.py:47
  65.0 3.2 %collective-permute-done.17 = bf16[192,256]{1,0:T(8,128)(2,1)} collective-permute-done((bf16[192,256]{1,0:T(8,128)(2,1)S(1)}, bf16[192,256]{1,0:T(8,128)(2,1)}, u32[]{:S(2)}, u32[]{:S(2)}) %collective-permute-start.17) | collective-permute-done | bytes 98336 | tf_op jit(solution)/shard_map/ppermute | solution.py:47
  69.0 1.6 %bitcast_dynamic-update-slice_fusion.3 = (bf16[4,192,256]{2,1,0:T(8,128)(2,1)S(1)}, bf16[192,256]{1,0:T(8,128)(2,1)}) fusion(bf16[4,192,256]{2,1,0:T(8,128)(2,1)S(1)} %broadcast_in_dim.119, s32[]{:T(128)S(6)} %select_n.123, bf16[192,256]{1,0:T(8,128)(2,1)} %collective-permute-done.17, bf16[192,256]{1,0:T(8,128)(2,1)S(1)} %copy-done.9), kind=kLoop, calls=%fused_computation.18 | loop fusion | flops 196608 | bytes 393220 | tf_op jit(solution)/shard_map/jit(dynamic_update_index_in_dim)/dynamic_update_slice | solution.py:455
  71.9 1.6 %collective-permute-start.15 = (bf16[256,512]{1,0:T(8,128)(2,1)S(1)}, bf16[256,512]{1,0:T(8,128)(2,1)S(1)}, u32[]{:S(2)}, u32[]{:S(2)}) collective-permute-start(bf16[256,512]{1,0:T(8,128)(2,1)S(1)} %get-tuple-element.49), channel_id=1, source_target_pairs={{0,2},{2,0},{4,6},{6,4},{8,10},{10,8},{12,14},{14,12},{1,3},{3,1},... | collective-permute-start | bytes 786440 | tf_op jit(solution)/shard_map/ppermute | solution.py:47
  73.5 4.3 %collective-permute-start.19 = (bf16[192,256]{1,0:T(8,128)(2,1)}, bf16[192,256]{1,0:T(8,128)(2,1)S(1)}, u32[]{:S(2)}, u32[]{:S(2)}) collective-permute-start(bf16[192,256]{1,0:T(8,128)(2,1)} %get-tuple-element.57), channel_id=1, source_target_pairs={{0,4},{2,6},{4,0},{6,2},{8,12},{10,14},{12,8},{14,10},{1,5},{3,7},... | collective-permute-start | bytes 294920 | tf_op jit(solution)/shard_map/ppermute | solution.py:47
  78.7 1.9 %collective-permute-done.19 = bf16[192,256]{1,0:T(8,128)(2,1)S(1)} collective-permute-done((bf16[192,256]{1,0:T(8,128)(2,1)}, bf16[192,256]{1,0:T(8,128)(2,1)S(1)}, u32[]{:S(2)}, u32[]{:S(2)}) %collective-permute-start.19) | collective-permute-done | bytes 98336 | tf_op jit(solution)/shard_map/ppermute | solution.py:47
  80.6 2.9 %collective-permute-done.20 = bf16[192,256]{1,0:T(8,128)(2,1)S(1)} collective-permute-done((bf16[192,256]{1,0:T(8,128)(2,1)}, bf16[192,256]{1,0:T(8,128)(2,1)S(1)}, u32[]{:S(2)}, u32[]{:S(2)}) %collective-permute-start.20) | collective-permute-done | bytes 98336 | tf_op jit(solution)/shard_map/ppermute | solution.py:47
  83.7 1.2 %fusion.3 = (bf16[256,512]{1,0:T(8,128)(2,1)S(1)}, bf16[256,512]{1,0:T(8,128)(2,1)S(1)}) fusion(f32[256,512]{1,0:T(8,128)S(1)} %get-tuple-element.47, bf16[352,512]{1,0:T(8,128)(2,1)S(1)} %copy-done.11, pred[]{:T(512)S(6)} %ne.3, bf16[352,512]{1,0:T(8,128)(2,1)} %copy-done.12, f32[256,512]{1,0:T(8,128)S(1)} %get-tuple-element.44, ...), kind=kLoop, calls=%fused_computation.5 | loop fusion | flops 1441792 | bytes 2359297 | tf_op jit(solution)/shard_map/convert_element_type | solution.py:447
  87.1 1.6 %context.1 = bf16[512,256]{1,0:T(8,128)(2,1)} custom-call(s32[6]{0:T(128)S(1)} %concatenate.12.meta, bf16[512,256]{1,0:T(8,128)(2,1)S(1)} %get-tuple-element.38.hidden, bf16[64,256]{1,0:T(8,128)(2,1)S(1)} %collective-permute-done.8.halo, f32[512,256]{1,0:T(8,128)S(1)} %get-tuple-element.39.residual, f32[1,256]{1,0:T(1,128)S(1)} %constant_dynamic-slice_fusion.gain, ...), custom_call_target="tpu_custom_call" | custom-call | flops 201326592 | bytes 1048576 | tf_op jit(solution)/shard_map/context/pallas_call | solution.py:64
  88.7 4.9 %collective-permute-done.12.first = bf16[256,512]{1,0:T(8,128)(2,1)S(1)} collective-permute-done((bf16[256,512]{1,0:T(8,128)(2,1)S(1)}, bf16[256,512]{1,0:T(8,128)(2,1)S(1)}, u32[]{:S(2)}, u32[]{:S(2)}) %collective-permute-start.12) | collective-permute-done | bytes 262176 | tf_op jit(solution)/shard_map/ppermute | solution.py:53
  94.5 1.7 %weight_gradients.1 = (f32[256,256]{1,0:T(8,128)}, f32[256,256]{1,0:T(8,128)}, f32[256,256]{1,0:T(8,128)}, f32[3,256,256]{2,1,0:T(8,128)}) custom-call(s32[6]{0:T(128)S(1)} %concatenate.12.meta, bf16[768,256]{1,0:T(8,128)(2,1)S(1)} %bitcast.27, bf16[768,256]{1,0:T(8,128)(2,1)S(1)} %collective-permute-done.21.other), custom_call_target="tpu_custom_call" | custom-call | flops 393216 | bytes 2359296 | tf_op jit(solution)/shard_map/weight_gradients/pallas_call | solution.py:64
  (74 shorter events, 12.8 us)
Async XLA Ops:
  0.6 15.6 %copy-start = (f32[64,256]{1,0:T(8,128)S(1)}, f32[64,256]{1,0:T(8,128)}, u32[]{:S(2)}) copy-start(f32[64,256]{1,0:T(8,128)} %param.14) | copy-start | bytes 196612
  0.6 9.5 %collective-permute-start = (bf16[512,256]{1,0:T(8,128)(2,1)}, bf16[512,256]{1,0:T(8,128)(2,1)S(1)}, u32[]{:S(2)}, u32[]{:S(2)}) collective-permute-start(bf16[512,256]{1,0:T(8,128)(2,1)} %bitcast.30), channel_id=1, source_target_pairs={{4,8},{6,10},{8,4},{10,6},{5,9},{7,11},{9,5},{11,7},{20,24},{22,26... | collective-permute-start | bytes 786440 | tf_op jit(solution)/shard_map/ppermute | solution.py:53
  1.5 12.5 %collective-permute-start.2 = (bf16[512,256]{1,0:T(8,128)(2,1)}, bf16[512,256]{1,0:T(8,128)(2,1)S(1)}, u32[]{:S(2)}, u32[]{:S(2)}) collective-permute-start(bf16[512,256]{1,0:T(8,128)(2,1)} %bitcast.31), channel_id=1, source_target_pairs={{0,4},{2,6},{8,12},{10,14},{4,0},{6,2},{12,8},{14,10},{1,5},{3,7},... | collective-permute-start | bytes 786440 | tf_op jit(solution)/shard_map/ppermute | solution.py:53
  7.4 12.1 %collective-permute-start.4 = (bf16[512,256]{1,0:T(8,128)(2,1)}, bf16[512,256]{1,0:T(8,128)(2,1)S(1)}, u32[]{:S(2)}, u32[]{:S(2)}) collective-permute-start(bf16[512,256]{1,0:T(8,128)(2,1)} %bitcast.32), channel_id=1, source_target_pairs={{0,2},{2,0},{4,6},{6,4},{8,10},{10,8},{12,14},{14,12},{1,3},{3,1},... | collective-permute-start | bytes 786440 | tf_op jit(solution)/shard_map/ppermute | solution.py:47
  10.2 9.2 %collective-permute-start.1 = (bf16[512,256]{1,0:T(8,128)(2,1)S(1)}, bf16[512,256]{1,0:T(8,128)(2,1)S(1)}, u32[]{:S(2)}, u32[]{:S(2)}) collective-permute-start(bf16[512,256]{1,0:T(8,128)(2,1)S(1)} %collective-permute-done), channel_id=1, source_target_pairs={{0,4},{2,6},{8,12},{10,14},{4,0},{6,2},{12,8},{14,10},{1,5},{3,7},... | collective-permute-start | bytes 786440 | tf_op jit(solution)/shard_map/ppermute | solution.py:53
  14.0 5.4 %collective-permute-start.3 = (bf16[512,256]{1,0:T(8,128)(2,1)S(1)}, bf16[512,256]{1,0:T(8,128)(2,1)S(1)}, u32[]{:S(2)}, u32[]{:S(2)}) collective-permute-start(bf16[512,256]{1,0:T(8,128)(2,1)S(1)} %collective-permute-done.2), channel_id=1, source_target_pairs={{4,8},{6,10},{8,4},{10,6},{5,9},{7,11},{9,5},{11,7},{20,24},{22,26... | collective-permute-start | bytes 786440 | tf_op jit(solution)/shard_map/ppermute | solution.py:53
  14.7 7.0 %collective-permute-start.5 = (bf16[512,256]{1,0:T(8,128)(2,1)S(1)}, bf16[512,256]{1,0:T(8,128)(2,1)S(1)}, u32[]{:S(2)}, u32[]{:S(2)}) collective-permute-start(bf16[512,256]{1,0:T(8,128)(2,1)S(1)} %get-tuple-element.58), channel_id=1, source_target_pairs={{0,2},{2,0},{4,6},{6,4},{8,10},{10,8},{12,14},{14,12},{1,3},{3,1},... | collective-permute-start | bytes 786440 | tf_op jit(solution)/shard_map/ppermute | solution.py:47
  22.0 3.4 %collective-permute-start.6 = (bf16[2,128,256]{2,1,0:T(8,128)(2,1)S(1)}, bf16[2,128,256]{2,1,0:T(8,128)(2,1)S(1)}, u32[]{:S(2)}, u32[]{:S(2)}) collective-permute-start(bf16[2,128,256]{2,1,0:T(8,128)(2,1)S(1)} %slice_select_fusion), channel_id=1, source_target_pairs={{0,1},{1,0},{2,3},{3,2},{4,5},{5,4},{6,7},{7,6},{8,9},{9,8},{10,11... | collective-permute-start | bytes 393224 | tf_op jit(solution)/shard_map/ppermute | solution.py:47
  22.6 1.3 %collective-permute-start.7 = (bf16[64,256]{1,0:T(8,128)(2,1)S(1)}, bf16[64,256]{1,0:T(8,128)(2,1)S(1)}, u32[]{:S(2)}, u32[]{:S(2)}) collective-permute-start(bf16[64,256]{1,0:T(8,128)(2,1)S(1)} %fusion.4), channel_id=1, source_target_pairs={{0,1},{1,0},{2,3},{3,2},{4,5},{5,4},{6,7},{7,6},{8,9},{9,8},{10,11... | collective-permute-start | bytes 98312 | tf_op jit(solution)/shard_map/ppermute | solution.py:47
  42.3 2.0 %collective-permute-start.9 = (bf16[1024,256]{1,0:T(8,128)(2,1)S(1)}, bf16[1024,256]{1,0:T(8,128)(2,1)S(1)}, u32[]{:S(2)}, u32[]{:S(2)}) collective-permute-start(bf16[1024,256]{1,0:T(8,128)(2,1)S(1)} %get-tuple-element.43), channel_id=1, source_target_pairs={{0,1},{1,0},{2,3},{3,2},{4,5},{5,4},{6,7},{7,6},{8,9},{9,8},{10,11... | collective-permute-start | bytes 1572872 | tf_op jit(solution)/shard_map/ppermute | solution.py:47
  45.3 16.2 %copy-start.4 = (bf16[256,512]{1,0:T(8,128)(2,1)}, bf16[256,512]{1,0:T(8,128)(2,1)S(1)}, u32[]{:S(2)}) copy-start(bf16[256,512]{1,0:T(8,128)(2,1)S(1)} %get-tuple-element.45) | copy-start | bytes 786436
  45.3 14.8 %collective-permute-start.13 = (bf16[352,512]{1,0:T(8,128)(2,1)S(1)}, bf16[352,512]{1,0:T(8,128)(2,1)S(1)}, u32[]{:S(2)}, u32[]{:S(2)}) collective-permute-start(bf16[352,512]{1,0:T(8,128)(2,1)S(1)} %get-tuple-element.48), channel_id=1, source_target_pairs={{0,4},{2,6},{8,12},{10,14},{4,0},{6,2},{12,8},{14,10},{1,5},{3,7},... | collective-permute-start | bytes 1081352 | tf_op jit(solution)/shard_map/ppermute | solution.py:53
  48.2 11.9 %collective-permute-start.16 = (bf16[96,512]{1,0:T(8,128)(2,1)S(1)}, bf16[96,512]{1,0:T(8,128)(2,1)S(1)}, u32[]{:S(2)}, u32[]{:S(2)}) collective-permute-start(bf16[96,512]{1,0:T(8,128)(2,1)S(1)} %get-tuple-element.51), channel_id=1, source_target_pairs={{0,6},{2,4},{4,2},{6,0},{8,14},{10,12},{12,10},{14,8},{1,7},{3,5},... | collective-permute-start | bytes 294920 | tf_op jit(solution)/shard_map/ppermute | solution.py:47
  49.2 12.3 %collective-permute-start.11 = (bf16[352,512]{1,0:T(8,128)(2,1)S(1)}, bf16[352,512]{1,0:T(8,128)(2,1)S(1)}, u32[]{:S(2)}, u32[]{:S(2)}) collective-permute-start(bf16[352,512]{1,0:T(8,128)(2,1)S(1)} %get-tuple-element.46), channel_id=1, source_target_pairs={{0,2},{2,0},{4,6},{6,4},{8,10},{10,8},{12,14},{14,12},{1,3},{3,1},... | collective-permute-start | bytes 1081352 | tf_op jit(solution)/shard_map/ppermute | solution.py:47
  62.3 5.8 %collective-permute-start.17 = (bf16[192,256]{1,0:T(8,128)(2,1)S(1)}, bf16[192,256]{1,0:T(8,128)(2,1)}, u32[]{:S(2)}, u32[]{:S(2)}) collective-permute-start(bf16[192,256]{1,0:T(8,128)(2,1)S(1)} %add_convert_fusion.1), channel_id=1, source_target_pairs={{0,8},{2,10},{4,12},{6,14},{8,0},{10,2},{12,4},{14,6},{1,9},{3,11}... | collective-permute-start | bytes 294920 | tf_op jit(solution)/shard_map/ppermute | solution.py:47
  70.6 7.2 %collective-permute-start.18 = (bf16[192,256]{1,0:T(8,128)(2,1)}, bf16[192,256]{1,0:T(8,128)(2,1)}, u32[]{:S(2)}, u32[]{:S(2)}) collective-permute-start(bf16[192,256]{1,0:T(8,128)(2,1)} %get-tuple-element.57), channel_id=1, source_target_pairs={{0,2},{2,0},{4,6},{6,4},{8,10},{10,8},{12,14},{14,12},{1,3},{3,1},... | collective-permute-start | bytes 294920 | tf_op jit(solution)/shard_map/ppermute | solution.py:47
  71.1 12.5 %collective-permute-start.10 = (bf16[256,512]{1,0:T(8,128)(2,1)}, bf16[256,512]{1,0:T(8,128)(2,1)S(1)}, u32[]{:S(2)}, u32[]{:S(2)}) collective-permute-start(bf16[256,512]{1,0:T(8,128)(2,1)} %copy-done.4), channel_id=1, source_target_pairs={{4,8},{6,10},{8,4},{10,6},{5,9},{7,11},{9,5},{11,7},{20,24},{22,26... | collective-permute-start | bytes 786440 | tf_op jit(solution)/shard_map/ppermute | solution.py:53
  71.9 16.8 %collective-permute-start.15 = (bf16[256,512]{1,0:T(8,128)(2,1)S(1)}, bf16[256,512]{1,0:T(8,128)(2,1)S(1)}, u32[]{:S(2)}, u32[]{:S(2)}) collective-permute-start(bf16[256,512]{1,0:T(8,128)(2,1)S(1)} %get-tuple-element.49), channel_id=1, source_target_pairs={{0,2},{2,0},{4,6},{6,4},{8,10},{10,8},{12,14},{14,12},{1,3},{3,1},... | collective-permute-start | bytes 786440 | tf_op jit(solution)/shard_map/ppermute | solution.py:47
  73.5 7.1 %collective-permute-start.19 = (bf16[192,256]{1,0:T(8,128)(2,1)}, bf16[192,256]{1,0:T(8,128)(2,1)S(1)}, u32[]{:S(2)}, u32[]{:S(2)}) collective-permute-start(bf16[192,256]{1,0:T(8,128)(2,1)} %get-tuple-element.57), channel_id=1, source_target_pairs={{0,4},{2,6},{4,0},{6,2},{8,12},{10,14},{12,8},{14,10},{1,5},{3,7},... | collective-permute-start | bytes 294920 | tf_op jit(solution)/shard_map/ppermute | solution.py:47
  77.8 5.7 %collective-permute-start.20 = (bf16[192,256]{1,0:T(8,128)(2,1)}, bf16[192,256]{1,0:T(8,128)(2,1)S(1)}, u32[]{:S(2)}, u32[]{:S(2)}) collective-permute-start(bf16[192,256]{1,0:T(8,128)(2,1)} %get-tuple-element.57), channel_id=1, source_target_pairs={{0,6},{2,4},{4,2},{6,0},{8,14},{10,12},{12,10},{14,8},{1,7},{3,5},... | collective-permute-start | bytes 294920 | tf_op jit(solution)/shard_map/ppermute | solution.py:47
  83.6 11.0 %collective-permute-start.21 = (bf16[768,256]{1,0:T(8,128)(2,1)S(1)}, bf16[768,256]{1,0:T(8,128)(2,1)S(1)}, u32[]{:S(2)}, u32[]{:S(2)}) collective-permute-start(bf16[768,256]{1,0:T(8,128)(2,1)S(1)} %bitcast.26), channel_id=1, source_target_pairs={{0,1},{1,0},{2,3},{3,2},{4,5},{5,4},{6,7},{7,6},{8,9},{9,8},{10,11... | collective-permute-start | bytes 1179656 | tf_op jit(solution)/shard_map/ppermute | solution.py:47
  84.8 8.8 %collective-permute-start.12 = (bf16[256,512]{1,0:T(8,128)(2,1)S(1)}, bf16[256,512]{1,0:T(8,128)(2,1)S(1)}, u32[]{:S(2)}, u32[]{:S(2)}) collective-permute-start(bf16[256,512]{1,0:T(8,128)(2,1)S(1)} %get-tuple-element.70), channel_id=1, source_target_pairs={{0,4},{2,6},{8,12},{10,14},{4,0},{6,2},{12,8},{14,10},{1,5},{3,7},... | collective-permute-start | bytes 786440 | tf_op jit(solution)/shard_map/ppermute | solution.py:53
  85.1 8.4 %collective-permute-start.14 = (bf16[256,512]{1,0:T(8,128)(2,1)S(1)}, bf16[256,512]{1,0:T(8,128)(2,1)S(1)}, u32[]{:S(2)}, u32[]{:S(2)}) collective-permute-start(bf16[256,512]{1,0:T(8,128)(2,1)S(1)} %get-tuple-element.69), channel_id=1, source_target_pairs={{4,8},{6,10},{8,4},{10,6},{5,9},{7,11},{9,5},{11,7},{20,24},{22,26... | collective-permute-start | bytes 786440 | tf_op jit(solution)/shard_map/ppermute | solution.py:53
  85.8 1.3 %collective-permute-start.8 = (bf16[64,256]{1,0:T(8,128)(2,1)S(1)}, bf16[64,256]{1,0:T(8,128)(2,1)S(1)}, u32[]{:S(2)}, u32[]{:S(2)}) collective-permute-start(bf16[64,256]{1,0:T(8,128)(2,1)S(1)} %slice_select_fusion.1), channel_id=1, source_target_pairs={{0,1},{1,0},{2,3},{3,2},{4,5},{5,4},{6,7},{7,6},{8,9},{9,8},{10,11... | collective-permute-start | bytes 98312 | tf_op jit(solution)/shard_map/ppermute | solution.py:47
  (12 other events, 30.8 us)

commit v3 on v2

--- a/solution.py
+++ b/solution.py
@@ -278,9 +278,68 @@
     coded_out[...] = ((residual[...] + total) * gain[...]).astype(BF16)
 
 
-def final_kernel(base, first, second, third, grad_out):
-    returned = first[...].astype(F32) + second[...].astype(F32) + third[...].astype(F32)
+def select_kernel(meta, pair, cross, first, second, far_first, far_second, _, slots_out, edge_out):
+    frame_id, row_id = meta[0], meta[2]
+    count = pair.shape[0]
+    rim = WMAX * COLS
+    pair_step = jnp.where((frame_id & 1) == 0, 1, -1)
+    link_step = jnp.where((frame_id & 2) == 0, 2, -2)
+    for slot in range(2):
+        step = meta[4 + slot] - frame_id
+        for distance, source in (
+            (pair_step, pair),
+            (-pair_step, cross),
+            (link_step, first),
+            (-link_step, second),
+            (2 * link_step, far_first),
+            (-2 * link_step, far_second),
+        ):
+
+            @pl.when(step == distance)
+            def _(source=source):
+                slots_out[slot] = source[...]
+                begin = pl.multiple_of((1 - row_id) * (count - rim), rim)
+                edge_out[slot] = source[pl.ds(begin, rim)]
+
+
+def relay_kernel(
+    meta, across, first, second, third, first_keep, second_keep, own, pair,
+    first_out, second_out, pair_out, own_out,
+):
+    frame_id = meta[0]
+    width = first_keep.shape[0]
+    packed = third.shape[0]
+    pair_out[...] = pair[...]
+    crossing = across[:width].astype(F32)
+    none = jnp.zeros_like(crossing)
+    with_first = (frame_id & 1) == ((frame_id >> 1) & 1)
+    first_out[...] = (
+        first_keep[...] + second[...].astype(F32) + jnp.where(with_first, crossing, none)
+    ).astype(BF16)
+    second_out[...] = (
+        second_keep[...] + first[:width].astype(F32) + jnp.where(with_first, none, crossing)
+    ).astype(BF16)
+    for part in range(2):
+        rows = slice(part * packed, (part + 1) * packed)
+        lanes = slice(part * width, (part + 1) * width)
+        own_out[rows] = (
+            (own[rows] + across[width:, lanes].astype(F32))
+            + (first[width:, lanes].astype(F32) + third[:, lanes].astype(F32))
+        ).astype(BF16)
+
+
+def final_kernel(base, first, second, pair, own, other, grad_out, own_out):
+    returned = first[...].astype(F32) + second[...].astype(F32) + pair[...].astype(F32)
     grad_out[...] = (base[...] + returned.T).astype(BF16)
+    own_out[...] = (own[...].astype(F32) + other[...].astype(F32)).astype(BF16)
+
+
+def gather_kernel(meta, own, first, second, third, pieces_out):
+    me = meta[0] & 3
+    piece = own.shape[0]
+    for mask, part in enumerate((own, first, second, third)):
+        begin = pl.multiple_of((me ^ mask) * piece, piece)
+        pieces_out[pl.ds(begin, piece)] = part[...]
 
 
 def weights_kernel(meta, own, other, shared_out, value_out, output_out, taps_out, *, norm):
@@ -346,16 +405,16 @@
     far_first = along(from_second, 0)
     far_second = along(from_first, 2)
     from_cross = swapped(jnp.where(odd, from_before, from_after), "frame", 1)
-    from_before_2 = jnp.where(low_link, far_second, far_first)
-    from_after_2 = jnp.where(low_link, far_first, far_second)
-    pair_step = jnp.where(odd, -1, 1)
-    distance = (refs - frame_id)[:, None, None]
-    slots = jnp.where(distance == pair_step, from_pair[None], from_cross[None])
-    for step, source in (
-        (-2, from_before), (2, from_after), (-4, from_before_2), (4, from_after_2)
-    ):
-        slots = jnp.where(distance == step, source[None], slots)
-    halo = swapped(jnp.where(row_id == 0, slots[:, count - rim :], slots[:, :rim]), "row", 1)
+    slots, edge = whole_call(
+        select_kernel,
+        [((2, count, width), BF16), ((2, rim, width), BF16)],
+        (meta, from_pair, from_cross, from_first, from_second, far_first, far_second, upt),
+        smem=(0,),
+        flops=count * width,
+        moved=count * width * 8,
+        name="slots",
+    )
+    halo = swapped(edge, "row", 1)
 
     block = BROWS * COLS
     span = block + 2 * rim
@@ -426,38 +485,46 @@
     second = along(second, 2)
     third = swapped(third, "frame", 3)
 
-    def unpacked(array):
-        return jnp.concatenate([array[:, :width], array[:, width:]], 0).astype(F32)
-
-    total = (own + unpacked(across[width:])) + (unpacked(first[width:]) + unpacked(third))
+    back_first, back_second, back_pair, own = whole_call(
+        relay_kernel,
+        [
+            ((width, count), BF16),
+            ((width, count), BF16),
+            ((width, count), BF16),
+            ((piece, width), BF16),
+        ],
+        (meta, across, first, second, third, first_keep, second_keep, own, pair),
+        smem=(0,),
+        flops=count * width * 4,
+        moved=count * width * 16,
+        name="relay",
+    )
+    back_first = along(back_first, 0)
+    back_second = along(back_second, 2)
+    back_pair = swapped(back_pair, "frame", 1)
     mask = 4
-    while mask < frames:
-        total = total.astype(BF16)
-        total = total.astype(F32) + swapped(total, "frame", mask).astype(F32)
+    other = swapped(own, "frame", mask)
+    while 2 * mask < frames:
         mask *= 2
-    own = total.astype(BF16)
-
-    back_pair = swapped(pair, "frame", 1)
-    crossing = across[:width].astype(F32)
-    with_first = odd != low_link
-    back_first = along(
-        (first_keep + second.astype(F32) + jnp.where(with_first, crossing, 0.0)).astype(BF16), 0
-    )
-    back_second = along(
-        (second_keep + first[:width].astype(F32) + jnp.where(with_first, 0.0, crossing)).astype(
-            BF16
-        ),
-        2,
-    )
-
-    me = frame_id & 3
-    pieces = jnp.zeros((4, piece, width), BF16)
-    pieces = lax.dynamic_update_index_in_dim(pieces, own, me, 0)
-    for mask in (1, 2, 3):
-        pieces = lax.dynamic_update_index_in_dim(
-            pieces, swapped(own, "frame", mask), me ^ mask, 0
-        )
-    pieces = pieces.reshape(half, width)
+        own = (own.astype(F32) + other.astype(F32)).astype(BF16)
+        other = swapped(own, "frame", mask)
+    grad_latents, own = whole_call(
+        final_kernel,
+        [((count, width), BF16), ((piece, width), BF16)],
+        (base, back_first, back_second, back_pair, own, other),
+        flops=count * width * 4,
+        moved=count * width * 12,
+        name="latent_gradient",
+    )
+    (pieces,) = whole_call(
+        gather_kernel,
+        [((half, width), BF16)],
+        (meta, own, *[swapped(own, "frame", mask) for mask in (1, 2, 3)]),
+        smem=(0,),
+        flops=half * width,
+        moved=half * width * 4,
+        name="pieces",
+    )
     other = swapped(pieces, "row", 1)
     shared_grad, value_grad, output_grad, taps_grad = whole_call(
         functools.partial(
@@ -485,14 +552,6 @@
         flops=2 * 3 * count * width * width,
         moved=count * width * 8,
         name="context",
-    )
-    (grad_latents,) = whole_call(
-        final_kernel,
-        [((count, width), BF16)],
-        (base, back_first, back_second, back_pair),
-        flops=count * width * 4,
-        moved=count * width * 12,
-        name="latent_gradient",
     )
     return (
         coded[None],

time: 97.2 us -> 89.9 us (0.925)
  waiting for transfers between devices: 33.1 us -> 28.1 us
  other arithmetic: 3.18 us -> 0.06 us
  local copies, waits for them, and re-layouts: 3.92 us -> 1.73 us
  Pallas kernels: 23.6 us -> 25.7 us
  starting transfers between devices: 30.2 us -> 31.9 us
    ppermute x8, waiting for transfers between devices: 7.99 us -> 4.22 us  [along(): return lax.ppermute(array, 'frame', pairs + [(j, i) for i, j in pairs])]
    pallas_call x6 -> x9, Pallas kernels: 23.6 us -> 25.7 us  [whole_call(): pl.pallas_call(body, out_shape=[jax.ShapeDtypeStruct(shape, dtype) for sh...]
    dynamic_update_slice x1 -> x0, other arithmetic: 1.56 us -> none  [local(): pieces = lax.dynamic_update_index_in_dim(pieces, own, me, 0)]
    ppermute x14, waiting for transfers between devices: 25.1 us -> 23.8 us  [swapped(): return lax.ppermute(array, axis, pairs)]
    ppermute x8, starting transfers between devices: 15.8 us -> 17 us  [along(): return lax.ppermute(array, 'frame', pairs + [(j, i) for i, j in pairs])]
    convert_element_type x2 -> x0, other arithmetic: 1.22 us -> none  [the longest x1 1.17 us: local(): (second_keep + first[:width].astype(F32) + jnp.where(with_first, 0.0, cro...]
    unnamed x28 -> x18, local copies, waits for them, and re-layouts: 2.86 us -> 1.64 us
  transfers between devices with their start and end apart: 22 -> 22, of which waited for: 11 -> 10; matrix products, arithmetic and copies ran while one was open for 2% -> 0% of each run, Pallas kernels for 4% -> 3%
where the time goes in v3:
time: 89.9 us; the launch traced here: 89.7 us
  starting transfers between devices  31.9 us (35%)
  waiting for transfers between devices  28.1 us (31%)
  Pallas kernels  25.7 us (29%)
  between operations  2.21 us (2%)
  local copies, waits for them, and re-layouts  1.73 us (2%)
    pallas_call x9, Pallas kernels, whole_call(): pl.pallas_call(body, out_shape=[jax.ShapeDtypeStruct(shape, dtype) for sh...  25.7 us
    ppermute x14, waiting for transfers between devices, swapped(): return lax.ppermute(array, axis, pairs)  23.8 us
    ppermute x8, starting transfers between devices, along(): return lax.ppermute(array, 'frame', pairs + [(j, i) for i, j in pairs])  17 us
    ppermute x14, starting transfers between devices, swapped(): return lax.ppermute(array, axis, pairs)  14.9 us
    ppermute x8, waiting for transfers between devices, along(): return lax.ppermute(array, 'frame', pairs + [(j, i) for i, j in pairs])  4.22 us
  transfers between devices with their start and end apart: 22, of which 10 were waited for; matrix products, arithmetic and copies ran while one was open for 0% of the time, Pallas kernels for 3%

profile of v3, /device:TPU:0, one launch (start us, length us, event | category | flops | bytes accessed | tf_op | source)
XLA Modules:
  0.0 89.7 jit_solution(16830426350467033015)
XLA Ops:
  0.6 3.1 %collective-permute-start.2 = (bf16[512,256]{1,0:T(8,128)(2,1)}, bf16[512,256]{1,0:T(8,128)(2,1)S(1)}, u32[]{:S(2)}, u32[]{:S(2)}) collective-permute-start(bf16[512,256]{1,0:T(8,128)(2,1)} %bitcast.17), channel_id=1, source_target_pairs={{0,4},{2,6},{8,12},{10,14},{4,0},{6,2},{12,8},{14,10},{1,5},{3,7},... | collective-permute-start | bytes 786440 | tf_op jit(solution)/shard_map/ppermute | solution.py:53
  4.4 1.6 %collective-permute-start = (bf16[512,256]{1,0:T(8,128)(2,1)}, bf16[512,256]{1,0:T(8,128)(2,1)S(1)}, u32[]{:S(2)}, u32[]{:S(2)}) collective-permute-start(bf16[512,256]{1,0:T(8,128)(2,1)} %bitcast.19), channel_id=1, source_target_pairs={{0,2},{2,0},{4,6},{6,4},{8,10},{10,8},{12,14},{14,12},{1,3},{3,1},... | collective-permute-start | bytes 786440 | tf_op jit(solution)/shard_map/ppermute | solution.py:47
  6.7 3.5 %collective-permute-done.2.first = bf16[512,256]{1,0:T(8,128)(2,1)S(1)} collective-permute-done((bf16[512,256]{1,0:T(8,128)(2,1)}, bf16[512,256]{1,0:T(8,128)(2,1)S(1)}, u32[]{:S(2)}, u32[]{:S(2)}) %collective-permute-start.2) | collective-permute-done | bytes 262176 | tf_op jit(solution)/shard_map/ppermute | solution.py:53
  10.3 1.7 %collective-permute-start.3 = (bf16[512,256]{1,0:T(8,128)(2,1)S(1)}, bf16[512,256]{1,0:T(8,128)(2,1)S(1)}, u32[]{:S(2)}, u32[]{:S(2)}) collective-permute-start(bf16[512,256]{1,0:T(8,128)(2,1)S(1)} %select_select_fusion), channel_id=1, source_target_pairs={{0,2},{2,0},{4,6},{6,4},{8,10},{10,8},{12,14},{14,12},{1,3},{3,1},... | collective-permute-start | bytes 786440 | tf_op jit(solution)/shard_map/ppermute | solution.py:47
  12.7 7.6 %collective-permute-start.4 = (bf16[512,256]{1,0:T(8,128)(2,1)S(1)}, bf16[512,256]{1,0:T(8,128)(2,1)S(1)}, u32[]{:S(2)}, u32[]{:S(2)}) collective-permute-start(bf16[512,256]{1,0:T(8,128)(2,1)S(1)} %collective-permute-done.1.second), channel_id=1, source_target_pairs={{0,4},{2,6},{8,12},{10,14},{4,0},{6,2},{12,8},{14,10},{1,5},{3,7},... | collective-permute-start | bytes 786440 | tf_op jit(solution)/shard_map/ppermute | solution.py:53
  21.8 0.9 %copy-done.3 = bf16[1,512,256]{2,1,0:T(8,128)(2,1)S(1)} copy-done((bf16[1,512,256]{2,1,0:T(8,128)(2,1)S(1)}, bf16[1,512,256]{2,1,0:T(8,128)(2,1)}, u32[]{:S(2)}) %copy-start.3) | copy-done | bytes 262168
  22.8 1.4 %gradient_path.1 = (f32[512,256]{1,0:T(8,128)S(1)}, bf16[512,256]{1,0:T(8,128)(2,1)S(1)}, bf16[640,256]{1,0:T(8,128)(2,1)S(1)}, bf16[512,256]{1,0:T(8,128)(2,1)S...) custom-call(s32[6]{0:T(128)S(1)} %concatenate.3.meta, ...), custom_call_target="tpu_custom_call" | custom-call | flops 335544320 | bytes 3145728 | tf_op jit(solution)/shard_map/gradient_path/pallas_call | solution.py:64
  25.6 1.3 %collective-permute-done.7.halo = bf16[2,128,256]{2,1,0:T(8,128)(2,1)S(1)} collective-permute-done((bf16[2,128,256]{2,1,0:T(8,128)(2,1)S(1)}, bf16[2,128,256]{2,1,0:T(8,128)(2,1)S(1)}, u32[]{:S(2)}, u32[]{:S(2)}) %collective-permute-start.7) | collective-permute-done | bytes 131104 | tf_op jit(solution)/shard_map/ppermute | solution.py:47
  26.9 17.0 %attention.1 = (f32[2,256,512]{2,1,0:T(8,128)S(1)}, bf16[1024,256]{1,0:T(8,128)(2,1)S(1)}, f32[768,256]{1,0:T(8,128)S(1)}, bf16[512,256]{1,0:T(8,128)(2,1)S(1)},...) custom-call(s32[6]{0:T(128)S(1)} %concatenate.3.meta, bf16[2,512,256]{2,1,0:T(8,128)(2,1)S(1)} %get-tuple-element.40.slots, ...), custom_call_target="tpu_custom_call" | custom-call | flops 9663676416 | bytes 7864320 | tf_op jit(solution)/shard_map/attention/pallas_call | solution.py:64
  44.2 1.8 %collective-permute-done.9.got = bf16[1024,256]{1,0:T(8,128)(2,1)S(1)} collective-permute-done((bf16[1024,256]{1,0:T(8,128)(2,1)S(1)}, bf16[1024,256]{1,0:T(8,128)(2,1)S(1)}, u32[]{:S(2)}, u32[]{:S(2)}) %collective-permute-start.9) | collective-permute-done | bytes 524320 | tf_op jit(solution)/shard_map/ppermute | solution.py:47
  45.9 1.0 %spread.1 = (bf16[256,512]{1,0:T(8,128)(2,1)S(1)}, bf16[352,512]{1,0:T(8,128)(2,1)S(1)}, bf16[352,512]{1,0:T(8,128)(2,1)S(1)}, bf16[256,512]{1,0:T(8,128)(2,1)S(...) custom-call(s32[6]{0:T(128)S(1)} %concatenate.3.meta, ...), custom_call_target="tpu_custom_call" | custom-call | flops 1572864 | bytes 3932160 | tf_op jit(solution)/shard_map/spread/pallas_call | solution.py:64
  47.6 1.8 %collective-permute-start.11 = (bf16[352,512]{1,0:T(8,128)(2,1)S(1)}, bf16[352,512]{1,0:T(8,128)(2,1)S(1)}, u32[]{:S(2)}, u32[]{:S(2)}) collective-permute-start(bf16[352,512]{1,0:T(8,128)(2,1)S(1)} %get-tuple-element.55), channel_id=1, source_target_pairs={{0,4},{2,6},{8,12},{10,14},{4,0},{6,2},{12,8},{14,10},{1,5},{3,7},... | collective-permute-start | bytes 1081352 | tf_op jit(solution)/shard_map/ppermute | solution.py:53
  50.1 3.0 %collective-permute-start.13 = (bf16[96,512]{1,0:T(8,128)(2,1)S(1)}, bf16[96,512]{1,0:T(8,128)(2,1)S(1)}, u32[]{:S(2)}, u32[]{:S(2)}) collective-permute-start(bf16[96,512]{1,0:T(8,128)(2,1)S(1)} %get-tuple-element.57), channel_id=1, source_target_pairs={{0,6},{2,4},{4,2},{6,0},{8,14},{10,12},{12,10},{14,8},{1,7},{3,5},... | collective-permute-start | bytes 294920 | tf_op jit(solution)/shard_map/ppermute | solution.py:47
  53.1 7.8 %collective-permute-done.13.third = bf16[96,512]{1,0:T(8,128)(2,1)S(1)} collective-permute-done((bf16[96,512]{1,0:T(8,128)(2,1)S(1)}, bf16[96,512]{1,0:T(8,128)(2,1)S(1)}, u32[]{:S(2)}, u32[]{:S(2)}) %collective-permute-start.13) | collective-permute-done | bytes 98336 | tf_op jit(solution)/shard_map/ppermute | solution.py:47
  61.7 1.8 %collective-permute-start.14 = (bf16[256,512]{1,0:T(8,128)(2,1)S(1)}, bf16[256,512]{1,0:T(8,128)(2,1)S(1)}, u32[]{:S(2)}, u32[]{:S(2)}) collective-permute-start(bf16[256,512]{1,0:T(8,128)(2,1)S(1)} %get-tuple-element.62), channel_id=1, source_target_pairs={{0,4},{2,6},{8,12},{10,14},{4,0},{6,2},{12,8},{14,10},{1,5},{3,7},... | collective-permute-start | bytes 786440 | tf_op jit(solution)/shard_map/ppermute | solution.py:53
  64.8 3.0 %collective-permute-start.17 = (bf16[192,256]{1,0:T(8,128)(2,1)S(1)}, bf16[192,256]{1,0:T(8,128)(2,1)S(1)}, u32[]{:S(2)}, u32[]{:S(2)}) collective-permute-start(bf16[192,256]{1,0:T(8,128)(2,1)S(1)} %get-tuple-element.65.own), channel_id=1, source_target_pairs={{0,8},{2,10},{4,12},{6,14},{8,0},{10,2},{12,4},{14,6},{1,9},{3,11}... | collective-permute-start | bytes 294920 | tf_op jit(solution)/shard_map/ppermute | solution.py:47
  67.8 8.6 %collective-permute-done.17.other = bf16[192,256]{1,0:T(8,128)(2,1)S(1)} collective-permute-done((bf16[192,256]{1,0:T(8,128)(2,1)S(1)}, bf16[192,256]{1,0:T(8,128)(2,1)S(1)}, u32[]{:S(2)}, u32[]{:S(2)}) %collective-permute-start.17) | collective-permute-done | bytes 98336 | tf_op jit(solution)/shard_map/ppermute | solution.py:47
  77.3 2.0 %collective-permute-start.19 = (bf16[192,256]{1,0:T(8,128)(2,1)S(1)}, bf16[192,256]{1,0:T(8,128)(2,1)S(1)}, u32[]{:S(2)}, u32[]{:S(2)}) collective-permute-start(bf16[192,256]{1,0:T(8,128)(2,1)S(1)} %get-tuple-element.67.own), channel_id=1, source_target_pairs={{0,4},{2,6},{4,0},{6,2},{8,12},{10,14},{12,8},{14,10},{1,5},{3,7},... | collective-permute-start | bytes 294920 | tf_op jit(solution)/shard_map/ppermute | solution.py:47
  79.3 1.5 %collective-permute-start.18 = (bf16[192,256]{1,0:T(8,128)(2,1)S(1)}, bf16[192,256]{1,0:T(8,128)(2,1)S(1)}, u32[]{:S(2)}, u32[]{:S(2)}) collective-permute-start(bf16[192,256]{1,0:T(8,128)(2,1)S(1)} %get-tuple-element.67.own), channel_id=1, source_target_pairs={{0,2},{2,0},{4,6},{6,4},{8,10},{10,8},{12,14},{14,12},{1,3},{3,1},... | collective-permute-start | bytes 294920 | tf_op jit(solution)/shard_map/ppermute | solution.py:47
  80.8 2.0 %collective-permute-done.20.third = bf16[192,256]{1,0:T(8,128)(2,1)S(1)} collective-permute-done((bf16[192,256]{1,0:T(8,128)(2,1)S(1)}, bf16[192,256]{1,0:T(8,128)(2,1)S(1)}, u32[]{:S(2)}, u32[]{:S(2)}) %collective-permute-start.20) | collective-permute-done | bytes 98336 | tf_op jit(solution)/shard_map/ppermute | solution.py:47
  82.9 1.0 %collective-permute-done.18.first = bf16[192,256]{1,0:T(8,128)(2,1)S(1)} collective-permute-done((bf16[192,256]{1,0:T(8,128)(2,1)S(1)}, bf16[192,256]{1,0:T(8,128)(2,1)S(1)}, u32[]{:S(2)}, u32[]{:S(2)}) %collective-permute-start.18) | collective-permute-done | bytes 98336 | tf_op jit(solution)/shard_map/ppermute | solution.py:47
  85.1 1.3 %collective-permute-done.8.halo = bf16[64,256]{1,0:T(8,128)(2,1)S(1)} collective-permute-done((bf16[64,256]{1,0:T(8,128)(2,1)S(1)}, bf16[64,256]{1,0:T(8,128)(2,1)S(1)}, u32[]{:S(2)}, u32[]{:S(2)}) %collective-permute-start.8) | collective-permute-done | bytes 32800 | tf_op jit(solution)/shard_map/ppermute | solution.py:47
  86.3 1.6 %context.1 = bf16[512,256]{1,0:T(8,128)(2,1)} custom-call(s32[6]{0:T(128)S(1)} %concatenate.3.meta, bf16[512,256]{1,0:T(8,128)(2,1)S(1)} %get-tuple-element.48.hidden, bf16[64,256]{1,0:T(8,128)(2,1)S(1)} %collective-permute-done.8.halo, f32[512,256]{1,0:T(8,128)S(1)} %get-tuple-element.49.residual, f32[1,256]{1,0:T(1,128)S(1)} %constant_dynamic-slice_fusion.gain, ...), custom_call_target="tpu_custom_call" | custom-call | flops 201326592 | bytes 1048576 | tf_op jit(solution)/shard_map/context/pallas_call | solution.py:64
  87.9 1.7 %weight_gradients.1 = (f32[256,256]{1,0:T(8,128)}, f32[256,256]{1,0:T(8,128)}, f32[256,256]{1,0:T(8,128)}, f32[3,256,256]{2,1,0:T(8,128)}) custom-call(s32[6]{0:T(128)S(1)} %concatenate.3.meta, bf16[768,256]{1,0:T(8,128)(2,1)S(1)} %pieces.1.own, bf16[768,256]{1,0:T(8,128)(2,1)S(1)} %collective-permute-done.21.other), custom_call_target="tpu_custom_call" | custom-call | flops 393216 | bytes 2359296 | tf_op jit(solution)/shard_map/weight_gradients/pallas_call | solution.py:64
  (52 shorter events, 9.4 us)
Async XLA Ops:
  0.6 9.6 %collective-permute-start.2 = (bf16[512,256]{1,0:T(8,128)(2,1)}, bf16[512,256]{1,0:T(8,128)(2,1)S(1)}, u32[]{:S(2)}, u32[]{:S(2)}) collective-permute-start(bf16[512,256]{1,0:T(8,128)(2,1)} %bitcast.17), channel_id=1, source_target_pairs={{0,4},{2,6},{8,12},{10,14},{4,0},{6,2},{12,8},{14,10},{1,5},{3,7},... | collective-permute-start | bytes 786440 | tf_op jit(solution)/shard_map/ppermute | solution.py:53
  3.7 6.5 %collective-permute-start.1 = (bf16[512,256]{1,0:T(8,128)(2,1)}, bf16[512,256]{1,0:T(8,128)(2,1)S(1)}, u32[]{:S(2)}, u32[]{:S(2)}) collective-permute-start(bf16[512,256]{1,0:T(8,128)(2,1)} %bitcast.18), channel_id=1, source_target_pairs={{4,8},{6,10},{8,4},{10,6},{5,9},{7,11},{9,5},{11,7},{20,24},{22,26... | collective-permute-start | bytes 786440 | tf_op jit(solution)/shard_map/ppermute | solution.py:53
  4.4 19.8 %collective-permute-start = (bf16[512,256]{1,0:T(8,128)(2,1)}, bf16[512,256]{1,0:T(8,128)(2,1)S(1)}, u32[]{:S(2)}, u32[]{:S(2)}) collective-permute-start(bf16[512,256]{1,0:T(8,128)(2,1)} %bitcast.19), channel_id=1, source_target_pairs={{0,2},{2,0},{4,6},{6,4},{8,10},{10,8},{12,14},{14,12},{1,3},{3,1},... | collective-permute-start | bytes 786440 | tf_op jit(solution)/shard_map/ppermute | solution.py:47
  6.0 15.8 %copy-start.6 = (bf16[256,256]{1,0:T(8,128)(2,1)S(1)}, bf16[256,256]{1,0:T(8,128)(2,1)}, u32[]{:S(2)}) copy-start(bf16[256,256]{1,0:T(8,128)(2,1)} %outp.3) | copy-start | bytes 393220
  6.7 15.1 %copy-start.1 = (bf16[3,256,256]{2,1,0:T(8,128)(2,1)S(1)}, bf16[3,256,256]{2,1,0:T(8,128)(2,1)}, u32[]{:S(2)}) copy-start(bf16[3,256,256]{2,1,0:T(8,128)(2,1)} %taps.3) | copy-start | bytes 1179652
  10.3 13.9 %collective-permute-start.3 = (bf16[512,256]{1,0:T(8,128)(2,1)S(1)}, bf16[512,256]{1,0:T(8,128)(2,1)S(1)}, u32[]{:S(2)}, u32[]{:S(2)}) collective-permute-start(bf16[512,256]{1,0:T(8,128)(2,1)S(1)} %select_select_fusion), channel_id=1, source_target_pairs={{0,2},{2,0},{4,6},{6,4},{8,10},{10,8},{12,14},{14,12},{1,3},{3,1},... | collective-permute-start | bytes 786440 | tf_op jit(solution)/shard_map/ppermute | solution.py:47
  12.0 12.2 %collective-permute-start.5 = (bf16[512,256]{1,0:T(8,128)(2,1)S(1)}, bf16[512,256]{1,0:T(8,128)(2,1)S(1)}, u32[]{:S(2)}, u32[]{:S(2)}) collective-permute-start(bf16[512,256]{1,0:T(8,128)(2,1)S(1)} %collective-permute-done.2.first), channel_id=1, source_target_pairs={{4,8},{6,10},{8,4},{10,6},{5,9},{7,11},{9,5},{11,7},{20,24},{22,26... | collective-permute-start | bytes 786440 | tf_op jit(solution)/shard_map/ppermute | solution.py:53
  12.7 12.2 %collective-permute-start.4 = (bf16[512,256]{1,0:T(8,128)(2,1)S(1)}, bf16[512,256]{1,0:T(8,128)(2,1)S(1)}, u32[]{:S(2)}, u32[]{:S(2)}) collective-permute-start(bf16[512,256]{1,0:T(8,128)(2,1)S(1)} %collective-permute-done.1.second), channel_id=1, source_target_pairs={{0,4},{2,6},{8,12},{10,14},{4,0},{6,2},{12,8},{14,10},{1,5},{3,7},... | collective-permute-start | bytes 786440 | tf_op jit(solution)/shard_map/ppermute | solution.py:53
  20.3 1.5 %collective-permute-start.6 = (bf16[64,256]{1,0:T(8,128)(2,1)S(1)}, bf16[64,256]{1,0:T(8,128)(2,1)S(1)}, u32[]{:S(2)}, u32[]{:S(2)}) collective-permute-start(bf16[64,256]{1,0:T(8,128)(2,1)S(1)} %fusion), channel_id=1, source_target_pairs={{0,1},{1,0},{2,3},{3,2},{4,5},{5,4},{6,7},{7,6},{8,9},{9,8},{10,11... | collective-permute-start | bytes 98312 | tf_op jit(solution)/shard_map/ppermute | solution.py:47
  25.5 1.4 %collective-permute-start.7 = (bf16[2,128,256]{2,1,0:T(8,128)(2,1)S(1)}, bf16[2,128,256]{2,1,0:T(8,128)(2,1)S(1)}, u32[]{:S(2)}, u32[]{:S(2)}) collective-permute-start(bf16[2,128,256]{2,1,0:T(8,128)(2,1)S(1)} %get-tuple-element.41), channel_id=1, source_target_pairs={{0,1},{1,0},{2,3},{3,2},{4,5},{5,4},{6,7},{7,6},{8,9},{9,8},{10,11... | collective-permute-start | bytes 393224 | tf_op jit(solution)/shard_map/ppermute | solution.py:47
  43.9 2.0 %collective-permute-start.9 = (bf16[1024,256]{1,0:T(8,128)(2,1)S(1)}, bf16[1024,256]{1,0:T(8,128)(2,1)S(1)}, u32[]{:S(2)}, u32[]{:S(2)}) collective-permute-start(bf16[1024,256]{1,0:T(8,128)(2,1)S(1)} %get-tuple-element.53), channel_id=1, source_target_pairs={{0,1},{1,0},{2,3},{3,2},{4,5},{5,4},{6,7},{7,6},{8,9},{9,8},{10,11... | collective-permute-start | bytes 1572872 | tf_op jit(solution)/shard_map/ppermute | solution.py:47
  47.0 13.9 %collective-permute-start.10 = (bf16[352,512]{1,0:T(8,128)(2,1)S(1)}, bf16[352,512]{1,0:T(8,128)(2,1)S(1)}, u32[]{:S(2)}, u32[]{:S(2)}) collective-permute-start(bf16[352,512]{1,0:T(8,128)(2,1)S(1)} %get-tuple-element.54), channel_id=1, source_target_pairs={{0,2},{2,0},{4,6},{6,4},{8,10},{10,8},{12,14},{14,12},{1,3},{3,1},... | collective-permute-start | bytes 1081352 | tf_op jit(solution)/shard_map/ppermute | solution.py:47
  47.6 13.3 %collective-permute-start.11 = (bf16[352,512]{1,0:T(8,128)(2,1)S(1)}, bf16[352,512]{1,0:T(8,128)(2,1)S(1)}, u32[]{:S(2)}, u32[]{:S(2)}) collective-permute-start(bf16[352,512]{1,0:T(8,128)(2,1)S(1)} %get-tuple-element.55), channel_id=1, source_target_pairs={{0,4},{2,6},{8,12},{10,14},{4,0},{6,2},{12,8},{14,10},{1,5},{3,7},... | collective-permute-start | bytes 1081352 | tf_op jit(solution)/shard_map/ppermute | solution.py:53
  49.4 11.5 %collective-permute-start.12 = (bf16[256,512]{1,0:T(8,128)(2,1)S(1)}, bf16[256,512]{1,0:T(8,128)(2,1)S(1)}, u32[]{:S(2)}, u32[]{:S(2)}) collective-permute-start(bf16[256,512]{1,0:T(8,128)(2,1)S(1)} %get-tuple-element.56), channel_id=1, source_target_pairs={{4,8},{6,10},{8,4},{10,6},{5,9},{7,11},{9,5},{11,7},{20,24},{22,26... | collective-permute-start | bytes 786440 | tf_op jit(solution)/shard_map/ppermute | solution.py:53
  50.1 10.8 %collective-permute-start.13 = (bf16[96,512]{1,0:T(8,128)(2,1)S(1)}, bf16[96,512]{1,0:T(8,128)(2,1)S(1)}, u32[]{:S(2)}, u32[]{:S(2)}) collective-permute-start(bf16[96,512]{1,0:T(8,128)(2,1)S(1)} %get-tuple-element.57), channel_id=1, source_target_pairs={{0,6},{2,4},{4,2},{6,0},{8,14},{10,12},{12,10},{14,8},{1,7},{3,5},... | collective-permute-start | bytes 294920 | tf_op jit(solution)/shard_map/ppermute | solution.py:47
  61.7 14.6 %collective-permute-start.14 = (bf16[256,512]{1,0:T(8,128)(2,1)S(1)}, bf16[256,512]{1,0:T(8,128)(2,1)S(1)}, u32[]{:S(2)}, u32[]{:S(2)}) collective-permute-start(bf16[256,512]{1,0:T(8,128)(2,1)S(1)} %get-tuple-element.62), channel_id=1, source_target_pairs={{0,4},{2,6},{8,12},{10,14},{4,0},{6,2},{12,8},{14,10},{1,5},{3,7},... | collective-permute-start | bytes 786440 | tf_op jit(solution)/shard_map/ppermute | solution.py:53
  63.5 12.8 %collective-permute-start.15 = (bf16[256,512]{1,0:T(8,128)(2,1)S(1)}, bf16[256,512]{1,0:T(8,128)(2,1)S(1)}, u32[]{:S(2)}, u32[]{:S(2)}) collective-permute-start(bf16[256,512]{1,0:T(8,128)(2,1)S(1)} %get-tuple-element.63), channel_id=1, source_target_pairs={{4,8},{6,10},{8,4},{10,6},{5,9},{7,11},{9,5},{11,7},{20,24},{22,26... | collective-permute-start | bytes 786440 | tf_op jit(solution)/shard_map/ppermute | solution.py:53
  64.2 12.2 %collective-permute-start.16 = (bf16[256,512]{1,0:T(8,128)(2,1)S(1)}, bf16[256,512]{1,0:T(8,128)(2,1)S(1)}, u32[]{:S(2)}, u32[]{:S(2)}) collective-permute-start(bf16[256,512]{1,0:T(8,128)(2,1)S(1)} %get-tuple-element.64), channel_id=1, source_target_pairs={{0,2},{2,0},{4,6},{6,4},{8,10},{10,8},{12,14},{14,12},{1,3},{3,1},... | collective-permute-start | bytes 786440 | tf_op jit(solution)/shard_map/ppermute | solution.py:47
  64.8 11.6 %collective-permute-start.17 = (bf16[192,256]{1,0:T(8,128)(2,1)S(1)}, bf16[192,256]{1,0:T(8,128)(2,1)S(1)}, u32[]{:S(2)}, u32[]{:S(2)}) collective-permute-start(bf16[192,256]{1,0:T(8,128)(2,1)S(1)} %get-tuple-element.65.own), channel_id=1, source_target_pairs={{0,8},{2,10},{4,12},{6,14},{8,0},{10,2},{12,4},{14,6},{1,9},{3,11}... | collective-permute-start | bytes 294920 | tf_op jit(solution)/shard_map/ppermute | solution.py:47
  77.3 5.5 %collective-permute-start.20 = (bf16[192,256]{1,0:T(8,128)(2,1)S(1)}, bf16[192,256]{1,0:T(8,128)(2,1)S(1)}, u32[]{:S(2)}, u32[]{:S(2)}) collective-permute-start(bf16[192,256]{1,0:T(8,128)(2,1)S(1)} %get-tuple-element.67.own), channel_id=1, source_target_pairs={{0,6},{2,4},{4,2},{6,0},{8,14},{10,12},{12,10},{14,8},{1,7},{3,5},... | collective-permute-start | bytes 294920 | tf_op jit(solution)/shard_map/ppermute | solution.py:47
  77.3 5.6 %collective-permute-start.19 = (bf16[192,256]{1,0:T(8,128)(2,1)S(1)}, bf16[192,256]{1,0:T(8,128)(2,1)S(1)}, u32[]{:S(2)}, u32[]{:S(2)}) collective-permute-start(bf16[192,256]{1,0:T(8,128)(2,1)S(1)} %get-tuple-element.67.own), channel_id=1, source_target_pairs={{0,4},{2,6},{4,0},{6,2},{8,12},{10,14},{12,8},{14,10},{1,5},{3,7},... | collective-permute-start | bytes 294920 | tf_op jit(solution)/shard_map/ppermute | solution.py:47
  79.3 4.6 %collective-permute-start.18 = (bf16[192,256]{1,0:T(8,128)(2,1)S(1)}, bf16[192,256]{1,0:T(8,128)(2,1)S(1)}, u32[]{:S(2)}, u32[]{:S(2)}) collective-permute-start(bf16[192,256]{1,0:T(8,128)(2,1)S(1)} %get-tuple-element.67.own), channel_id=1, source_target_pairs={{0,2},{2,0},{4,6},{6,4},{8,10},{10,8},{12,14},{14,12},{1,3},{3,1},... | collective-permute-start | bytes 294920 | tf_op jit(solution)/shard_map/ppermute | solution.py:47
  84.5 3.5 %collective-permute-start.21 = (bf16[768,256]{1,0:T(8,128)(2,1)S(1)}, bf16[768,256]{1,0:T(8,128)(2,1)S(1)}, u32[]{:S(2)}, u32[]{:S(2)}) collective-permute-start(bf16[768,256]{1,0:T(8,128)(2,1)S(1)} %pieces.1.own), channel_id=1, source_target_pairs={{0,1},{1,0},{2,3},{3,2},{4,5},{5,4},{6,7},{7,6},{8,9},{9,8},{10,11... | collective-permute-start | bytes 1179656 | tf_op jit(solution)/shard_map/ppermute | solution.py:47
  84.6 1.7 %collective-permute-start.8 = (bf16[64,256]{1,0:T(8,128)(2,1)S(1)}, bf16[64,256]{1,0:T(8,128)(2,1)S(1)}, u32[]{:S(2)}, u32[]{:S(2)}) collective-permute-start(bf16[64,256]{1,0:T(8,128)(2,1)S(1)} %slice_select_fusion), channel_id=1, source_target_pairs={{0,1},{1,0},{2,3},{3,2},{4,5},{5,4},{6,7},{7,6},{8,9},{9,8},{10,11... | collective-permute-start | bytes 98312 | tf_op jit(solution)/shard_map/ppermute | solution.py:47
  (7 other events, 40.5 us)

commit v4 on v3

--- a/solution.py
+++ b/solution.py
@@ -47,10 +47,13 @@
     return lax.ppermute(array, axis, pairs)
 
 
-def along(array, parity):
+def along(array, parity, relayed=False):
     devices = lax.axis_size("frame")
     pairs = [(i, i + 2) for i in range(devices) if (i & 2) == parity and i + 2 < devices]
-    return lax.ppermute(array, "frame", pairs + [(j, i) for i, j in pairs])
+    pairs = pairs + [(j, i) for i, j in pairs]
+    if relayed:
+        pairs = [(i, j) for i, j in pairs if 0 <= 2 * i - j < devices]
+    return lax.ppermute(array, "frame", pairs)
 
 
 def whole_call(
@@ -75,13 +78,15 @@
 
 
 def before_kernel(
-    meta, cot, gain, edge, tokens, taps, shared, outp,
-    resid_out, rb_out, ext_out, up_out, upt_out, query_out, queryt_out,
+    level, scale, edge, cot, tokens, taps, shared, outp,
+    resid_out, rb_out, ext_out, up_out, upt_out, query_out, queryt_out, gain_out,
 ):
-    row_id = meta[2]
+    row_id = lax.axis_index("row")
     count = cot.shape[0]
-    grad_z = cot[...].astype(F32) * gain[...]
-    got = edge[...]
+    gain = scale[pl.ds(level[0], 1), :]
+    gain_out[...] = gain
+    grad_z = cot[...].astype(F32) * gain
+    got = (edge[...].astype(F32) * gain).astype(BF16)
     none = jnp.zeros_like(got)
     ext_out[:COLS] = jnp.where(row_id == 0, none, got)
     ext_out[COLS : COLS + count] = grad_z.astype(BF16)
@@ -102,12 +107,13 @@
 
 
 def attention_kernel(
-    meta, slots, halo, query, queryt, up, upt, tokens, rb, ext, resid_grad, shared, value, outp,
+    windows, slots, halo, query, queryt, up, upt, tokens, rb, ext, resid_grad, shared, value, outp,
     mid_out, send_out, keep_out, hidden_out, resid_out, base_out,
     key_all, val_all, key_blk, val_blk, keyt_blk, valt_blk, bias, mixed_all, dq_all, dkt, dvt, sums,
+    *, total_rows,
 ):
     step = pl.program_id(0)
-    window, row_id, total_rows = meta[1], meta[2], meta[3]
+    window, row_id = windows[0], lax.axis_index("row")
     width = query.shape[1]
     count = query.shape[0]
     rim = WMAX * COLS
@@ -218,11 +224,11 @@
 
 
 def spread_kernel(
-    meta, mid, keep, got,
+    refs, mid, keep, got,
     pair_out, across_out, first_out, second_out, third_out, first_keep, second_keep, own_out,
 ):
-    frame_id, row_id = meta[0], meta[2]
-    steps = [meta[4] - frame_id, meta[5] - frame_id]
+    frame_id, row_id = lax.axis_index("frame"), lax.axis_index("row")
+    steps = [refs[0, 0] - frame_id, refs[0, 1] - frame_id]
     width, count = mid.shape[1], mid.shape[2]
     rim = WMAX * COLS
     half = keep.shape[0]
@@ -263,8 +269,9 @@
         out[begin:, width:] = rows[piece // 2 :]
 
 
-def coded_kernel(meta, hidden, halo, residual, gain, taps, coded_out, ext):
-    row_id = meta[2]
+def coded_kernel(hidden, halo, residual, gain, taps, coded_out, gain_out, ext):
+    gain_out[...] = gain[...]
+    row_id = lax.axis_index("row")
     count = hidden.shape[0]
     got = halo[...]
     none = jnp.zeros_like(got)
@@ -278,14 +285,14 @@
     coded_out[...] = ((residual[...] + total) * gain[...]).astype(BF16)
 
 
-def select_kernel(meta, pair, cross, first, second, far_first, far_second, _, slots_out, edge_out):
-    frame_id, row_id = meta[0], meta[2]
+def select_kernel(refs, pair, cross, first, second, far_first, far_second, _, slots_out, edge_out):
+    frame_id, row_id = lax.axis_index("frame"), lax.axis_index("row")
     count = pair.shape[0]
     rim = WMAX * COLS
     pair_step = jnp.where((frame_id & 1) == 0, 1, -1)
     link_step = jnp.where((frame_id & 2) == 0, 2, -2)
     for slot in range(2):
-        step = meta[4 + slot] - frame_id
+        step = refs[0, slot] - frame_id
         for distance, source in (
             (pair_step, pair),
             (-pair_step, cross),
@@ -303,10 +310,10 @@
 
 
 def relay_kernel(
-    meta, across, first, second, third, first_keep, second_keep, own, pair,
+    across, first, second, third, first_keep, second_keep, own, pair, _,
     first_out, second_out, pair_out, own_out,
 ):
-    frame_id = meta[0]
+    frame_id = lax.axis_index("frame")
     width = first_keep.shape[0]
     packed = third.shape[0]
     pair_out[...] = pair[...]
@@ -328,22 +335,22 @@
         ).astype(BF16)
 
 
-def final_kernel(base, first, second, pair, own, other, grad_out, own_out):
+def final_kernel(base, first, second, pair, grad_out, last_out):
     returned = first[...].astype(F32) + second[...].astype(F32) + pair[...].astype(F32)
     grad_out[...] = (base[...] + returned.T).astype(BF16)
-    own_out[...] = (own[...].astype(F32) + other[...].astype(F32)).astype(BF16)
-
-
-def gather_kernel(meta, own, first, second, third, pieces_out):
-    me = meta[0] & 3
+    last_out[...] = returned[:16, :128]
+
+
+def gather_kernel(own, first, second, third, _, pieces_out):
+    me = lax.axis_index("frame") & 3
     piece = own.shape[0]
     for mask, part in enumerate((own, first, second, third)):
         begin = pl.multiple_of((me ^ mask) * piece, piece)
         pieces_out[pl.ds(begin, piece)] = part[...]
 
 
-def weights_kernel(meta, own, other, shared_out, value_out, output_out, taps_out, *, norm):
-    row_id = meta[2]
+def weights_kernel(own, other, shared_out, value_out, output_out, taps_out, *, norm):
+    row_id = lax.axis_index("row")
     width = shared_out.shape[1]
     low = jnp.where(row_id == 0, own[...].astype(F32), other[...].astype(F32)) * norm
     high = jnp.where(row_id == 0, other[...].astype(F32), own[...].astype(F32)) * norm
@@ -363,28 +370,17 @@
     rows_dev = count // COLS
     frames = lax.axis_size("frame")
     total_rows = rows_dev * lax.axis_size("row")
-    frame_id = lax.axis_index("frame")
     row_id = lax.axis_index("row")
-    refs = ref_frames[0]
-    odd = (frame_id & 1) == 1
     rim = WMAX * COLS
     tokens = latents[0]
-    low_link = (frame_id & 2) == 0
-    meta = jnp.concatenate(
-        [jnp.stack([frame_id, windows[0], row_id, jnp.int32(total_rows)]).astype(jnp.int32), refs]
-    )
-    gain = lax.dynamic_slice_in_dim(quant_scale, quant_level[0], 1, 0)
-
-    from_pair = swapped(tokens, "frame", 1)
+    cot = cotangent[0]
+
+    cot_edge = swapped(jnp.where(row_id == 0, cot[count - COLS :], cot[:COLS]), "row", 1)
     from_first = along(tokens, 0)
     from_second = along(tokens, 2)
-    from_before = jnp.where(low_link, from_second, from_first)
-    from_after = jnp.where(low_link, from_first, from_second)
-
-    cot = cotangent[0]
-    cot_edge = jnp.where(row_id == 0, cot[count - COLS :], cot[:COLS])
-    grad_edge = swapped((cot_edge.astype(F32) * gain).astype(BF16), "row", 1)
-    grad_resid, grad_rb, grad_ext, up, upt, query, queryt = whole_call(
+    from_pair = swapped(tokens, "frame", 1)
+
+    grad_resid, grad_rb, grad_ext, up, upt, query, queryt, gain = whole_call(
         before_kernel,
         [
             ((count, width), F32),
@@ -394,21 +390,26 @@
             ((width, count), BF16),
             ((count, width), BF16),
             ((width, count), BF16),
+            ((1, width), F32),
         ],
-        (meta, cot, gain, grad_edge, tokens, conv_taps, shared_proj, output_proj),
+        (
+            quant_level, quant_scale, cot_edge, cot, tokens, conv_taps, shared_proj, output_proj,
+        ),
         smem=(0,),
         flops=2 * 5 * count * width * width,
         moved=4 * count * width * 6,
         name="gradient_path",
     )
 
-    far_first = along(from_second, 0)
-    far_second = along(from_first, 2)
-    from_cross = swapped(jnp.where(odd, from_before, from_after), "frame", 1)
+    frame_id = lax.axis_index("frame")
+    by_second = (frame_id & 1) != ((frame_id >> 1) & 1)
+    far_first = along(from_second, 0, relayed=True)
+    far_second = along(from_first, 2, relayed=True)
+    from_cross = swapped(jnp.where(by_second, from_second, from_first), "frame", 1)
     slots, edge = whole_call(
         select_kernel,
         [((2, count, width), BF16), ((2, rim, width), BF16)],
-        (meta, from_pair, from_cross, from_first, from_second, far_first, far_second, upt),
+        (ref_frames, from_pair, from_cross, from_first, from_second, far_first, far_second, gain),
         smem=(0,),
         flops=count * width,
         moved=count * width * 8,
@@ -421,7 +422,7 @@
     ext_count = count + 2 * rim
     half = 3 * width
     mid, send, keep, hidden, residual, base = whole_call(
-        attention_kernel,
+        functools.partial(attention_kernel, total_rows=total_rows),
         [
             ((2, width, count), F32),
             ((half + width, width), BF16),
@@ -431,7 +432,7 @@
             ((count, width), F32),
         ],
         (
-            meta, slots, halo, query, queryt, up, upt, tokens, grad_rb, grad_ext, grad_resid,
+            windows, slots, halo, query, queryt, up, upt, tokens, grad_rb, grad_ext, grad_resid,
             shared_proj, value_proj, output_proj,
         ),
         smem=(0,),
@@ -473,18 +474,26 @@
             ((width, count), F32),
             ((piece, width), F32),
         ],
-        (meta, mid, keep, got),
+        (ref_frames, mid, keep, got),
         smem=(0,),
         flops=count * width * 12,
         moved=count * width * 30,
         name="spread",
     )
 
+    third = swapped(third, "frame", 3)
     across = swapped(across, "frame", 1)
     first = along(first, 0)
     second = along(second, 2)
-    third = swapped(third, "frame", 3)
-
+    coded, gain = whole_call(
+        coded_kernel,
+        [((count, width), BF16), ((1, width), F32)],
+        (hidden, hidden_halo, residual, gain, conv_taps),
+        scratch=[pltpu.VMEM((count + 2 * COLS, width), BF16)],
+        flops=2 * 3 * count * width * width,
+        moved=count * width * 8,
+        name="context",
+    )
     back_first, back_second, back_pair, own = whole_call(
         relay_kernel,
         [
@@ -493,25 +502,25 @@
             ((width, count), BF16),
             ((piece, width), BF16),
         ],
-        (meta, across, first, second, third, first_keep, second_keep, own, pair),
-        smem=(0,),
+        (across, first, second, third, first_keep, second_keep, own, pair, gain),
         flops=count * width * 4,
         moved=count * width * 16,
         name="relay",
     )
+    mask = 4
+    other = swapped(own, "frame", mask)
     back_first = along(back_first, 0)
     back_second = along(back_second, 2)
     back_pair = swapped(back_pair, "frame", 1)
-    mask = 4
-    other = swapped(own, "frame", mask)
     while 2 * mask < frames:
         mask *= 2
         own = (own.astype(F32) + other.astype(F32)).astype(BF16)
         other = swapped(own, "frame", mask)
-    grad_latents, own = whole_call(
+    own = (own.astype(F32) + other.astype(F32)).astype(BF16)
+    grad_latents, last = whole_call(
         final_kernel,
-        [((count, width), BF16), ((piece, width), BF16)],
-        (base, back_first, back_second, back_pair, own, other),
+        [((count, width), BF16), ((16, 128), F32)],
+        (base, back_first, back_second, back_pair),
         flops=count * width * 4,
         moved=count * width * 12,
         name="latent_gradient",
@@ -519,8 +528,7 @@
     (pieces,) = whole_call(
         gather_kernel,
         [((half, width), BF16)],
-        (meta, own, *[swapped(own, "frame", mask) for mask in (1, 2, 3)]),
-        smem=(0,),
+        (own, *[swapped(own, "frame", mask) for mask in (1, 2, 3)], last),
         flops=half * width,
         moved=half * width * 4,
         name="pieces",
@@ -536,23 +544,12 @@
             ((width, width), F32),
             ((3, width, width), F32),
         ],
-        (meta, pieces, other),
-        smem=(0,),
+        (pieces, other),
         flops=6 * width * width,
         moved=6 * width * width * 6,
         name="weight_gradients",
     )
 
-    (coded,) = whole_call(
-        coded_kernel,
-        [((count, width), BF16)],
-        (meta, hidden, hidden_halo, residual, gain, conv_taps),
-        smem=(0,),
-        scratch=[pltpu.VMEM((count + 2 * COLS, width), BF16)],
-        flops=2 * 3 * count * width * width,
-        moved=count * width * 8,
-        name="context",
-    )
     return (
         coded[None],
         grad_latents[None],

time: 89.9 us -> 80.8 us (0.90)
  starting transfers between devices: 31.9 us -> 19.7 us
  waiting for transfers between devices: 28.1 us -> 34.3 us
  Pallas kernels: 25.7 us -> 22.4 us
    ppermute x8, waiting for transfers between devices: 4.22 us -> 14 us  [along(): return lax.ppermute(array, 'frame', pairs)]
    ppermute x8, starting transfers between devices: 17 us -> 8.93 us  [along(): return lax.ppermute(array, 'frame', pairs)]
    ppermute x14, starting transfers between devices: 14.9 us -> 10.8 us  [swapped(): return lax.ppermute(array, axis, pairs)]
    ppermute x14, waiting for transfers between devices: 23.8 us -> 20.3 us  [swapped(): return lax.ppermute(array, axis, pairs)]
    pallas_call x9, Pallas kernels: 25.7 us -> 22.4 us  [whole_call(): pl.pallas_call(body, out_shape=[jax.ShapeDtypeStruct(shape, dtype) for sh...]
    unnamed x18 -> x20, local copies, waits for them, and re-layouts: 1.64 us -> 1.88 us
  transfers between devices with their start and end apart: 22 -> 22, of which waited for: 10 -> 13; matrix products, arithmetic and copies ran while one was open for 0% -> 0% of each run, Pallas kernels for 3% -> 4%
where the time goes in v4:
time: 80.8 us; the launch traced here: 80.5 us
  waiting for transfers between devices  34.3 us (42%)
  Pallas kernels  22.4 us (28%)
  starting transfers between devices  19.7 us (24%)
  between operations  2.15 us (3%)
  local copies, waits for them, and re-layouts  1.88 us (2%)
    pallas_call x9, Pallas kernels, whole_call(): pl.pallas_call(body, out_shape=[jax.ShapeDtypeStruct(shape, dtype) for sh...  22.4 us
    ppermute x14, waiting for transfers between devices, swapped(): return lax.ppermute(array, axis, pairs)  20.3 us
    ppermute x8, waiting for transfers between devices, along(): return lax.ppermute(array, 'frame', pairs)  14 us
    ppermute x14, starting transfers between devices, swapped(): return lax.ppermute(array, axis, pairs)  10.8 us
    ppermute x8, starting transfers between devices, along(): return lax.ppermute(array, 'frame', pairs)  8.93 us
    unnamed x20, local copies, waits for them, and re-layouts  1.88 us
  transfers between devices with their start and end apart: 22, of which 13 were waited for; matrix products, arithmetic and copies ran while one was open for 0% of the time, Pallas kernels for 4%

profile of v4, /device:TPU:0, one launch (start us, length us, event | category | flops | bytes accessed | tf_op | source)
XLA Modules:
  0.0 80.5 jit_solution(7533164730726533328)
XLA Ops:
  0.6 3.1 %collective-permute-start.2 = (bf16[512,256]{1,0:T(8,128)(2,1)}, bf16[512,256]{1,0:T(8,128)(2,1)S(1)}, u32[]{:S(2)}, u32[]{:S(2)}) collective-permute-start(bf16[512,256]{1,0:T(8,128)(2,1)} %bitcast.7), channel_id=1, source_target_pairs={{0,4},{2,6},{8,12},{10,14},{4,0},{6,2},{12,8},{14,10},{1,5},{3,7},... | collective-permute-start | bytes 786440 | tf_op jit(solution)/shard_map/ppermute | solution.py:56
  4.4 1.6 %collective-permute-start = (bf16[512,256]{1,0:T(8,128)(2,1)}, bf16[512,256]{1,0:T(8,128)(2,1)S(1)}, u32[]{:S(2)}, u32[]{:S(2)}) collective-permute-start(bf16[512,256]{1,0:T(8,128)(2,1)} %bitcast.9), channel_id=1, source_target_pairs={{0,2},{2,0},{4,6},{6,4},{8,10},{10,8},{12,14},{14,12},{1,3},{3,1},... | collective-permute-start | bytes 786440 | tf_op jit(solution)/shard_map/ppermute | solution.py:47
  6.0 4.3 %collective-permute-done.2.first = bf16[512,256]{1,0:T(8,128)(2,1)S(1)} collective-permute-done((bf16[512,256]{1,0:T(8,128)(2,1)}, bf16[512,256]{1,0:T(8,128)(2,1)S(1)}, u32[]{:S(2)}, u32[]{:S(2)}) %collective-permute-start.2) | collective-permute-done | bytes 262176 | tf_op jit(solution)/shard_map/ppermute | solution.py:56
  10.3 1.7 %collective-permute-start.3 = (bf16[512,256]{1,0:T(8,128)(2,1)S(1)}, bf16[512,256]{1,0:T(8,128)(2,1)S(1)}, u32[]{:S(2)}, u32[]{:S(2)}) collective-permute-start(bf16[512,256]{1,0:T(8,128)(2,1)S(1)} %broadcast_select_fusion), channel_id=1, source_target_pairs={{0,2},{2,0},{4,6},{6,4},{8,10},{10,8},{12,14},{14,12},{1,3},{3,1},... | collective-permute-start | bytes 786440 | tf_op jit(solution)/shard_map/ppermute | solution.py:47
  12.7 1.3 %collective-permute-start.4 = (bf16[512,256]{1,0:T(8,128)(2,1)S(1)}, bf16[512,256]{1,0:T(8,128)(2,1)S(1)}, u32[]{:S(2)}, u32[]{:S(2)}) collective-permute-start(bf16[512,256]{1,0:T(8,128)(2,1)S(1)} %collective-permute-done.1.second), channel_id=1, source_target_pairs={{8,12},{10,14},{4,0},{6,2},{9,13},{11,15},{5,1},{7,3},{24,28},{26,... | collective-permute-start | bytes 786440 | tf_op jit(solution)/shard_map/ppermute | solution.py:56
  15.3 0.9 %copy-done.2 = bf16[1,512,256]{2,1,0:T(8,128)(2,1)S(1)} copy-done((bf16[1,512,256]{2,1,0:T(8,128)(2,1)S(1)}, bf16[1,512,256]{2,1,0:T(8,128)(2,1)}, u32[]{:S(2)}) %copy-start.2) | copy-done | bytes 262168
  16.2 0.9 %copy-done.5 = bf16[256,256]{1,0:T(8,128)(2,1)S(1)} copy-done((bf16[256,256]{1,0:T(8,128)(2,1)S(1)}, bf16[256,256]{1,0:T(8,128)(2,1)}, u32[]{:S(2)}) %copy-start.5) | copy-done | bytes 131096
  17.2 0.8 %gradient_path.1 = (f32[512,256]{1,0:T(8,128)S(1)}, bf16[512,256]{1,0:T(8,128)(2,1)S(1)}, bf16[640,256]{1,0:T(8,128)(2,1)S(1)}, bf16[512,256]{1,0:T(8,128)(2,1)S...) custom-call(s32[1]{0:T(128)S(6)} %copy.17.level, ...), custom_call_target="tpu_custom_call" | custom-call | flops 335544320 | bytes 3145728 | tf_op jit(solution)/shard_map/gradient_path/pallas_call | solution.py:67
  18.1 8.0 %collective-permute-done.4.far_first = bf16[512,256]{1,0:T(8,128)(2,1)S(1)} collective-permute-done((bf16[512,256]{1,0:T(8,128)(2,1)S(1)}, bf16[512,256]{1,0:T(8,128)(2,1)S(1)}, u32[]{:S(2)}, u32[]{:S(2)}) %collective-permute-start.4) | collective-permute-done | bytes 262176 | tf_op jit(solution)/shard_map/ppermute | solution.py:56
  28.2 16.4 %attention.1 = (f32[2,256,512]{2,1,0:T(8,128)S(1)}, bf16[1024,256]{1,0:T(8,128)(2,1)S(1)}, f32[768,256]{1,0:T(8,128)S(1)}, bf16[512,256]{1,0:T(8,128)(2,1)S(1)},...) custom-call(s32[1]{0:T(128)S(6)} %copy.16.windows, bf16[2,512,256]{2,1,0:T(8,128)(2,1)S(1)} %get-tuple-element.43.slots, ...), custom_call_target="tpu_custom_call" | custom-call | flops 9663676416 | bytes 7864320 | tf_op jit(solution)/shard_map/attention/pallas_call | solution.py:67
  44.8 1.8 %collective-permute-done.9.got = bf16[1024,256]{1,0:T(8,128)(2,1)S(1)} collective-permute-done((bf16[1024,256]{1,0:T(8,128)(2,1)S(1)}, bf16[1024,256]{1,0:T(8,128)(2,1)S(1)}, u32[]{:S(2)}, u32[]{:S(2)}) %collective-permute-start.9) | collective-permute-done | bytes 524320 | tf_op jit(solution)/shard_map/ppermute | solution.py:47
  46.6 1.0 %spread.1 = (bf16[256,512]{1,0:T(8,128)(2,1)S(1)}, bf16[352,512]{1,0:T(8,128)(2,1)S(1)}, bf16[352,512]{1,0:T(8,128)(2,1)S(1)}, bf16[256,512]{1,0:T(8,128)(2,1)S(...) custom-call(s32[1,2]{1,0:T(1,128)S(1)} %copy-done.8, ...), custom_call_target="tpu_custom_call" | custom-call | flops 1572864 | bytes 3932160 | tf_op jit(solution)/shard_map/spread/pallas_call | solution.py:67
  48.3 2.8 %collective-permute-start.13 = (bf16[96,512]{1,0:T(8,128)(2,1)S(1)}, bf16[96,512]{1,0:T(8,128)(2,1)S(1)}, u32[]{:S(2)}, u32[]{:S(2)}) collective-permute-start(bf16[96,512]{1,0:T(8,128)(2,1)S(1)} %get-tuple-element.62), channel_id=1, source_target_pairs={{0,6},{2,4},{4,2},{6,0},{8,14},{10,12},{12,10},{14,8},{1,7},{3,5},... | collective-permute-start | bytes 294920 | tf_op jit(solution)/shard_map/ppermute | solution.py:47
  51.9 1.2 %collective-permute-done.8.halo = bf16[64,256]{1,0:T(8,128)(2,1)S(1)} collective-permute-done((bf16[64,256]{1,0:T(8,128)(2,1)S(1)}, bf16[64,256]{1,0:T(8,128)(2,1)S(1)}, u32[]{:S(2)}, u32[]{:S(2)}) %collective-permute-start.8) | collective-permute-done | bytes 32800 | tf_op jit(solution)/shard_map/ppermute | solution.py:47
  53.1 1.1 %context.1 = (bf16[512,256]{1,0:T(8,128)(2,1)}, f32[1,256]{1,0:T(1,128)S(1)}) custom-call(bf16[512,256]{1,0:T(8,128)(2,1)S(1)} %get-tuple-element.52.hidden, bf16[64,256]{1,0:T(8,128)(2,1)S(1)} %collective-permute-done.8.halo, f32[512,256]{1,0:T(8,128)S(1)} %get-tuple-element.53.residual, f32[1,256]{1,0:T(1,128)S(1)} %get-tuple-element.42._.gain, ...), custom_call_target="tpu_custom_call" | custom-call | flops 201326592 | bytes 1048576 | tf_op jit(solution)/shard_map/context/pallas_call | solution.py:67
  54.2 7.2 %collective-permute-done.13.third = bf16[96,512]{1,0:T(8,128)(2,1)S(1)} collective-permute-done((bf16[96,512]{1,0:T(8,128)(2,1)S(1)}, bf16[96,512]{1,0:T(8,128)(2,1)S(1)}, u32[]{:S(2)}, u32[]{:S(2)}) %collective-permute-start.13) | collective-permute-done | bytes 98336 | tf_op jit(solution)/shard_map/ppermute | solution.py:47
  62.1 1.7 %collective-permute-start.14 = (bf16[256,512]{1,0:T(8,128)(2,1)S(1)}, bf16[256,512]{1,0:T(8,128)(2,1)S(1)}, u32[]{:S(2)}, u32[]{:S(2)}) collective-permute-start(bf16[256,512]{1,0:T(8,128)(2,1)S(1)} %get-tuple-element.68), channel_id=1, source_target_pairs={{0,4},{2,6},{8,12},{10,14},{4,0},{6,2},{12,8},{14,10},{1,5},{3,7},... | collective-permute-start | bytes 786440 | tf_op jit(solution)/shard_map/ppermute | solution.py:56
  65.1 4.0 %collective-permute-done.17 = bf16[192,256]{1,0:T(8,128)(2,1)S(1)} collective-permute-done((bf16[192,256]{1,0:T(8,128)(2,1)S(1)}, bf16[192,256]{1,0:T(8,128)(2,1)S(1)}, u32[]{:S(2)}, u32[]{:S(2)}) %collective-permute-start.17) | collective-permute-done | bytes 98336 | tf_op jit(solution)/shard_map/ppermute | solution.py:47
  69.2 2.0 %collective-permute-start.19 = (bf16[192,256]{1,0:T(8,128)(2,1)S(1)}, bf16[192,256]{1,0:T(8,128)(2,1)S(1)}, u32[]{:S(2)}, u32[]{:S(2)}) collective-permute-start(bf16[192,256]{1,0:T(8,128)(2,1)S(1)} %add_convert_fusion.own), channel_id=1, source_target_pairs={{0,4},{2,6},{4,0},{6,2},{8,12},{10,14},{12,8},{14,10},{1,5},{3,7},... | collective-permute-start | bytes 294920 | tf_op jit(solution)/shard_map/ppermute | solution.py:47
  71.2 1.7 %collective-permute-done.14.first = bf16[256,512]{1,0:T(8,128)(2,1)S(1)} collective-permute-done((bf16[256,512]{1,0:T(8,128)(2,1)S(1)}, bf16[256,512]{1,0:T(8,128)(2,1)S(1)}, u32[]{:S(2)}, u32[]{:S(2)}) %collective-permute-start.14) | collective-permute-done | bytes 262176 | tf_op jit(solution)/shard_map/ppermute | solution.py:56
  73.4 0.9 %latent_gradient.1 = (bf16[512,256]{1,0:T(8,128)(2,1)}, f32[16,128]{1,0:T(8,128)S(1)}) custom-call(f32[512,256]{1,0:T(8,128)S(1)} %get-tuple-element.55.base, bf16[256,512]{1,0:T(8,128)(2,1)S(1)} %collective-permute-done.14.first, bf16[256,512]{1,0:T(8,128)(2,1)S(1)} %collective-permute-done.15.second, bf16[256,512]{1,0:T(8,128)(2,1)S(1)} %collective-permute-done.16.pair), custom_call_target="tpu_custom_call" | custom-call | flops 524288 | bytes 1572864 | tf_op jit(solution)/shard_map/latent_gradient/pallas_call | solution.py:67
  75.5 2.0 %collective-permute-done.18.first = bf16[192,256]{1,0:T(8,128)(2,1)S(1)} collective-permute-done((bf16[192,256]{1,0:T(8,128)(2,1)S(1)}, bf16[192,256]{1,0:T(8,128)(2,1)S(1)}, u32[]{:S(2)}, u32[]{:S(2)}) %collective-permute-start.18) | collective-permute-done | bytes 98336 | tf_op jit(solution)/shard_map/ppermute | solution.py:47
  77.6 1.7 %collective-permute-done.21.other = bf16[768,256]{1,0:T(8,128)(2,1)S(1)} collective-permute-done((bf16[768,256]{1,0:T(8,128)(2,1)S(1)}, bf16[768,256]{1,0:T(8,128)(2,1)S(1)}, u32[]{:S(2)}, u32[]{:S(2)}) %collective-permute-start.21) | collective-permute-done | bytes 393248 | tf_op jit(solution)/shard_map/ppermute | solution.py:47
  79.3 1.2 %weight_gradients.1 = (f32[256,256]{1,0:T(8,128)}, f32[256,256]{1,0:T(8,128)}, f32[256,256]{1,0:T(8,128)}, f32[3,256,256]{2,1,0:T(8,128)}) custom-call(bf16[768,256]{1,0:T(8,128)(2,1)S(1)} %pieces.1.own, bf16[768,256]{1,0:T(8,128)(2,1)S(1)} %collective-permute-done.21.other), custom_call_target="tpu_custom_call" | custom-call | flops 393216 | bytes 2359296 | tf_op jit(solution)/shard_map/weight_gradients/pallas_call | solution.py:67
  (53 shorter events, 9.0 us)
Async XLA Ops:
  0.6 9.6 %collective-permute-start.2 = (bf16[512,256]{1,0:T(8,128)(2,1)}, bf16[512,256]{1,0:T(8,128)(2,1)S(1)}, u32[]{:S(2)}, u32[]{:S(2)}) collective-permute-start(bf16[512,256]{1,0:T(8,128)(2,1)} %bitcast.7), channel_id=1, source_target_pairs={{0,4},{2,6},{8,12},{10,14},{4,0},{6,2},{12,8},{14,10},{1,5},{3,7},... | collective-permute-start | bytes 786440 | tf_op jit(solution)/shard_map/ppermute | solution.py:56
  3.7 6.5 %collective-permute-start.1 = (bf16[512,256]{1,0:T(8,128)(2,1)}, bf16[512,256]{1,0:T(8,128)(2,1)S(1)}, u32[]{:S(2)}, u32[]{:S(2)}) collective-permute-start(bf16[512,256]{1,0:T(8,128)(2,1)} %bitcast.8), channel_id=1, source_target_pairs={{4,8},{6,10},{8,4},{10,6},{5,9},{7,11},{9,5},{11,7},{20,24},{22,26... | collective-permute-start | bytes 786440 | tf_op jit(solution)/shard_map/ppermute | solution.py:56
  4.4 13.6 %collective-permute-start = (bf16[512,256]{1,0:T(8,128)(2,1)}, bf16[512,256]{1,0:T(8,128)(2,1)S(1)}, u32[]{:S(2)}, u32[]{:S(2)}) collective-permute-start(bf16[512,256]{1,0:T(8,128)(2,1)} %bitcast.9), channel_id=1, source_target_pairs={{0,2},{2,0},{4,6},{6,4},{8,10},{10,8},{12,14},{14,12},{1,3},{3,1},... | collective-permute-start | bytes 786440 | tf_op jit(solution)/shard_map/ppermute | solution.py:47
  6.0 9.3 %copy-start = (bf16[3,256,256]{2,1,0:T(8,128)(2,1)S(1)}, bf16[3,256,256]{2,1,0:T(8,128)(2,1)}, u32[]{:S(2)}) copy-start(bf16[3,256,256]{2,1,0:T(8,128)(2,1)} %taps.3) | copy-start | bytes 1179652
  10.3 7.8 %collective-permute-start.3 = (bf16[512,256]{1,0:T(8,128)(2,1)S(1)}, bf16[512,256]{1,0:T(8,128)(2,1)S(1)}, u32[]{:S(2)}, u32[]{:S(2)}) collective-permute-start(bf16[512,256]{1,0:T(8,128)(2,1)S(1)} %broadcast_select_fusion), channel_id=1, source_target_pairs={{0,2},{2,0},{4,6},{6,4},{8,10},{10,8},{12,14},{14,12},{1,3},{3,1},... | collective-permute-start | bytes 786440 | tf_op jit(solution)/shard_map/ppermute | solution.py:47
  12.0 6.0 %collective-permute-start.5 = (bf16[512,256]{1,0:T(8,128)(2,1)S(1)}, bf16[512,256]{1,0:T(8,128)(2,1)S(1)}, u32[]{:S(2)}, u32[]{:S(2)}) collective-permute-start(bf16[512,256]{1,0:T(8,128)(2,1)S(1)} %collective-permute-done.2.first), channel_id=1, source_target_pairs={{4,8},{6,10},{8,4},{10,6},{5,9},{7,11},{9,5},{11,7},{20,24},{22,26... | collective-permute-start | bytes 786440 | tf_op jit(solution)/shard_map/ppermute | solution.py:56
  12.7 13.4 %collective-permute-start.4 = (bf16[512,256]{1,0:T(8,128)(2,1)S(1)}, bf16[512,256]{1,0:T(8,128)(2,1)S(1)}, u32[]{:S(2)}, u32[]{:S(2)}) collective-permute-start(bf16[512,256]{1,0:T(8,128)(2,1)S(1)} %collective-permute-done.1.second), channel_id=1, source_target_pairs={{8,12},{10,14},{4,0},{6,2},{9,13},{11,15},{5,1},{7,3},{24,28},{26,... | collective-permute-start | bytes 786440 | tf_op jit(solution)/shard_map/ppermute | solution.py:56
  14.0 1.3 %collective-permute-start.6 = (bf16[64,256]{1,0:T(8,128)(2,1)S(1)}, bf16[64,256]{1,0:T(8,128)(2,1)S(1)}, u32[]{:S(2)}, u32[]{:S(2)}) collective-permute-start(bf16[64,256]{1,0:T(8,128)(2,1)S(1)} %select_bitcast_fusion), channel_id=1, source_target_pairs={{0,1},{1,0},{2,3},{3,2},{4,5},{5,4},{6,7},{7,6},{8,9},{9,8},{10,11... | collective-permute-start | bytes 98312 | tf_op jit(solution)/shard_map/ppermute | solution.py:47
  18.0 8.1 %copy-start.8 = (s32[1,2]{1,0:T(1,128)S(1)}, s32[1,2]{1,0:T(1,128)}, u32[]{:S(2)}) copy-start(s32[1,2]{1,0:T(1,128)} %refs.3) | copy-start | bytes 28
  26.8 1.4 %collective-permute-start.7 = (bf16[2,128,256]{2,1,0:T(8,128)(2,1)S(1)}, bf16[2,128,256]{2,1,0:T(8,128)(2,1)S(1)}, u32[]{:S(2)}, u32[]{:S(2)}) collective-permute-start(bf16[2,128,256]{2,1,0:T(8,128)(2,1)S(1)} %get-tuple-element.44), channel_id=1, source_target_pairs={{0,1},{1,0},{2,3},{3,2},{4,5},{5,4},{6,7},{7,6},{8,9},{9,8},{10,11... | collective-permute-start | bytes 393224 | tf_op jit(solution)/shard_map/ppermute | solution.py:47
  44.6 2.0 %collective-permute-start.9 = (bf16[1024,256]{1,0:T(8,128)(2,1)S(1)}, bf16[1024,256]{1,0:T(8,128)(2,1)S(1)}, u32[]{:S(2)}, u32[]{:S(2)}) collective-permute-start(bf16[1024,256]{1,0:T(8,128)(2,1)S(1)} %get-tuple-element.58), channel_id=1, source_target_pairs={{0,1},{1,0},{2,3},{3,2},{4,5},{5,4},{6,7},{7,6},{8,9},{9,8},{10,11... | collective-permute-start | bytes 1572872 | tf_op jit(solution)/shard_map/ppermute | solution.py:47
  47.6 13.8 %collective-permute-start.10 = (bf16[352,512]{1,0:T(8,128)(2,1)S(1)}, bf16[352,512]{1,0:T(8,128)(2,1)S(1)}, u32[]{:S(2)}, u32[]{:S(2)}) collective-permute-start(bf16[352,512]{1,0:T(8,128)(2,1)S(1)} %get-tuple-element.59), channel_id=1, source_target_pairs={{0,2},{2,0},{4,6},{6,4},{8,10},{10,8},{12,14},{14,12},{1,3},{3,1},... | collective-permute-start | bytes 1081352 | tf_op jit(solution)/shard_map/ppermute | solution.py:47
  48.2 13.2 %collective-permute-start.11 = (bf16[352,512]{1,0:T(8,128)(2,1)S(1)}, bf16[352,512]{1,0:T(8,128)(2,1)S(1)}, u32[]{:S(2)}, u32[]{:S(2)}) collective-permute-start(bf16[352,512]{1,0:T(8,128)(2,1)S(1)} %get-tuple-element.60), channel_id=1, source_target_pairs={{0,4},{2,6},{8,12},{10,14},{4,0},{6,2},{12,8},{14,10},{1,5},{3,7},... | collective-permute-start | bytes 1081352 | tf_op jit(solution)/shard_map/ppermute | solution.py:56
  48.3 13.1 %collective-permute-start.13 = (bf16[96,512]{1,0:T(8,128)(2,1)S(1)}, bf16[96,512]{1,0:T(8,128)(2,1)S(1)}, u32[]{:S(2)}, u32[]{:S(2)}) collective-permute-start(bf16[96,512]{1,0:T(8,128)(2,1)S(1)} %get-tuple-element.62), channel_id=1, source_target_pairs={{0,6},{2,4},{4,2},{6,0},{8,14},{10,12},{12,10},{14,8},{1,7},{3,5},... | collective-permute-start | bytes 294920 | tf_op jit(solution)/shard_map/ppermute | solution.py:47
  51.1 10.3 %collective-permute-start.12 = (bf16[256,512]{1,0:T(8,128)(2,1)S(1)}, bf16[256,512]{1,0:T(8,128)(2,1)S(1)}, u32[]{:S(2)}, u32[]{:S(2)}) collective-permute-start(bf16[256,512]{1,0:T(8,128)(2,1)S(1)} %get-tuple-element.61), channel_id=1, source_target_pairs={{4,8},{6,10},{8,4},{10,6},{5,9},{7,11},{9,5},{11,7},{20,24},{22,26... | collective-permute-start | bytes 786440 | tf_op jit(solution)/shard_map/ppermute | solution.py:56
  51.8 1.3 %collective-permute-start.8 = (bf16[64,256]{1,0:T(8,128)(2,1)S(1)}, bf16[64,256]{1,0:T(8,128)(2,1)S(1)}, u32[]{:S(2)}, u32[]{:S(2)}) collective-permute-start(bf16[64,256]{1,0:T(8,128)(2,1)S(1)} %slice_select_fusion), channel_id=1, source_target_pairs={{0,1},{1,0},{2,3},{3,2},{4,5},{5,4},{6,7},{7,6},{8,9},{9,8},{10,11... | collective-permute-start | bytes 98312 | tf_op jit(solution)/shard_map/ppermute | solution.py:47
  61.7 7.4 %collective-permute-start.17 = (bf16[192,256]{1,0:T(8,128)(2,1)S(1)}, bf16[192,256]{1,0:T(8,128)(2,1)S(1)}, u32[]{:S(2)}, u32[]{:S(2)}) collective-permute-start(bf16[192,256]{1,0:T(8,128)(2,1)S(1)} %get-tuple-element.72), channel_id=1, source_target_pairs={{0,8},{2,10},{4,12},{6,14},{8,0},{10,2},{12,4},{14,6},{1,9},{3,11}... | collective-permute-start | bytes 294920 | tf_op jit(solution)/shard_map/ppermute | solution.py:47
  62.1 10.8 %collective-permute-start.14 = (bf16[256,512]{1,0:T(8,128)(2,1)S(1)}, bf16[256,512]{1,0:T(8,128)(2,1)S(1)}, u32[]{:S(2)}, u32[]{:S(2)}) collective-permute-start(bf16[256,512]{1,0:T(8,128)(2,1)S(1)} %get-tuple-element.68), channel_id=1, source_target_pairs={{0,4},{2,6},{8,12},{10,14},{4,0},{6,2},{12,8},{14,10},{1,5},{3,7},... | collective-permute-start | bytes 786440 | tf_op jit(solution)/shard_map/ppermute | solution.py:56
  63.8 9.6 %collective-permute-start.15 = (bf16[256,512]{1,0:T(8,128)(2,1)S(1)}, bf16[256,512]{1,0:T(8,128)(2,1)S(1)}, u32[]{:S(2)}, u32[]{:S(2)}) collective-permute-start(bf16[256,512]{1,0:T(8,128)(2,1)S(1)} %get-tuple-element.69), channel_id=1, source_target_pairs={{4,8},{6,10},{8,4},{10,6},{5,9},{7,11},{9,5},{11,7},{20,24},{22,26... | collective-permute-start | bytes 786440 | tf_op jit(solution)/shard_map/ppermute | solution.py:56
  64.5 8.9 %collective-permute-start.16 = (bf16[256,512]{1,0:T(8,128)(2,1)S(1)}, bf16[256,512]{1,0:T(8,128)(2,1)S(1)}, u32[]{:S(2)}, u32[]{:S(2)}) collective-permute-start(bf16[256,512]{1,0:T(8,128)(2,1)S(1)} %get-tuple-element.70), channel_id=1, source_target_pairs={{0,2},{2,0},{4,6},{6,4},{8,10},{10,8},{12,14},{14,12},{1,3},{3,1},... | collective-permute-start | bytes 786440 | tf_op jit(solution)/shard_map/ppermute | solution.py:47
  69.1 5.6 %collective-permute-start.20 = (bf16[192,256]{1,0:T(8,128)(2,1)S(1)}, bf16[192,256]{1,0:T(8,128)(2,1)S(1)}, u32[]{:S(2)}, u32[]{:S(2)}) collective-permute-start(bf16[192,256]{1,0:T(8,128)(2,1)S(1)} %add_convert_fusion.own), channel_id=1, source_target_pairs={{0,6},{2,4},{4,2},{6,0},{8,14},{10,12},{12,10},{14,8},{1,7},{3,5},... | collective-permute-start | bytes 294920 | tf_op jit(solution)/shard_map/ppermute | solution.py:47
  69.2 6.3 %collective-permute-start.19 = (bf16[192,256]{1,0:T(8,128)(2,1)S(1)}, bf16[192,256]{1,0:T(8,128)(2,1)S(1)}, u32[]{:S(2)}, u32[]{:S(2)}) collective-permute-start(bf16[192,256]{1,0:T(8,128)(2,1)S(1)} %add_convert_fusion.own), channel_id=1, source_target_pairs={{0,4},{2,6},{4,0},{6,2},{8,12},{10,14},{12,8},{14,10},{1,5},{3,7},... | collective-permute-start | bytes 294920 | tf_op jit(solution)/shard_map/ppermute | solution.py:47
  72.9 4.6 %collective-permute-start.18 = (bf16[192,256]{1,0:T(8,128)(2,1)S(1)}, bf16[192,256]{1,0:T(8,128)(2,1)S(1)}, u32[]{:S(2)}, u32[]{:S(2)}) collective-permute-start(bf16[192,256]{1,0:T(8,128)(2,1)S(1)} %add_convert_fusion.own), channel_id=1, source_target_pairs={{0,2},{2,0},{4,6},{6,4},{8,10},{10,8},{12,14},{14,12},{1,3},{3,1},... | collective-permute-start | bytes 294920 | tf_op jit(solution)/shard_map/ppermute | solution.py:47
  77.5 1.8 %collective-permute-start.21 = (bf16[768,256]{1,0:T(8,128)(2,1)S(1)}, bf16[768,256]{1,0:T(8,128)(2,1)S(1)}, u32[]{:S(2)}, u32[]{:S(2)}) collective-permute-start(bf16[768,256]{1,0:T(8,128)(2,1)S(1)} %pieces.1.own), channel_id=1, source_target_pairs={{0,1},{1,0},{2,3},{3,2},{4,5},{5,4},{6,7},{7,6},{8,9},{9,8},{10,11... | collective-permute-start | bytes 1179656 | tf_op jit(solution)/shard_map/ppermute | solution.py:47
  (8 other events, 26.2 us)

commit v5 on v4

--- a/solution.py
+++ b/solution.py
@@ -13,6 +13,7 @@
 COLS = 64
 WMAX = 2
 BROWS = 2
+GROUP = 2
 
 SCALE = 1.5 / math.sqrt(DH)
 MASKED = -1e30
@@ -110,7 +111,7 @@
     windows, slots, halo, query, queryt, up, upt, tokens, rb, ext, resid_grad, shared, value, outp,
     mid_out, send_out, keep_out, hidden_out, resid_out, base_out,
     key_all, val_all, key_blk, val_blk, keyt_blk, valt_blk, bias, mixed_all, dq_all, dkt, dvt, sums,
-    *, total_rows,
+    score_all, grad_all, *, total_rows,
 ):
     step = pl.program_id(0)
     window, row_id = windows[0], lax.axis_index("row")
@@ -147,39 +148,51 @@
     bias[:, :span] = one_bias
     bias[:, span:] = one_bias
 
-    def all_heads(rows):
-        return jnp.concatenate([rows * mask.astype(BF16) for mask in masks], 0)
-
-    def own_lanes(stacked):
-        total = jnp.zeros((block, width), F32)
-        for head, mask in enumerate(masks):
-            total = total + stacked[head * block : (head + 1) * block] * mask
-        return total
-
     lane_head = lax.broadcasted_iota(jnp.int32, (1, width), 1) // DH
     masks = [(lane_head == head).astype(F32) for head in range(HEADS)]
-    cube = (HEADS, block, 2 * span)
-    flat = (HEADS * block, 2 * span)
-    scores = dot(all_heads(query[pl.ds(begin, block), :]), keyt_blk[...]).reshape(cube)
-    scores = scores + bias[...][None]
-    top = jnp.max(scores, axis=2, keepdims=True)
-    terms = jnp.exp2((scores - top) * (SCALE * LOG2E))
-    weights = terms * (1.0 / jnp.sum(terms, axis=2, keepdims=True))
-    prob = weights.astype(BF16)
-    mixed_all[pl.ds(begin, block), :] = own_lanes(
-        dot(prob.reshape(flat), val_blk[...])
-    ).astype(BF16)
-    grad_prob = dot(all_heads(up[pl.ds(begin, block), :]), valt_blk[...]).reshape(cube)
-    inner = jnp.sum(weights * grad_prob, axis=2, keepdims=True)
-    grad_score = ((weights * (grad_prob - inner)) * SCALE).astype(BF16)
-    dq_all[pl.ds(begin, block), :] = own_lanes(dot(grad_score.reshape(flat), key_blk[...]))
-    for head in range(HEADS):
-        lanes = slice(head * DH, (head + 1) * DH)
-        dv = dot(upt[lanes, pl.ds(begin, block)], prob[head])
-        dk = dot(queryt[lanes, pl.ds(begin, block)], grad_score[head])
-        for slot in range(2):
-            dvt[slot, lanes, pl.ds(begin, span)] += dv[:, slot * span : (slot + 1) * span]
-            dkt[slot, lanes, pl.ds(begin, span)] += dk[:, slot * span : (slot + 1) * span]
+    tall = GROUP * block
+    group_bias = jnp.concatenate([bias[...]] * GROUP, 0)
+    query_b, up_b = query[pl.ds(begin, block), :], up[pl.ds(begin, block), :]
+    mixed = jnp.zeros((block, width), F32)
+    grad_q = jnp.zeros((block, width), F32)
+
+    def products(group):
+        own = masks[group * GROUP : (group + 1) * GROUP]
+        stacked_q = jnp.concatenate([query_b * mask.astype(BF16) for mask in own], 0)
+        stacked_u = jnp.concatenate([up_b * mask.astype(BF16) for mask in own], 0)
+        rows = slice(group * tall, (group + 1) * tall)
+        score_all[rows] = dot(stacked_q, keyt_blk[...])
+        grad_all[rows] = dot(stacked_u, valt_blk[...])
+
+    products(0)
+    for group in range(HEADS // GROUP):
+        if (group + 1) * GROUP < HEADS:
+            products(group + 1)
+        rows = slice(group * tall, (group + 1) * tall)
+        scores = score_all[rows] + group_bias
+        top = jnp.max(scores, axis=1, keepdims=True)
+        terms = jnp.exp2((scores - top) * (SCALE * LOG2E))
+        weights = terms * (1.0 / jnp.sum(terms, axis=1, keepdims=True))
+        prob = weights.astype(BF16)
+        grad_prob = grad_all[rows]
+        inner = jnp.sum(weights * grad_prob, axis=1, keepdims=True)
+        grad_score = ((weights * (grad_prob - inner)) * SCALE).astype(BF16)
+        mixed_g = dot(prob, val_blk[...])
+        grad_q_g = dot(grad_score, key_blk[...])
+        for member in range(GROUP):
+            head = group * GROUP + member
+            part = slice(member * block, (member + 1) * block)
+            mixed = mixed + mixed_g[part] * masks[head]
+            grad_q = grad_q + grad_q_g[part] * masks[head]
+            lanes = slice(head * DH, (head + 1) * DH)
+            dv = dot(upt[lanes, pl.ds(begin, block)], prob[part])
+            dk = dot(queryt[lanes, pl.ds(begin, block)], grad_score[part])
+            for slot in range(2):
+                keys = slice(slot * span, (slot + 1) * span)
+                dvt[slot, lanes, pl.ds(begin, span)] += dv[:, keys]
+                dkt[slot, lanes, pl.ds(begin, span)] += dk[:, keys]
+    mixed_all[pl.ds(begin, block), :] = mixed.astype(BF16)
+    dq_all[pl.ds(begin, block), :] = grad_q
 
     @pl.when(step == pl.num_programs(0) - 1)
     def _():
@@ -233,29 +246,43 @@
     rim = WMAX * COLS
     half = keep.shape[0]
     piece = half // 4
-    parts = []
-    for slot in range(2):
+
+    def folded(slot):
         rims = got[half:, slot * rim : (slot + 1) * rim].astype(F32)
         none = jnp.zeros_like(rims)
         part = mid[slot]
         first = part[:, :rim] + jnp.where(row_id == 0, none, rims)
         last = part[:, count - rim :] + jnp.where(row_id == 0, rims, none)
-        parts.append(jnp.concatenate([first, part[:, rim : count - rim], last], 1))
-
-    def part_for(step):
-        chosen = jnp.zeros((width, count), F32)
-        for slot in range(2):
-            chosen = chosen + jnp.where(steps[slot] == step, parts[slot], 0.0)
-        return chosen
+        return jnp.concatenate([first, part[:, rim : count - rim], last], 1)
 
     pair_step = jnp.where((frame_id & 1) == 0, 1, -1)
     link_step = jnp.where((frame_id & 2) == 0, 1, -1)
-    pair_out[...] = part_for(pair_step).astype(BF16)
-    across_out[:width] = part_for(-pair_step).astype(BF16)
-    first_out[:width] = part_for(4 * link_step).astype(BF16)
-    second_out[...] = part_for(-4 * link_step).astype(BF16)
-    first_keep[...] = part_for(2 * link_step)
-    second_keep[...] = part_for(-2 * link_step)
+    for step, out in (
+        (pair_step, pair_out),
+        (-pair_step, across_out),
+        (4 * link_step, first_out),
+        (-4 * link_step, second_out),
+        (2 * link_step, first_keep),
+        (-2 * link_step, second_keep),
+    ):
+        by_zero, by_one = steps[0] == step, steps[1] == step
+
+        @pl.when(by_zero & by_one)
+        def _(out=out):
+            out[:width] = (folded(0) + folded(1)).astype(out.dtype)
+
+        @pl.when(by_zero & ~by_one)
+        def _(out=out):
+            out[:width] = folded(0).astype(out.dtype)
+
+        @pl.when(by_one & ~by_zero)
+        def _(out=out):
+            out[:width] = folded(1).astype(out.dtype)
+
+        @pl.when(~by_zero & ~by_one)
+        def _(out=out):
+            out[:width] = jnp.zeros((width, count), out.dtype)
+
     me = frame_id & 3
 
     def rows_of(index):
@@ -304,7 +331,7 @@
 
             @pl.when(step == distance)
             def _(source=source):
-                slots_out[slot] = source[...]
+                slots_out[slot] = source[:count]
                 begin = pl.multiple_of((1 - row_id) * (count - rim), rim)
                 edge_out[slot] = source[pl.ds(begin, rim)]
 
@@ -403,7 +430,8 @@
 
     frame_id = lax.axis_index("frame")
     by_second = (frame_id & 1) != ((frame_id >> 1) & 1)
-    far_first = along(from_second, 0, relayed=True)
+    longer = jnp.concatenate([from_second, from_second[:COLS]], 0)
+    far_first = along(longer, 0, relayed=True)
     far_second = along(from_first, 2, relayed=True)
     from_cross = swapped(jnp.where(by_second, from_second, from_first), "frame", 1)
     slots, edge = whole_call(
@@ -449,6 +477,8 @@
             pltpu.VMEM((2, width, ext_count), F32),
             pltpu.VMEM((2, width, ext_count), F32),
             pltpu.VMEM((2 * half, width), F32),
+            pltpu.VMEM((HEADS * block, 2 * span), F32),
+            pltpu.VMEM((HEADS * block, 2 * span), F32),
         ],
         grid=(count // block,),
         flops=6 * 2 * count * 2 * span * width * HEADS,

time: 80.8 us -> 78.6 us (0.973)
  starting transfers between devices: 19.7 us -> 26.1 us
  waiting for transfers between devices: 34.3 us -> 28.5 us
  local copies, waits for them, and re-layouts: 1.88 us -> 0.05 us
  Pallas kernels: 22.4 us -> 21.4 us
    ppermute x8, waiting for transfers between devices: 14 us -> 7.17 us  [along(): return lax.ppermute(array, 'frame', pairs)]
    ppermute x8, starting transfers between devices: 8.93 us -> 13.7 us  [along(): return lax.ppermute(array, 'frame', pairs)]
    unnamed x20 -> x16, local copies, waits for them, and re-layouts: 1.88 us -> 0.04 us
    ppermute x14, starting transfers between devices: 10.8 us -> 12.4 us  [swapped(): return lax.ppermute(array, axis, pairs)]
    ppermute x14, waiting for transfers between devices: 20.3 us -> 21.3 us  [swapped(): return lax.ppermute(array, axis, pairs)]
    pallas_call x9, Pallas kernels: 22.4 us -> 21.4 us  [whole_call(): pl.pallas_call(body, out_shape=[jax.ShapeDtypeStruct(shape, dtype) for sh...]
  transfers between devices with their start and end apart: 22 -> 22, of which waited for: 13 -> 14; matrix products, arithmetic and copies ran while one was open for 0% -> 0% of each run, Pallas kernels for 4% -> 4%
where the time goes in v5:
time: 78.6 us; the launch traced here: 78.3 us
  waiting for transfers between devices  28.5 us (36%)
  starting transfers between devices  26.1 us (33%)
  Pallas kernels  21.4 us (27%)
  between operations  2.17 us (3%)
    pallas_call x9, Pallas kernels, whole_call(): pl.pallas_call(body, out_shape=[jax.ShapeDtypeStruct(shape, dtype) for sh...  21.4 us
    ppermute x14, waiting for transfers between devices, swapped(): return lax.ppermute(array, axis, pairs)  21.3 us
    ppermute x8, starting transfers between devices, along(): return lax.ppermute(array, 'frame', pairs)  13.7 us
    ppermute x14, starting transfers between devices, swapped(): return lax.ppermute(array, axis, pairs)  12.4 us
    ppermute x8, waiting for transfers between devices, along(): return lax.ppermute(array, 'frame', pairs)  7.17 us
  transfers between devices with their start and end apart: 22, of which 14 were waited for; matrix products, arithmetic and copies ran while one was open for 0% of the time, Pallas kernels for 4%

profile of v5, /device:TPU:0, one launch (start us, length us, event | category | flops | bytes accessed | tf_op | source)
XLA Modules:
  0.0 78.3 jit_solution(11678369531209665485)
XLA Ops:
  1.3 5.9 %collective-permute-start.2 = (bf16[512,256]{1,0:T(8,128)(2,1)}, bf16[512,256]{1,0:T(8,128)(2,1)S(1)}, u32[]{:S(2)}, u32[]{:S(2)}) collective-permute-start(bf16[512,256]{1,0:T(8,128)(2,1)} %bitcast.8), channel_id=1, source_target_pairs={{0,4},{2,6},{8,12},{10,14},{4,0},{6,2},{12,8},{14,10},{1,5},{3,7},... | collective-permute-start | bytes 786440 | tf_op jit(solution)/shard_map/ppermute | solution.py:57
  7.2 1.5 %collective-permute-start = (bf16[512,256]{1,0:T(8,128)(2,1)}, bf16[512,256]{1,0:T(8,128)(2,1)S(1)}, u32[]{:S(2)}, u32[]{:S(2)}) collective-permute-start(bf16[512,256]{1,0:T(8,128)(2,1)} %bitcast.9), channel_id=1, source_target_pairs={{0,2},{2,0},{4,6},{6,4},{8,10},{10,8},{12,14},{14,12},{1,3},{3,1},... | collective-permute-start | bytes 786440 | tf_op jit(solution)/shard_map/ppermute | solution.py:48
  8.8 1.4 %collective-permute-start.4 = (bf16[576,256]{1,0:T(8,128)(2,1)S(1)}, bf16[576,256]{1,0:T(8,128)(2,1)S(1)}, u32[]{:S(2)}, u32[]{:S(2)}) collective-permute-start(bf16[576,256]{1,0:T(8,128)(2,1)S(1)} %pad_maximum_fusion), channel_id=1, source_target_pairs={{8,12},{10,14},{4,0},{6,2},{9,13},{11,15},{5,1},{7,3},{24,28},{26,... | collective-permute-start | bytes 884744 | tf_op jit(solution)/shard_map/ppermute | solution.py:57
  10.2 3.2 %collective-permute-done.2.first = bf16[512,256]{1,0:T(8,128)(2,1)S(1)} collective-permute-done((bf16[512,256]{1,0:T(8,128)(2,1)}, bf16[512,256]{1,0:T(8,128)(2,1)S(1)}, u32[]{:S(2)}, u32[]{:S(2)}) %collective-permute-start.2) | collective-permute-done | bytes 262176 | tf_op jit(solution)/shard_map/ppermute | solution.py:57
  13.5 1.6 %collective-permute-start.3 = (bf16[512,256]{1,0:T(8,128)(2,1)S(1)}, bf16[512,256]{1,0:T(8,128)(2,1)S(1)}, u32[]{:S(2)}, u32[]{:S(2)}) collective-permute-start(bf16[512,256]{1,0:T(8,128)(2,1)S(1)} %broadcast_select_fusion), channel_id=1, source_target_pairs={{0,2},{2,0},{4,6},{6,4},{8,10},{10,8},{12,14},{14,12},{1,3},{3,1},... | collective-permute-start | bytes 786440 | tf_op jit(solution)/shard_map/ppermute | solution.py:48
  17.9 2.8 %collective-permute-done.3.cross = bf16[512,256]{1,0:T(8,128)(2,1)S(1)} collective-permute-done((bf16[512,256]{1,0:T(8,128)(2,1)S(1)}, bf16[512,256]{1,0:T(8,128)(2,1)S(1)}, u32[]{:S(2)}, u32[]{:S(2)}) %collective-permute-start.3) | collective-permute-done | bytes 262176 | tf_op jit(solution)/shard_map/ppermute | solution.py:48
  23.5 15.5 %attention.1 = (f32[2,256,512]{2,1,0:T(8,128)S(1)}, bf16[1024,256]{1,0:T(8,128)(2,1)S(1)}, f32[768,256]{1,0:T(8,128)S(1)}, bf16[512,256]{1,0:T(8,128)(2,1)S(1)},...) custom-call(s32[1]{0:T(128)S(6)} %copy.16.windows, bf16[2,512,256]{2,1,0:T(8,128)(2,1)S(1)} %get-tuple-element.43.slots, ...), custom_call_target="tpu_custom_call" | custom-call | flops 9663676416 | bytes 7864320 | tf_op jit(solution)/shard_map/attention/pallas_call | solution.py:68
  39.2 1.7 %collective-permute-done.9.got = bf16[1024,256]{1,0:T(8,128)(2,1)S(1)} collective-permute-done((bf16[1024,256]{1,0:T(8,128)(2,1)S(1)}, bf16[1024,256]{1,0:T(8,128)(2,1)S(1)}, u32[]{:S(2)}, u32[]{:S(2)}) %collective-permute-start.9) | collective-permute-done | bytes 524320 | tf_op jit(solution)/shard_map/ppermute | solution.py:48
  41.0 0.9 %spread.1 = (bf16[256,512]{1,0:T(8,128)(2,1)S(1)}, bf16[352,512]{1,0:T(8,128)(2,1)S(1)}, bf16[352,512]{1,0:T(8,128)(2,1)S(1)}, bf16[256,512]{1,0:T(8,128)(2,1)S(...) custom-call(s32[1,2]{1,0:T(1,128)S(1)} %copy-done.6, ...), custom_call_target="tpu_custom_call" | custom-call | flops 1572864 | bytes 3932160 | tf_op jit(solution)/shard_map/spread/pallas_call | solution.py:68
  41.9 1.6 %collective-permute-start.10 = (bf16[352,512]{1,0:T(8,128)(2,1)S(1)}, bf16[352,512]{1,0:T(8,128)(2,1)S(1)}, u32[]{:S(2)}, u32[]{:S(2)}) collective-permute-start(bf16[352,512]{1,0:T(8,128)(2,1)S(1)} %get-tuple-element.59), channel_id=1, source_target_pairs={{0,2},{2,0},{4,6},{6,4},{8,10},{10,8},{12,14},{14,12},{1,3},{3,1},... | collective-permute-start | bytes 1081352 | tf_op jit(solution)/shard_map/ppermute | solution.py:48
  43.5 3.4 %collective-permute-start.11 = (bf16[352,512]{1,0:T(8,128)(2,1)S(1)}, bf16[352,512]{1,0:T(8,128)(2,1)S(1)}, u32[]{:S(2)}, u32[]{:S(2)}) collective-permute-start(bf16[352,512]{1,0:T(8,128)(2,1)S(1)} %get-tuple-element.60), channel_id=1, source_target_pairs={{0,4},{2,6},{8,12},{10,14},{4,0},{6,2},{12,8},{14,10},{1,5},{3,7},... | collective-permute-start | bytes 1081352 | tf_op jit(solution)/shard_map/ppermute | solution.py:57
  46.9 0.9 %collective-permute-start.13 = (bf16[96,512]{1,0:T(8,128)(2,1)S(1)}, bf16[96,512]{1,0:T(8,128)(2,1)S(1)}, u32[]{:S(2)}, u32[]{:S(2)}) collective-permute-start(bf16[96,512]{1,0:T(8,128)(2,1)S(1)} %get-tuple-element.62), channel_id=1, source_target_pairs={{0,6},{2,4},{4,2},{6,0},{8,14},{10,12},{12,10},{14,8},{1,7},{3,5},... | collective-permute-start | bytes 294920 | tf_op jit(solution)/shard_map/ppermute | solution.py:48
  48.5 1.2 %collective-permute-done.8.halo = bf16[64,256]{1,0:T(8,128)(2,1)S(1)} collective-permute-done((bf16[64,256]{1,0:T(8,128)(2,1)S(1)}, bf16[64,256]{1,0:T(8,128)(2,1)S(1)}, u32[]{:S(2)}, u32[]{:S(2)}) %collective-permute-start.8) | collective-permute-done | bytes 32800 | tf_op jit(solution)/shard_map/ppermute | solution.py:48
  49.7 1.1 %context.1 = (bf16[512,256]{1,0:T(8,128)(2,1)}, f32[1,256]{1,0:T(1,128)S(1)}) custom-call(bf16[512,256]{1,0:T(8,128)(2,1)S(1)} %get-tuple-element.52.hidden, bf16[64,256]{1,0:T(8,128)(2,1)S(1)} %collective-permute-done.8.halo, f32[512,256]{1,0:T(8,128)S(1)} %get-tuple-element.53.residual, f32[1,256]{1,0:T(1,128)S(1)} %get-tuple-element.42._.gain, ...), custom_call_target="tpu_custom_call" | custom-call | flops 201326592 | bytes 1048576 | tf_op jit(solution)/shard_map/context/pallas_call | solution.py:68
  50.8 7.5 %collective-permute-done.13.third = bf16[96,512]{1,0:T(8,128)(2,1)S(1)} collective-permute-done((bf16[96,512]{1,0:T(8,128)(2,1)S(1)}, bf16[96,512]{1,0:T(8,128)(2,1)S(1)}, u32[]{:S(2)}, u32[]{:S(2)}) %collective-permute-start.13) | collective-permute-done | bytes 98336 | tf_op jit(solution)/shard_map/ppermute | solution.py:48
  58.6 2.8 %collective-permute-start.17 = (bf16[192,256]{1,0:T(8,128)(2,1)S(1)}, bf16[192,256]{1,0:T(8,128)(2,1)S(1)}, u32[]{:S(2)}, u32[]{:S(2)}) collective-permute-start(bf16[192,256]{1,0:T(8,128)(2,1)S(1)} %get-tuple-element.72), channel_id=1, source_target_pairs={{0,8},{2,10},{4,12},{6,14},{8,0},{10,2},{12,4},{14,6},{1,9},{3,11}... | collective-permute-start | bytes 294920 | tf_op jit(solution)/shard_map/ppermute | solution.py:48
  63.0 2.0 %collective-permute-done.17 = bf16[192,256]{1,0:T(8,128)(2,1)S(1)} collective-permute-done((bf16[192,256]{1,0:T(8,128)(2,1)S(1)}, bf16[192,256]{1,0:T(8,128)(2,1)S(1)}, u32[]{:S(2)}, u32[]{:S(2)}) %collective-permute-start.17) | collective-permute-done | bytes 98336 | tf_op jit(solution)/shard_map/ppermute | solution.py:48
  65.0 2.4 %collective-permute-start.20 = (bf16[192,256]{1,0:T(8,128)(2,1)S(1)}, bf16[192,256]{1,0:T(8,128)(2,1)S(1)}, u32[]{:S(2)}, u32[]{:S(2)}) collective-permute-start(bf16[192,256]{1,0:T(8,128)(2,1)S(1)} %add_convert_fusion.own), channel_id=1, source_target_pairs={{0,6},{2,4},{4,2},{6,0},{8,14},{10,12},{12,10},{14,8},{1,7},{3,5},... | collective-permute-start | bytes 294920 | tf_op jit(solution)/shard_map/ppermute | solution.py:48
  67.4 3.3 %collective-permute-done.14.first = bf16[256,512]{1,0:T(8,128)(2,1)S(1)} collective-permute-done((bf16[256,512]{1,0:T(8,128)(2,1)S(1)}, bf16[256,512]{1,0:T(8,128)(2,1)S(1)}, u32[]{:S(2)}, u32[]{:S(2)}) %collective-permute-start.14) | collective-permute-done | bytes 262176 | tf_op jit(solution)/shard_map/ppermute | solution.py:57
  71.3 0.9 %latent_gradient.1 = (bf16[512,256]{1,0:T(8,128)(2,1)}, f32[16,128]{1,0:T(8,128)S(1)}) custom-call(f32[512,256]{1,0:T(8,128)S(1)} %get-tuple-element.55.base, bf16[256,512]{1,0:T(8,128)(2,1)S(1)} %collective-permute-done.14.first, bf16[256,512]{1,0:T(8,128)(2,1)S(1)} %collective-permute-done.15.second, bf16[256,512]{1,0:T(8,128)(2,1)S(1)} %collective-permute-done.16.pair), custom_call_target="tpu_custom_call" | custom-call | flops 524288 | bytes 1572864 | tf_op jit(solution)/shard_map/latent_gradient/pallas_call | solution.py:68
  72.8 0.9 %collective-permute-done.19.second = bf16[192,256]{1,0:T(8,128)(2,1)S(1)} collective-permute-done((bf16[192,256]{1,0:T(8,128)(2,1)S(1)}, bf16[192,256]{1,0:T(8,128)(2,1)S(1)}, u32[]{:S(2)}, u32[]{:S(2)}) %collective-permute-start.19) | collective-permute-done | bytes 98336 | tf_op jit(solution)/shard_map/ppermute | solution.py:48
  73.7 1.6 %collective-permute-done.18.first = bf16[192,256]{1,0:T(8,128)(2,1)S(1)} collective-permute-done((bf16[192,256]{1,0:T(8,128)(2,1)S(1)}, bf16[192,256]{1,0:T(8,128)(2,1)S(1)}, u32[]{:S(2)}, u32[]{:S(2)}) %collective-permute-start.18) | collective-permute-done | bytes 98336 | tf_op jit(solution)/shard_map/ppermute | solution.py:48
  75.4 1.7 %collective-permute-done.21.other = bf16[768,256]{1,0:T(8,128)(2,1)S(1)} collective-permute-done((bf16[768,256]{1,0:T(8,128)(2,1)S(1)}, bf16[768,256]{1,0:T(8,128)(2,1)S(1)}, u32[]{:S(2)}, u32[]{:S(2)}) %collective-permute-start.21) | collective-permute-done | bytes 393248 | tf_op jit(solution)/shard_map/ppermute | solution.py:48
  77.1 1.2 %weight_gradients.1 = (f32[256,256]{1,0:T(8,128)}, f32[256,256]{1,0:T(8,128)}, f32[256,256]{1,0:T(8,128)}, f32[3,256,256]{2,1,0:T(8,128)}) custom-call(bf16[768,256]{1,0:T(8,128)(2,1)S(1)} %pieces.1.own, bf16[768,256]{1,0:T(8,128)(2,1)S(1)} %collective-permute-done.21.other), custom_call_target="tpu_custom_call" | custom-call | flops 393216 | bytes 2359296 | tf_op jit(solution)/shard_map/weight_gradients/pallas_call | solution.py:68
  (51 shorter events, 9.2 us)
Async XLA Ops:
  0.6 8.1 %collective-permute-start.1 = (bf16[512,256]{1,0:T(8,128)(2,1)}, bf16[512,256]{1,0:T(8,128)(2,1)S(1)}, u32[]{:S(2)}, u32[]{:S(2)}) collective-permute-start(bf16[512,256]{1,0:T(8,128)(2,1)} %bitcast.7), channel_id=1, source_target_pairs={{4,8},{6,10},{8,4},{10,6},{5,9},{7,11},{9,5},{11,7},{20,24},{22,26... | collective-permute-start | bytes 786440 | tf_op jit(solution)/shard_map/ppermute | solution.py:57
  1.3 12.1 %collective-permute-start.2 = (bf16[512,256]{1,0:T(8,128)(2,1)}, bf16[512,256]{1,0:T(8,128)(2,1)S(1)}, u32[]{:S(2)}, u32[]{:S(2)}) collective-permute-start(bf16[512,256]{1,0:T(8,128)(2,1)} %bitcast.8), channel_id=1, source_target_pairs={{0,4},{2,6},{8,12},{10,14},{4,0},{6,2},{12,8},{14,10},{1,5},{3,7},... | collective-permute-start | bytes 786440 | tf_op jit(solution)/shard_map/ppermute | solution.py:57
  7.2 10.7 %collective-permute-start = (bf16[512,256]{1,0:T(8,128)(2,1)}, bf16[512,256]{1,0:T(8,128)(2,1)S(1)}, u32[]{:S(2)}, u32[]{:S(2)}) collective-permute-start(bf16[512,256]{1,0:T(8,128)(2,1)} %bitcast.9), channel_id=1, source_target_pairs={{0,2},{2,0},{4,6},{6,4},{8,10},{10,8},{12,14},{14,12},{1,3},{3,1},... | collective-permute-start | bytes 786440 | tf_op jit(solution)/shard_map/ppermute | solution.py:48
  8.7 8.3 %copy-start.2 = (bf16[1,512,256]{2,1,0:T(8,128)(2,1)S(1)}, bf16[1,512,256]{2,1,0:T(8,128)(2,1)}, u32[]{:S(2)}) copy-start(bf16[1,512,256]{2,1,0:T(8,128)(2,1)} %param.10) | copy-start | bytes 786436
  8.7 8.3 %copy-start.4 = (bf16[256,256]{1,0:T(8,128)(2,1)S(1)}, bf16[256,256]{1,0:T(8,128)(2,1)}, u32[]{:S(2)}) copy-start(bf16[256,256]{1,0:T(8,128)(2,1)} %outp.3) | copy-start | bytes 393220
  8.8 12.6 %collective-permute-start.4 = (bf16[576,256]{1,0:T(8,128)(2,1)S(1)}, bf16[576,256]{1,0:T(8,128)(2,1)S(1)}, u32[]{:S(2)}, u32[]{:S(2)}) collective-permute-start(bf16[576,256]{1,0:T(8,128)(2,1)S(1)} %pad_maximum_fusion), channel_id=1, source_target_pairs={{8,12},{10,14},{4,0},{6,2},{9,13},{11,15},{5,1},{7,3},{24,28},{26,... | collective-permute-start | bytes 884744 | tf_op jit(solution)/shard_map/ppermute | solution.py:57
  13.5 7.2 %collective-permute-start.3 = (bf16[512,256]{1,0:T(8,128)(2,1)S(1)}, bf16[512,256]{1,0:T(8,128)(2,1)S(1)}, u32[]{:S(2)}, u32[]{:S(2)}) collective-permute-start(bf16[512,256]{1,0:T(8,128)(2,1)S(1)} %broadcast_select_fusion), channel_id=1, source_target_pairs={{0,2},{2,0},{4,6},{6,4},{8,10},{10,8},{12,14},{14,12},{1,3},{3,1},... | collective-permute-start | bytes 786440 | tf_op jit(solution)/shard_map/ppermute | solution.py:48
  15.1 2.9 %collective-permute-start.5 = (bf16[512,256]{1,0:T(8,128)(2,1)S(1)}, bf16[512,256]{1,0:T(8,128)(2,1)S(1)}, u32[]{:S(2)}, u32[]{:S(2)}) collective-permute-start(bf16[512,256]{1,0:T(8,128)(2,1)S(1)} %collective-permute-done.2.first), channel_id=1, source_target_pairs={{4,8},{6,10},{8,4},{10,6},{5,9},{7,11},{9,5},{11,7},{20,24},{22,26... | collective-permute-start | bytes 786440 | tf_op jit(solution)/shard_map/ppermute | solution.py:57
  15.8 1.3 %collective-permute-start.6 = (bf16[64,256]{1,0:T(8,128)(2,1)S(1)}, bf16[64,256]{1,0:T(8,128)(2,1)S(1)}, u32[]{:S(2)}, u32[]{:S(2)}) collective-permute-start(bf16[64,256]{1,0:T(8,128)(2,1)S(1)} %select_bitcast_fusion), channel_id=1, source_target_pairs={{0,1},{1,0},{2,3},{3,2},{4,5},{5,4},{6,7},{7,6},{8,9},{9,8},{10,11... | collective-permute-start | bytes 98312 | tf_op jit(solution)/shard_map/ppermute | solution.py:48
  22.1 1.4 %collective-permute-start.7 = (bf16[2,128,256]{2,1,0:T(8,128)(2,1)S(1)}, bf16[2,128,256]{2,1,0:T(8,128)(2,1)S(1)}, u32[]{:S(2)}, u32[]{:S(2)}) collective-permute-start(bf16[2,128,256]{2,1,0:T(8,128)(2,1)S(1)} %get-tuple-element.44), channel_id=1, source_target_pairs={{0,1},{1,0},{2,3},{3,2},{4,5},{5,4},{6,7},{7,6},{8,9},{9,8},{10,11... | collective-permute-start | bytes 393224 | tf_op jit(solution)/shard_map/ppermute | solution.py:48
  39.0 2.0 %collective-permute-start.9 = (bf16[1024,256]{1,0:T(8,128)(2,1)S(1)}, bf16[1024,256]{1,0:T(8,128)(2,1)S(1)}, u32[]{:S(2)}, u32[]{:S(2)}) collective-permute-start(bf16[1024,256]{1,0:T(8,128)(2,1)S(1)} %get-tuple-element.58), channel_id=1, source_target_pairs={{0,1},{1,0},{2,3},{3,2},{4,5},{5,4},{6,7},{7,6},{8,9},{9,8},{10,11... | collective-permute-start | bytes 1572872 | tf_op jit(solution)/shard_map/ppermute | solution.py:48
  41.9 16.4 %collective-permute-start.10 = (bf16[352,512]{1,0:T(8,128)(2,1)S(1)}, bf16[352,512]{1,0:T(8,128)(2,1)S(1)}, u32[]{:S(2)}, u32[]{:S(2)}) collective-permute-start(bf16[352,512]{1,0:T(8,128)(2,1)S(1)} %get-tuple-element.59), channel_id=1, source_target_pairs={{0,2},{2,0},{4,6},{6,4},{8,10},{10,8},{12,14},{14,12},{1,3},{3,1},... | collective-permute-start | bytes 1081352 | tf_op jit(solution)/shard_map/ppermute | solution.py:48
  43.5 14.9 %collective-permute-start.11 = (bf16[352,512]{1,0:T(8,128)(2,1)S(1)}, bf16[352,512]{1,0:T(8,128)(2,1)S(1)}, u32[]{:S(2)}, u32[]{:S(2)}) collective-permute-start(bf16[352,512]{1,0:T(8,128)(2,1)S(1)} %get-tuple-element.60), channel_id=1, source_target_pairs={{0,4},{2,6},{8,12},{10,14},{4,0},{6,2},{12,8},{14,10},{1,5},{3,7},... | collective-permute-start | bytes 1081352 | tf_op jit(solution)/shard_map/ppermute | solution.py:57
  46.9 11.5 %collective-permute-start.13 = (bf16[96,512]{1,0:T(8,128)(2,1)S(1)}, bf16[96,512]{1,0:T(8,128)(2,1)S(1)}, u32[]{:S(2)}, u32[]{:S(2)}) collective-permute-start(bf16[96,512]{1,0:T(8,128)(2,1)S(1)} %get-tuple-element.62), channel_id=1, source_target_pairs={{0,6},{2,4},{4,2},{6,0},{8,14},{10,12},{12,10},{14,8},{1,7},{3,5},... | collective-permute-start | bytes 294920 | tf_op jit(solution)/shard_map/ppermute | solution.py:48
  47.7 10.6 %collective-permute-start.12 = (bf16[256,512]{1,0:T(8,128)(2,1)S(1)}, bf16[256,512]{1,0:T(8,128)(2,1)S(1)}, u32[]{:S(2)}, u32[]{:S(2)}) collective-permute-start(bf16[256,512]{1,0:T(8,128)(2,1)S(1)} %get-tuple-element.61), channel_id=1, source_target_pairs={{4,8},{6,10},{8,4},{10,6},{5,9},{7,11},{9,5},{11,7},{20,24},{22,26... | collective-permute-start | bytes 786440 | tf_op jit(solution)/shard_map/ppermute | solution.py:57
  48.4 1.3 %collective-permute-start.8 = (bf16[64,256]{1,0:T(8,128)(2,1)S(1)}, bf16[64,256]{1,0:T(8,128)(2,1)S(1)}, u32[]{:S(2)}, u32[]{:S(2)}) collective-permute-start(bf16[64,256]{1,0:T(8,128)(2,1)S(1)} %slice_select_fusion), channel_id=1, source_target_pairs={{0,1},{1,0},{2,3},{3,2},{4,5},{5,4},{6,7},{7,6},{8,9},{9,8},{10,11... | collective-permute-start | bytes 98312 | tf_op jit(solution)/shard_map/ppermute | solution.py:48
  58.6 6.4 %collective-permute-start.17 = (bf16[192,256]{1,0:T(8,128)(2,1)S(1)}, bf16[192,256]{1,0:T(8,128)(2,1)S(1)}, u32[]{:S(2)}, u32[]{:S(2)}) collective-permute-start(bf16[192,256]{1,0:T(8,128)(2,1)S(1)} %get-tuple-element.72), channel_id=1, source_target_pairs={{0,8},{2,10},{4,12},{6,14},{8,0},{10,2},{12,4},{14,6},{1,9},{3,11}... | collective-permute-start | bytes 294920 | tf_op jit(solution)/shard_map/ppermute | solution.py:48
  61.4 9.3 %collective-permute-start.14 = (bf16[256,512]{1,0:T(8,128)(2,1)S(1)}, bf16[256,512]{1,0:T(8,128)(2,1)S(1)}, u32[]{:S(2)}, u32[]{:S(2)}) collective-permute-start(bf16[256,512]{1,0:T(8,128)(2,1)S(1)} %get-tuple-element.68), channel_id=1, source_target_pairs={{0,4},{2,6},{8,12},{10,14},{4,0},{6,2},{12,8},{14,10},{1,5},{3,7},... | collective-permute-start | bytes 786440 | tf_op jit(solution)/shard_map/ppermute | solution.py:57
  61.7 9.6 %collective-permute-start.15 = (bf16[256,512]{1,0:T(8,128)(2,1)S(1)}, bf16[256,512]{1,0:T(8,128)(2,1)S(1)}, u32[]{:S(2)}, u32[]{:S(2)}) collective-permute-start(bf16[256,512]{1,0:T(8,128)(2,1)S(1)} %get-tuple-element.69), channel_id=1, source_target_pairs={{4,8},{6,10},{8,4},{10,6},{5,9},{7,11},{9,5},{11,7},{20,24},{22,26... | collective-permute-start | bytes 786440 | tf_op jit(solution)/shard_map/ppermute | solution.py:57
  62.4 8.9 %collective-permute-start.16 = (bf16[256,512]{1,0:T(8,128)(2,1)S(1)}, bf16[256,512]{1,0:T(8,128)(2,1)S(1)}, u32[]{:S(2)}, u32[]{:S(2)}) collective-permute-start(bf16[256,512]{1,0:T(8,128)(2,1)S(1)} %get-tuple-element.70), channel_id=1, source_target_pairs={{0,2},{2,0},{4,6},{6,4},{8,10},{10,8},{12,14},{14,12},{1,3},{3,1},... | collective-permute-start | bytes 786440 | tf_op jit(solution)/shard_map/ppermute | solution.py:48
  65.0 7.7 %collective-permute-start.20 = (bf16[192,256]{1,0:T(8,128)(2,1)S(1)}, bf16[192,256]{1,0:T(8,128)(2,1)S(1)}, u32[]{:S(2)}, u32[]{:S(2)}) collective-permute-start(bf16[192,256]{1,0:T(8,128)(2,1)S(1)} %add_convert_fusion.own), channel_id=1, source_target_pairs={{0,6},{2,4},{4,2},{6,0},{8,14},{10,12},{12,10},{14,8},{1,7},{3,5},... | collective-permute-start | bytes 294920 | tf_op jit(solution)/shard_map/ppermute | solution.py:48
  67.4 6.3 %collective-permute-start.19 = (bf16[192,256]{1,0:T(8,128)(2,1)S(1)}, bf16[192,256]{1,0:T(8,128)(2,1)S(1)}, u32[]{:S(2)}, u32[]{:S(2)}) collective-permute-start(bf16[192,256]{1,0:T(8,128)(2,1)S(1)} %add_convert_fusion.own), channel_id=1, source_target_pairs={{0,4},{2,6},{4,0},{6,2},{8,12},{10,14},{12,8},{14,10},{1,5},{3,7},... | collective-permute-start | bytes 294920 | tf_op jit(solution)/shard_map/ppermute | solution.py:48
  70.7 4.6 %collective-permute-start.18 = (bf16[192,256]{1,0:T(8,128)(2,1)S(1)}, bf16[192,256]{1,0:T(8,128)(2,1)S(1)}, u32[]{:S(2)}, u32[]{:S(2)}) collective-permute-start(bf16[192,256]{1,0:T(8,128)(2,1)S(1)} %add_convert_fusion.own), channel_id=1, source_target_pairs={{0,2},{2,0},{4,6},{6,4},{8,10},{10,8},{12,14},{14,12},{1,3},{3,1},... | collective-permute-start | bytes 294920 | tf_op jit(solution)/shard_map/ppermute | solution.py:48
  75.3 1.8 %collective-permute-start.21 = (bf16[768,256]{1,0:T(8,128)(2,1)S(1)}, bf16[768,256]{1,0:T(8,128)(2,1)S(1)}, u32[]{:S(2)}, u32[]{:S(2)}) collective-permute-start(bf16[768,256]{1,0:T(8,128)(2,1)S(1)} %pieces.1.own), channel_id=1, source_target_pairs={{0,1},{1,0},{2,3},{3,2},{4,5},{5,4},{6,7},{7,6},{8,9},{9,8},{10,11... | collective-permute-start | bytes 1179656 | tf_op jit(solution)/shard_map/ppermute | solution.py:48
  (6 other events, 28.0 us)

commit v6 on v5

--- a/solution.py
+++ b/solution.py
@@ -337,13 +337,12 @@
 
 
 def relay_kernel(
-    across, first, second, third, first_keep, second_keep, own, pair, _,
-    first_out, second_out, pair_out, own_out,
+    across, first, second, third, first_keep, second_keep, own, _,
+    first_out, second_out, own_out,
 ):
     frame_id = lax.axis_index("frame")
     width = first_keep.shape[0]
     packed = third.shape[0]
-    pair_out[...] = pair[...]
     crossing = across[:width].astype(F32)
     none = jnp.zeros_like(crossing)
     with_first = (frame_id & 1) == ((frame_id >> 1) & 1)
@@ -366,6 +365,10 @@
     returned = first[...].astype(F32) + second[...].astype(F32) + pair[...].astype(F32)
     grad_out[...] = (base[...] + returned.T).astype(BF16)
     last_out[...] = returned[:16, :128]
+
+
+def total_kernel(own, other, _, own_out):
+    own_out[...] = (own[...].astype(F32) + other[...].astype(F32)).astype(BF16)
 
 
 def gather_kernel(own, first, second, third, _, pieces_out):
@@ -524,15 +527,14 @@
         moved=count * width * 8,
         name="context",
     )
-    back_first, back_second, back_pair, own = whole_call(
+    back_first, back_second, own = whole_call(
         relay_kernel,
         [
             ((width, count), BF16),
             ((width, count), BF16),
-            ((width, count), BF16),
             ((piece, width), BF16),
         ],
-        (across, first, second, third, first_keep, second_keep, own, pair, gain),
+        (across, first, second, third, first_keep, second_keep, own, gain),
         flops=count * width * 4,
         moved=count * width * 16,
         name="relay",
@@ -541,7 +543,7 @@
     other = swapped(own, "frame", mask)
     back_first = along(back_first, 0)
     back_second = along(back_second, 2)
-    back_pair = swapped(back_pair, "frame", 1)
+    back_pair = swapped(pair, "frame", 1)
     while 2 * mask < frames:
         mask *= 2
         own = (own.astype(F32) + other.astype(F32)).astype(BF16)

time: 78.6 us -> 77.2 us (0.982)
  waiting for transfers between devices: 28.5 us -> 27.4 us
where the time goes in v6:
time: 77.2 us; the launch traced here: 77 us
  waiting for transfers between devices  27.4 us (35%)
  starting transfers between devices  25.9 us (34%)
  Pallas kernels  21.4 us (28%)
  between operations  2.18 us (3%)
    pallas_call x9, Pallas kernels, whole_call(): pl.pallas_call(body, out_shape=[jax.ShapeDtypeStruct(shape, dtype) for sh...  21.4 us
    ppermute x14, waiting for transfers between devices, swapped(): return lax.ppermute(array, axis, pairs)  20.9 us
    ppermute x8, starting transfers between devices, along(): return lax.ppermute(array, 'frame', pairs)  13.6 us
    ppermute x14, starting transfers between devices, swapped(): return lax.ppermute(array, axis, pairs)  12.3 us
    ppermute x8, waiting for transfers between devices, along(): return lax.ppermute(array, 'frame', pairs)  6.51 us
  transfers between devices with their start and end apart: 22, of which 14 were waited for; matrix products, arithmetic and copies ran while one was open for 0% of the time, Pallas kernels for 4%

profile of v6, /device:TPU:0, one launch (start us, length us, event | category | flops | bytes accessed | tf_op | source)
XLA Modules:
  0.0 77.0 jit_solution(6701613113854621779)
XLA Ops:
  1.3 5.9 %collective-permute-start.2 = (bf16[512,256]{1,0:T(8,128)(2,1)}, bf16[512,256]{1,0:T(8,128)(2,1)S(1)}, u32[]{:S(2)}, u32[]{:S(2)}) collective-permute-start(bf16[512,256]{1,0:T(8,128)(2,1)} %bitcast.8), channel_id=1, source_target_pairs={{0,4},{2,6},{8,12},{10,14},{4,0},{6,2},{12,8},{14,10},{1,5},{3,7},... | collective-permute-start | bytes 786440 | tf_op jit(solution)/shard_map/ppermute | solution.py:57
  7.2 1.5 %collective-permute-start = (bf16[512,256]{1,0:T(8,128)(2,1)}, bf16[512,256]{1,0:T(8,128)(2,1)S(1)}, u32[]{:S(2)}, u32[]{:S(2)}) collective-permute-start(bf16[512,256]{1,0:T(8,128)(2,1)} %bitcast.9), channel_id=1, source_target_pairs={{0,2},{2,0},{4,6},{6,4},{8,10},{10,8},{12,14},{14,12},{1,3},{3,1},... | collective-permute-start | bytes 786440 | tf_op jit(solution)/shard_map/ppermute | solution.py:48
  8.8 1.4 %collective-permute-start.4 = (bf16[576,256]{1,0:T(8,128)(2,1)S(1)}, bf16[576,256]{1,0:T(8,128)(2,1)S(1)}, u32[]{:S(2)}, u32[]{:S(2)}) collective-permute-start(bf16[576,256]{1,0:T(8,128)(2,1)S(1)} %pad_maximum_fusion), channel_id=1, source_target_pairs={{8,12},{10,14},{4,0},{6,2},{9,13},{11,15},{5,1},{7,3},{24,28},{26,... | collective-permute-start | bytes 884744 | tf_op jit(solution)/shard_map/ppermute | solution.py:57
  10.2 3.2 %collective-permute-done.2.first = bf16[512,256]{1,0:T(8,128)(2,1)S(1)} collective-permute-done((bf16[512,256]{1,0:T(8,128)(2,1)}, bf16[512,256]{1,0:T(8,128)(2,1)S(1)}, u32[]{:S(2)}, u32[]{:S(2)}) %collective-permute-start.2) | collective-permute-done | bytes 262176 | tf_op jit(solution)/shard_map/ppermute | solution.py:57
  13.5 1.6 %collective-permute-start.3 = (bf16[512,256]{1,0:T(8,128)(2,1)S(1)}, bf16[512,256]{1,0:T(8,128)(2,1)S(1)}, u32[]{:S(2)}, u32[]{:S(2)}) collective-permute-start(bf16[512,256]{1,0:T(8,128)(2,1)S(1)} %broadcast_select_fusion), channel_id=1, source_target_pairs={{0,2},{2,0},{4,6},{6,4},{8,10},{10,8},{12,14},{14,12},{1,3},{3,1},... | collective-permute-start | bytes 786440 | tf_op jit(solution)/shard_map/ppermute | solution.py:48
  17.1 0.8 %gradient_path.1 = (f32[512,256]{1,0:T(8,128)S(1)}, bf16[512,256]{1,0:T(8,128)(2,1)S(1)}, bf16[640,256]{1,0:T(8,128)(2,1)S(1)}, bf16[512,256]{1,0:T(8,128)(2,1)S...) custom-call(s32[1]{0:T(128)S(6)} %copy.17.level, ...), custom_call_target="tpu_custom_call" | custom-call | flops 335544320 | bytes 3145728 | tf_op jit(solution)/shard_map/gradient_path/pallas_call | solution.py:68
  17.9 2.8 %collective-permute-done.3.cross = bf16[512,256]{1,0:T(8,128)(2,1)S(1)} collective-permute-done((bf16[512,256]{1,0:T(8,128)(2,1)S(1)}, bf16[512,256]{1,0:T(8,128)(2,1)S(1)}, u32[]{:S(2)}, u32[]{:S(2)}) %collective-permute-start.3) | collective-permute-done | bytes 262176 | tf_op jit(solution)/shard_map/ppermute | solution.py:48
  23.5 15.5 %attention.1 = (f32[2,256,512]{2,1,0:T(8,128)S(1)}, bf16[1024,256]{1,0:T(8,128)(2,1)S(1)}, f32[768,256]{1,0:T(8,128)S(1)}, bf16[512,256]{1,0:T(8,128)(2,1)S(1)},...) custom-call(s32[1]{0:T(128)S(6)} %copy.16.windows, bf16[2,512,256]{2,1,0:T(8,128)(2,1)S(1)} %get-tuple-element.42.slots, ...), custom_call_target="tpu_custom_call" | custom-call | flops 9663676416 | bytes 7864320 | tf_op jit(solution)/shard_map/attention/pallas_call | solution.py:68
  39.2 1.7 %collective-permute-done.9.got = bf16[1024,256]{1,0:T(8,128)(2,1)S(1)} collective-permute-done((bf16[1024,256]{1,0:T(8,128)(2,1)S(1)}, bf16[1024,256]{1,0:T(8,128)(2,1)S(1)}, u32[]{:S(2)}, u32[]{:S(2)}) %collective-permute-start.9) | collective-permute-done | bytes 524320 | tf_op jit(solution)/shard_map/ppermute | solution.py:48
  41.0 0.9 %spread.1 = (bf16[256,512]{1,0:T(8,128)(2,1)S(1)}, bf16[352,512]{1,0:T(8,128)(2,1)S(1)}, bf16[352,512]{1,0:T(8,128)(2,1)S(1)}, bf16[256,512]{1,0:T(8,128)(2,1)S(...) custom-call(s32[1,2]{1,0:T(1,128)S(1)} %copy-done.6, ...), custom_call_target="tpu_custom_call" | custom-call | flops 1572864 | bytes 3932160 | tf_op jit(solution)/shard_map/spread/pallas_call | solution.py:68
  41.9 1.5 %collective-permute-start.10 = (bf16[352,512]{1,0:T(8,128)(2,1)S(1)}, bf16[352,512]{1,0:T(8,128)(2,1)S(1)}, u32[]{:S(2)}, u32[]{:S(2)}) collective-permute-start(bf16[352,512]{1,0:T(8,128)(2,1)S(1)} %get-tuple-element.58), channel_id=1, source_target_pairs={{0,2},{2,0},{4,6},{6,4},{8,10},{10,8},{12,14},{14,12},{1,3},{3,1},... | collective-permute-start | bytes 1081352 | tf_op jit(solution)/shard_map/ppermute | solution.py:48
  43.5 3.4 %collective-permute-start.11 = (bf16[352,512]{1,0:T(8,128)(2,1)S(1)}, bf16[352,512]{1,0:T(8,128)(2,1)S(1)}, u32[]{:S(2)}, u32[]{:S(2)}) collective-permute-start(bf16[352,512]{1,0:T(8,128)(2,1)S(1)} %get-tuple-element.59), channel_id=1, source_target_pairs={{0,4},{2,6},{8,12},{10,14},{4,0},{6,2},{12,8},{14,10},{1,5},{3,7},... | collective-permute-start | bytes 1081352 | tf_op jit(solution)/shard_map/ppermute | solution.py:57
  46.8 1.0 %collective-permute-start.13 = (bf16[96,512]{1,0:T(8,128)(2,1)S(1)}, bf16[96,512]{1,0:T(8,128)(2,1)S(1)}, u32[]{:S(2)}, u32[]{:S(2)}) collective-permute-start(bf16[96,512]{1,0:T(8,128)(2,1)S(1)} %get-tuple-element.61), channel_id=1, source_target_pairs={{0,6},{2,4},{4,2},{6,0},{8,14},{10,12},{12,10},{14,8},{1,7},{3,5},... | collective-permute-start | bytes 294920 | tf_op jit(solution)/shard_map/ppermute | solution.py:48
  48.5 1.2 %collective-permute-done.8.halo = bf16[64,256]{1,0:T(8,128)(2,1)S(1)} collective-permute-done((bf16[64,256]{1,0:T(8,128)(2,1)S(1)}, bf16[64,256]{1,0:T(8,128)(2,1)S(1)}, u32[]{:S(2)}, u32[]{:S(2)}) %collective-permute-start.8) | collective-permute-done | bytes 32800 | tf_op jit(solution)/shard_map/ppermute | solution.py:48
  49.7 1.1 %context.1 = (bf16[512,256]{1,0:T(8,128)(2,1)}, f32[1,256]{1,0:T(1,128)S(1)}) custom-call(bf16[512,256]{1,0:T(8,128)(2,1)S(1)} %get-tuple-element.51.hidden, bf16[64,256]{1,0:T(8,128)(2,1)S(1)} %collective-permute-done.8.halo, f32[512,256]{1,0:T(8,128)S(1)} %get-tuple-element.52.residual, f32[1,256]{1,0:T(1,128)S(1)} %get-tuple-element.41._.gain, ...), custom_call_target="tpu_custom_call" | custom-call | flops 201326592 | bytes 1048576 | tf_op jit(solution)/shard_map/context/pallas_call | solution.py:68
  50.8 7.5 %collective-permute-done.13.third = bf16[96,512]{1,0:T(8,128)(2,1)S(1)} collective-permute-done((bf16[96,512]{1,0:T(8,128)(2,1)S(1)}, bf16[96,512]{1,0:T(8,128)(2,1)S(1)}, u32[]{:S(2)}, u32[]{:S(2)}) %collective-permute-start.13) | collective-permute-done | bytes 98336 | tf_op jit(solution)/shard_map/ppermute | solution.py:48
  58.6 2.8 %collective-permute-start.17 = (bf16[192,256]{1,0:T(8,128)(2,1)S(1)}, bf16[192,256]{1,0:T(8,128)(2,1)S(1)}, u32[]{:S(2)}, u32[]{:S(2)}) collective-permute-start(bf16[192,256]{1,0:T(8,128)(2,1)S(1)} %get-tuple-element.70), channel_id=1, source_target_pairs={{0,8},{2,10},{4,12},{6,14},{8,0},{10,2},{12,4},{14,6},{1,9},{3,11}... | collective-permute-start | bytes 294920 | tf_op jit(solution)/shard_map/ppermute | solution.py:48
  62.9 2.1 %collective-permute-done.17 = bf16[192,256]{1,0:T(8,128)(2,1)S(1)} collective-permute-done((bf16[192,256]{1,0:T(8,128)(2,1)S(1)}, bf16[192,256]{1,0:T(8,128)(2,1)S(1)}, u32[]{:S(2)}, u32[]{:S(2)}) %collective-permute-start.17) | collective-permute-done | bytes 98336 | tf_op jit(solution)/shard_map/ppermute | solution.py:48
  65.0 2.3 %collective-permute-start.20 = (bf16[192,256]{1,0:T(8,128)(2,1)S(1)}, bf16[192,256]{1,0:T(8,128)(2,1)S(1)}, u32[]{:S(2)}, u32[]{:S(2)}) collective-permute-start(bf16[192,256]{1,0:T(8,128)(2,1)S(1)} %add_convert_fusion.own), channel_id=1, source_target_pairs={{0,6},{2,4},{4,2},{6,0},{8,14},{10,12},{12,10},{14,8},{1,7},{3,5},... | collective-permute-start | bytes 294920 | tf_op jit(solution)/shard_map/ppermute | solution.py:48
  68.6 2.6 %collective-permute-done.14.first = bf16[256,512]{1,0:T(8,128)(2,1)S(1)} collective-permute-done((bf16[256,512]{1,0:T(8,128)(2,1)S(1)}, bf16[256,512]{1,0:T(8,128)(2,1)S(1)}, u32[]{:S(2)}, u32[]{:S(2)}) %collective-permute-start.14) | collective-permute-done | bytes 262176 | tf_op jit(solution)/shard_map/ppermute | solution.py:57
  71.2 0.9 %latent_gradient.1 = (bf16[512,256]{1,0:T(8,128)(2,1)}, f32[16,128]{1,0:T(8,128)S(1)}) custom-call(f32[512,256]{1,0:T(8,128)S(1)} %get-tuple-element.54.base, bf16[256,512]{1,0:T(8,128)(2,1)S(1)} %collective-permute-done.14.first, bf16[256,512]{1,0:T(8,128)(2,1)S(1)} %collective-permute-done.15.second, bf16[256,512]{1,0:T(8,128)(2,1)S(1)} %collective-permute-done.16.pair), custom_call_target="tpu_custom_call" | custom-call | flops 524288 | bytes 1572864 | tf_op jit(solution)/shard_map/latent_gradient/pallas_call | solution.py:68
  72.1 1.4 %collective-permute-done.20.third = bf16[192,256]{1,0:T(8,128)(2,1)S(1)} collective-permute-done((bf16[192,256]{1,0:T(8,128)(2,1)S(1)}, bf16[192,256]{1,0:T(8,128)(2,1)S(1)}, u32[]{:S(2)}, u32[]{:S(2)}) %collective-permute-start.20) | collective-permute-done | bytes 98336 | tf_op jit(solution)/shard_map/ppermute | solution.py:48
  74.1 1.7 %collective-permute-done.21.other = bf16[768,256]{1,0:T(8,128)(2,1)S(1)} collective-permute-done((bf16[768,256]{1,0:T(8,128)(2,1)S(1)}, bf16[768,256]{1,0:T(8,128)(2,1)S(1)}, u32[]{:S(2)}, u32[]{:S(2)}) %collective-permute-start.21) | collective-permute-done | bytes 393248 | tf_op jit(solution)/shard_map/ppermute | solution.py:48
  75.8 1.2 %weight_gradients.1 = (f32[256,256]{1,0:T(8,128)}, f32[256,256]{1,0:T(8,128)}, f32[256,256]{1,0:T(8,128)}, f32[3,256,256]{2,1,0:T(8,128)}) custom-call(bf16[768,256]{1,0:T(8,128)(2,1)S(1)} %pieces.1.own, bf16[768,256]{1,0:T(8,128)(2,1)S(1)} %collective-permute-done.21.other), custom_call_target="tpu_custom_call" | custom-call | flops 393216 | bytes 2359296 | tf_op jit(solution)/shard_map/weight_gradients/pallas_call | solution.py:68
  (51 shorter events, 8.8 us)
Async XLA Ops:
  0.6 8.1 %collective-permute-start.1 = (bf16[512,256]{1,0:T(8,128)(2,1)}, bf16[512,256]{1,0:T(8,128)(2,1)S(1)}, u32[]{:S(2)}, u32[]{:S(2)}) collective-permute-start(bf16[512,256]{1,0:T(8,128)(2,1)} %bitcast.7), channel_id=1, source_target_pairs={{4,8},{6,10},{8,4},{10,6},{5,9},{7,11},{9,5},{11,7},{20,24},{22,26... | collective-permute-start | bytes 786440 | tf_op jit(solution)/shard_map/ppermute | solution.py:57
  1.3 12.1 %collective-permute-start.2 = (bf16[512,256]{1,0:T(8,128)(2,1)}, bf16[512,256]{1,0:T(8,128)(2,1)S(1)}, u32[]{:S(2)}, u32[]{:S(2)}) collective-permute-start(bf16[512,256]{1,0:T(8,128)(2,1)} %bitcast.8), channel_id=1, source_target_pairs={{0,4},{2,6},{8,12},{10,14},{4,0},{6,2},{12,8},{14,10},{1,5},{3,7},... | collective-permute-start | bytes 786440 | tf_op jit(solution)/shard_map/ppermute | solution.py:57
  7.2 10.7 %collective-permute-start = (bf16[512,256]{1,0:T(8,128)(2,1)}, bf16[512,256]{1,0:T(8,128)(2,1)S(1)}, u32[]{:S(2)}, u32[]{:S(2)}) collective-permute-start(bf16[512,256]{1,0:T(8,128)(2,1)} %bitcast.9), channel_id=1, source_target_pairs={{0,2},{2,0},{4,6},{6,4},{8,10},{10,8},{12,14},{14,12},{1,3},{3,1},... | collective-permute-start | bytes 786440 | tf_op jit(solution)/shard_map/ppermute | solution.py:48
  8.7 8.3 %copy-start.2 = (bf16[1,512,256]{2,1,0:T(8,128)(2,1)S(1)}, bf16[1,512,256]{2,1,0:T(8,128)(2,1)}, u32[]{:S(2)}) copy-start(bf16[1,512,256]{2,1,0:T(8,128)(2,1)} %param.10) | copy-start | bytes 786436
  8.7 8.3 %copy-start.4 = (bf16[256,256]{1,0:T(8,128)(2,1)S(1)}, bf16[256,256]{1,0:T(8,128)(2,1)}, u32[]{:S(2)}) copy-start(bf16[256,256]{1,0:T(8,128)(2,1)} %outp.3) | copy-start | bytes 393220
  8.8 12.6 %collective-permute-start.4 = (bf16[576,256]{1,0:T(8,128)(2,1)S(1)}, bf16[576,256]{1,0:T(8,128)(2,1)S(1)}, u32[]{:S(2)}, u32[]{:S(2)}) collective-permute-start(bf16[576,256]{1,0:T(8,128)(2,1)S(1)} %pad_maximum_fusion), channel_id=1, source_target_pairs={{8,12},{10,14},{4,0},{6,2},{9,13},{11,15},{5,1},{7,3},{24,28},{26,... | collective-permute-start | bytes 884744 | tf_op jit(solution)/shard_map/ppermute | solution.py:57
  13.5 7.2 %collective-permute-start.3 = (bf16[512,256]{1,0:T(8,128)(2,1)S(1)}, bf16[512,256]{1,0:T(8,128)(2,1)S(1)}, u32[]{:S(2)}, u32[]{:S(2)}) collective-permute-start(bf16[512,256]{1,0:T(8,128)(2,1)S(1)} %broadcast_select_fusion), channel_id=1, source_target_pairs={{0,2},{2,0},{4,6},{6,4},{8,10},{10,8},{12,14},{14,12},{1,3},{3,1},... | collective-permute-start | bytes 786440 | tf_op jit(solution)/shard_map/ppermute | solution.py:48
  15.1 2.9 %collective-permute-start.5 = (bf16[512,256]{1,0:T(8,128)(2,1)S(1)}, bf16[512,256]{1,0:T(8,128)(2,1)S(1)}, u32[]{:S(2)}, u32[]{:S(2)}) collective-permute-start(bf16[512,256]{1,0:T(8,128)(2,1)S(1)} %collective-permute-done.2.first), channel_id=1, source_target_pairs={{4,8},{6,10},{8,4},{10,6},{5,9},{7,11},{9,5},{11,7},{20,24},{22,26... | collective-permute-start | bytes 786440 | tf_op jit(solution)/shard_map/ppermute | solution.py:57
  15.8 1.3 %collective-permute-start.6 = (bf16[64,256]{1,0:T(8,128)(2,1)S(1)}, bf16[64,256]{1,0:T(8,128)(2,1)S(1)}, u32[]{:S(2)}, u32[]{:S(2)}) collective-permute-start(bf16[64,256]{1,0:T(8,128)(2,1)S(1)} %select_bitcast_fusion), channel_id=1, source_target_pairs={{0,1},{1,0},{2,3},{3,2},{4,5},{5,4},{6,7},{7,6},{8,9},{9,8},{10,11... | collective-permute-start | bytes 98312 | tf_op jit(solution)/shard_map/ppermute | solution.py:48
  22.1 1.4 %collective-permute-start.7 = (bf16[2,128,256]{2,1,0:T(8,128)(2,1)S(1)}, bf16[2,128,256]{2,1,0:T(8,128)(2,1)S(1)}, u32[]{:S(2)}, u32[]{:S(2)}) collective-permute-start(bf16[2,128,256]{2,1,0:T(8,128)(2,1)S(1)} %get-tuple-element.43), channel_id=1, source_target_pairs={{0,1},{1,0},{2,3},{3,2},{4,5},{5,4},{6,7},{7,6},{8,9},{9,8},{10,11... | collective-permute-start | bytes 393224 | tf_op jit(solution)/shard_map/ppermute | solution.py:48
  39.0 2.0 %collective-permute-start.9 = (bf16[1024,256]{1,0:T(8,128)(2,1)S(1)}, bf16[1024,256]{1,0:T(8,128)(2,1)S(1)}, u32[]{:S(2)}, u32[]{:S(2)}) collective-permute-start(bf16[1024,256]{1,0:T(8,128)(2,1)S(1)} %get-tuple-element.57), channel_id=1, source_target_pairs={{0,1},{1,0},{2,3},{3,2},{4,5},{5,4},{6,7},{7,6},{8,9},{9,8},{10,11... | collective-permute-start | bytes 1572872 | tf_op jit(solution)/shard_map/ppermute | solution.py:48
  41.9 16.4 %collective-permute-start.10 = (bf16[352,512]{1,0:T(8,128)(2,1)S(1)}, bf16[352,512]{1,0:T(8,128)(2,1)S(1)}, u32[]{:S(2)}, u32[]{:S(2)}) collective-permute-start(bf16[352,512]{1,0:T(8,128)(2,1)S(1)} %get-tuple-element.58), channel_id=1, source_target_pairs={{0,2},{2,0},{4,6},{6,4},{8,10},{10,8},{12,14},{14,12},{1,3},{3,1},... | collective-permute-start | bytes 1081352 | tf_op jit(solution)/shard_map/ppermute | solution.py:48
  43.5 14.9 %collective-permute-start.11 = (bf16[352,512]{1,0:T(8,128)(2,1)S(1)}, bf16[352,512]{1,0:T(8,128)(2,1)S(1)}, u32[]{:S(2)}, u32[]{:S(2)}) collective-permute-start(bf16[352,512]{1,0:T(8,128)(2,1)S(1)} %get-tuple-element.59), channel_id=1, source_target_pairs={{0,4},{2,6},{8,12},{10,14},{4,0},{6,2},{12,8},{14,10},{1,5},{3,7},... | collective-permute-start | bytes 1081352 | tf_op jit(solution)/shard_map/ppermute | solution.py:57
  46.8 11.5 %collective-permute-start.13 = (bf16[96,512]{1,0:T(8,128)(2,1)S(1)}, bf16[96,512]{1,0:T(8,128)(2,1)S(1)}, u32[]{:S(2)}, u32[]{:S(2)}) collective-permute-start(bf16[96,512]{1,0:T(8,128)(2,1)S(1)} %get-tuple-element.61), channel_id=1, source_target_pairs={{0,6},{2,4},{4,2},{6,0},{8,14},{10,12},{12,10},{14,8},{1,7},{3,5},... | collective-permute-start | bytes 294920 | tf_op jit(solution)/shard_map/ppermute | solution.py:48
  47.8 10.6 %collective-permute-start.12 = (bf16[256,512]{1,0:T(8,128)(2,1)S(1)}, bf16[256,512]{1,0:T(8,128)(2,1)S(1)}, u32[]{:S(2)}, u32[]{:S(2)}) collective-permute-start(bf16[256,512]{1,0:T(8,128)(2,1)S(1)} %get-tuple-element.60), channel_id=1, source_target_pairs={{4,8},{6,10},{8,4},{10,6},{5,9},{7,11},{9,5},{11,7},{20,24},{22,26... | collective-permute-start | bytes 786440 | tf_op jit(solution)/shard_map/ppermute | solution.py:57
  48.5 1.3 %collective-permute-start.8 = (bf16[64,256]{1,0:T(8,128)(2,1)S(1)}, bf16[64,256]{1,0:T(8,128)(2,1)S(1)}, u32[]{:S(2)}, u32[]{:S(2)}) collective-permute-start(bf16[64,256]{1,0:T(8,128)(2,1)S(1)} %slice_select_fusion), channel_id=1, source_target_pairs={{0,1},{1,0},{2,3},{3,2},{4,5},{5,4},{6,7},{7,6},{8,9},{9,8},{10,11... | collective-permute-start | bytes 98312 | tf_op jit(solution)/shard_map/ppermute | solution.py:48
  58.6 6.4 %collective-permute-start.17 = (bf16[192,256]{1,0:T(8,128)(2,1)S(1)}, bf16[192,256]{1,0:T(8,128)(2,1)S(1)}, u32[]{:S(2)}, u32[]{:S(2)}) collective-permute-start(bf16[192,256]{1,0:T(8,128)(2,1)S(1)} %get-tuple-element.70), channel_id=1, source_target_pairs={{0,8},{2,10},{4,12},{6,14},{8,0},{10,2},{12,4},{14,6},{1,9},{3,11}... | collective-permute-start | bytes 294920 | tf_op jit(solution)/shard_map/ppermute | solution.py:48
  61.4 6.7 %collective-permute-start.16 = (bf16[256,512]{1,0:T(8,128)(2,1)S(1)}, bf16[256,512]{1,0:T(8,128)(2,1)S(1)}, u32[]{:S(2)}, u32[]{:S(2)}) collective-permute-start(bf16[256,512]{1,0:T(8,128)(2,1)S(1)} %get-tuple-element.68), channel_id=1, source_target_pairs={{0,2},{2,0},{4,6},{6,4},{8,10},{10,8},{12,14},{14,12},{1,3},{3,1},... | collective-permute-start | bytes 786440 | tf_op jit(solution)/shard_map/ppermute | solution.py:48
  61.9 9.2 %collective-permute-start.14 = (bf16[256,512]{1,0:T(8,128)(2,1)S(1)}, bf16[256,512]{1,0:T(8,128)(2,1)S(1)}, u32[]{:S(2)}, u32[]{:S(2)}) collective-permute-start(bf16[256,512]{1,0:T(8,128)(2,1)S(1)} %get-tuple-element.66), channel_id=1, source_target_pairs={{0,4},{2,6},{8,12},{10,14},{4,0},{6,2},{12,8},{14,10},{1,5},{3,7},... | collective-permute-start | bytes 786440 | tf_op jit(solution)/shard_map/ppermute | solution.py:57
  62.2 9.0 %collective-permute-start.15 = (bf16[256,512]{1,0:T(8,128)(2,1)S(1)}, bf16[256,512]{1,0:T(8,128)(2,1)S(1)}, u32[]{:S(2)}, u32[]{:S(2)}) collective-permute-start(bf16[256,512]{1,0:T(8,128)(2,1)S(1)} %get-tuple-element.67), channel_id=1, source_target_pairs={{4,8},{6,10},{8,4},{10,6},{5,9},{7,11},{9,5},{11,7},{20,24},{22,26... | collective-permute-start | bytes 786440 | tf_op jit(solution)/shard_map/ppermute | solution.py:57
  65.0 8.4 %collective-permute-start.20 = (bf16[192,256]{1,0:T(8,128)(2,1)S(1)}, bf16[192,256]{1,0:T(8,128)(2,1)S(1)}, u32[]{:S(2)}, u32[]{:S(2)}) collective-permute-start(bf16[192,256]{1,0:T(8,128)(2,1)S(1)} %add_convert_fusion.own), channel_id=1, source_target_pairs={{0,6},{2,4},{4,2},{6,0},{8,14},{10,12},{12,10},{14,8},{1,7},{3,5},... | collective-permute-start | bytes 294920 | tf_op jit(solution)/shard_map/ppermute | solution.py:48
  67.4 6.6 %collective-permute-start.19 = (bf16[192,256]{1,0:T(8,128)(2,1)S(1)}, bf16[192,256]{1,0:T(8,128)(2,1)S(1)}, u32[]{:S(2)}, u32[]{:S(2)}) collective-permute-start(bf16[192,256]{1,0:T(8,128)(2,1)S(1)} %add_convert_fusion.own), channel_id=1, source_target_pairs={{0,4},{2,6},{4,0},{6,2},{8,12},{10,14},{12,8},{14,10},{1,5},{3,7},... | collective-permute-start | bytes 294920 | tf_op jit(solution)/shard_map/ppermute | solution.py:48
  68.0 5.9 %collective-permute-start.18 = (bf16[192,256]{1,0:T(8,128)(2,1)S(1)}, bf16[192,256]{1,0:T(8,128)(2,1)S(1)}, u32[]{:S(2)}, u32[]{:S(2)}) collective-permute-start(bf16[192,256]{1,0:T(8,128)(2,1)S(1)} %add_convert_fusion.own), channel_id=1, source_target_pairs={{0,2},{2,0},{4,6},{6,4},{8,10},{10,8},{12,14},{14,12},{1,3},{3,1},... | collective-permute-start | bytes 294920 | tf_op jit(solution)/shard_map/ppermute | solution.py:48
  74.0 1.8 %collective-permute-start.21 = (bf16[768,256]{1,0:T(8,128)(2,1)S(1)}, bf16[768,256]{1,0:T(8,128)(2,1)S(1)}, u32[]{:S(2)}, u32[]{:S(2)}) collective-permute-start(bf16[768,256]{1,0:T(8,128)(2,1)S(1)} %pieces.1.own), channel_id=1, source_target_pairs={{0,1},{1,0},{2,3},{3,2},{4,5},{5,4},{6,7},{7,6},{8,9},{9,8},{10,11... | collective-permute-start | bytes 1179656 | tf_op jit(solution)/shard_map/ppermute | solution.py:48
  (6 other events, 28.0 us)

commit v7 on v6

--- a/solution.py
+++ b/solution.py
@@ -48,12 +48,14 @@
     return lax.ppermute(array, axis, pairs)
 
 
-def along(array, parity, relayed=False):
+def along(array, parity, relayed=False, passed_on=False):
     devices = lax.axis_size("frame")
     pairs = [(i, i + 2) for i in range(devices) if (i & 2) == parity and i + 2 < devices]
     pairs = pairs + [(j, i) for i, j in pairs]
     if relayed:
         pairs = [(i, j) for i, j in pairs if 0 <= 2 * i - j < devices]
+    if passed_on:
+        pairs = [(i, j) for i, j in pairs if 0 <= 2 * j - i < devices]
     return lax.ppermute(array, "frame", pairs)
 
 
@@ -238,7 +240,8 @@
 
 def spread_kernel(
     refs, mid, keep, got,
-    pair_out, across_out, first_out, second_out, third_out, first_keep, second_keep, own_out,
+    pair_out, across_out, first_out, second_out, one_out, two_out, three_out,
+    first_keep, second_keep, own_out,
 ):
     frame_id, row_id = lax.axis_index("frame"), lax.axis_index("row")
     steps = [refs[0, 0] - frame_id, refs[0, 1] - frame_id]
@@ -290,10 +293,8 @@
         return keep[rows] + got[rows].astype(F32)
 
     own_out[...] = rows_of(me)
-    for mask, out, begin in ((1, across_out, width), (2, first_out, width), (3, third_out, 0)):
-        rows = rows_of(me ^ mask).astype(BF16)
-        out[begin:, :width] = rows[: piece // 2]
-        out[begin:, width:] = rows[piece // 2 :]
+    for mask, out in ((1, one_out), (2, two_out), (3, three_out)):
+        out[...] = rows_of(me ^ mask).astype(BF16)
 
 
 def coded_kernel(hidden, halo, residual, gain, taps, coded_out, gain_out, ext):
@@ -337,38 +338,25 @@
 
 
 def relay_kernel(
-    across, first, second, third, first_keep, second_keep, own, _,
-    first_out, second_out, own_out,
+    across, first, second, first_keep, second_keep, _,
+    first_out, second_out,
 ):
     frame_id = lax.axis_index("frame")
-    width = first_keep.shape[0]
-    packed = third.shape[0]
-    crossing = across[:width].astype(F32)
+    crossing = across[...].astype(F32)
     none = jnp.zeros_like(crossing)
     with_first = (frame_id & 1) == ((frame_id >> 1) & 1)
     first_out[...] = (
         first_keep[...] + second[...].astype(F32) + jnp.where(with_first, crossing, none)
     ).astype(BF16)
     second_out[...] = (
-        second_keep[...] + first[:width].astype(F32) + jnp.where(with_first, none, crossing)
+        second_keep[...] + first[...].astype(F32) + jnp.where(with_first, none, crossing)
     ).astype(BF16)
-    for part in range(2):
-        rows = slice(part * packed, (part + 1) * packed)
-        lanes = slice(part * width, (part + 1) * width)
-        own_out[rows] = (
-            (own[rows] + across[width:, lanes].astype(F32))
-            + (first[width:, lanes].astype(F32) + third[:, lanes].astype(F32))
-        ).astype(BF16)
 
 
 def final_kernel(base, first, second, pair, grad_out, last_out):
     returned = first[...].astype(F32) + second[...].astype(F32) + pair[...].astype(F32)
     grad_out[...] = (base[...] + returned.T).astype(BF16)
     last_out[...] = returned[:16, :128]
-
-
-def total_kernel(own, other, _, own_out):
-    own_out[...] = (own[...].astype(F32) + other[...].astype(F32)).astype(BF16)
 
 
 def gather_kernel(own, first, second, third, _, pieces_out):
@@ -494,15 +482,16 @@
     hidden_edge = jnp.where(row_id == 0, hidden[count - COLS :], hidden[:COLS])
     hidden_halo = swapped(hidden_edge, "row", 1)
     piece = half // 4
-    packed = piece // 2
-    pair, across, first, second, third, first_keep, second_keep, own = whole_call(
+    pair, across, first, second, one, two, three, first_keep, second_keep, own = whole_call(
         spread_kernel,
         [
             ((width, count), BF16),
-            ((width + packed, count), BF16),
-            ((width + packed, count), BF16),
             ((width, count), BF16),
-            ((packed, count), BF16),
+            ((width, count), BF16),
+            ((width, count), BF16),
+            ((piece, width), BF16),
+            ((piece, width), BF16),
+            ((piece, width), BF16),
             ((width, count), F32),
             ((width, count), F32),
             ((piece, width), F32),
@@ -513,10 +502,19 @@
         moved=count * width * 30,
         name="spread",
     )
-
-    third = swapped(third, "frame", 3)
+    one, two, three = swapped(one, "frame", 1), swapped(two, "frame", 2), swapped(three, "frame", 3)
+    own = (own + one.astype(F32)) + (two.astype(F32) + three.astype(F32))
+    own = own.astype(BF16)
+    mask = 4
+    other = swapped(own, "frame", mask)
+    while 2 * mask < frames:
+        mask *= 2
+        own = (own.astype(F32) + other.astype(F32)).astype(BF16)
+        other = swapped(own, "frame", mask)
+    own = (own.astype(F32) + other.astype(F32)).astype(BF16)
+
     across = swapped(across, "frame", 1)
-    first = along(first, 0)
+    first = along(first, 0, passed_on=True)
     second = along(second, 2)
     coded, gain = whole_call(
         coded_kernel,
@@ -527,28 +525,17 @@
         moved=count * width * 8,
         name="context",
     )
-    back_first, back_second, own = whole_call(
+    back_first, back_second = whole_call(
         relay_kernel,
-        [
-            ((width, count), BF16),
-            ((width, count), BF16),
-            ((piece, width), BF16),
-        ],
-        (across, first, second, third, first_keep, second_keep, own, gain),
+        [((width, count), BF16)] * 2,
+        (across, first, second, first_keep, second_keep, gain),
         flops=count * width * 4,
         moved=count * width * 16,
         name="relay",
     )
-    mask = 4
-    other = swapped(own, "frame", mask)
     back_first = along(back_first, 0)
     back_second = along(back_second, 2)
     back_pair = swapped(pair, "frame", 1)
-    while 2 * mask < frames:
-        mask *= 2
-        own = (own.astype(F32) + other.astype(F32)).astype(BF16)
-        other = swapped(own, "frame", mask)
-    own = (own.astype(F32) + other.astype(F32)).astype(BF16)
     grad_latents, last = whole_call(
         final_kernel,
         [((count, width), BF16), ((16, 128), F32)],

time: 77.2 us -> 76.6 us (level)
  waiting for transfers between devices: 27.4 us -> 15.7 us
  starting transfers between devices: 25.9 us -> 37 us
    ppermute x14 -> x16, waiting for transfers between devices: 20.9 us -> 10.5 us  [swapped(): return lax.ppermute(array, axis, pairs)]
    ppermute x14 -> x16, starting transfers between devices: 12.3 us -> 18 us  [swapped(): return lax.ppermute(array, axis, pairs)]
    ppermute x8, starting transfers between devices: 13.6 us -> 19 us  [along(): return lax.ppermute(array, 'frame', pairs)]
    ppermute x8, waiting for transfers between devices: 6.51 us -> 5.19 us  [along(): return lax.ppermute(array, 'frame', pairs)]
  transfers between devices with their start and end apart: 22 -> 24, of which waited for: 14 -> 11; matrix products, arithmetic and copies ran while one was open for 0% -> 0% of each run, Pallas kernels for 4% -> 4%
where the time goes in v7:
time: 76.6 us; the launch traced here: 76.4 us
  starting transfers between devices  37 us (48%)
  Pallas kernels  21.3 us (28%)
  waiting for transfers between devices  15.7 us (20%)
  between operations  2.21 us (3%)
    pallas_call x9, Pallas kernels, whole_call(): pl.pallas_call(body, out_shape=[jax.ShapeDtypeStruct(shape, dtype) for sh...  21.3 us
    ppermute x8, starting transfers between devices, along(): return lax.ppermute(array, 'frame', pairs)  19 us
    ppermute x16, starting transfers between devices, swapped(): return lax.ppermute(array, axis, pairs)  18 us
    ppermute x16, waiting for transfers between devices, swapped(): return lax.ppermute(array, axis, pairs)  10.5 us
    ppermute x8, waiting for transfers between devices, along(): return lax.ppermute(array, 'frame', pairs)  5.19 us
  transfers between devices with their start and end apart: 24, of which 11 were waited for; matrix products, arithmetic and copies ran while one was open for 0% of the time, Pallas kernels for 4%

profile of v7, /device:TPU:0, one launch (start us, length us, event | category | flops | bytes accessed | tf_op | source)
XLA Modules:
  0.0 76.4 jit_solution(6661149628577875907)
XLA Ops:
  1.3 5.9 %collective-permute-start.2 = (bf16[512,256]{1,0:T(8,128)(2,1)}, bf16[512,256]{1,0:T(8,128)(2,1)S(1)}, u32[]{:S(2)}, u32[]{:S(2)}) collective-permute-start(bf16[512,256]{1,0:T(8,128)(2,1)} %bitcast.8), channel_id=1, source_target_pairs={{0,4},{2,6},{8,12},{10,14},{4,0},{6,2},{12,8},{14,10},{1,5},{3,7},... | collective-permute-start | bytes 786440 | tf_op jit(solution)/shard_map/ppermute | solution.py:59
  7.2 1.5 %collective-permute-start = (bf16[512,256]{1,0:T(8,128)(2,1)}, bf16[512,256]{1,0:T(8,128)(2,1)S(1)}, u32[]{:S(2)}, u32[]{:S(2)}) collective-permute-start(bf16[512,256]{1,0:T(8,128)(2,1)} %bitcast.9), channel_id=1, source_target_pairs={{0,2},{2,0},{4,6},{6,4},{8,10},{10,8},{12,14},{14,12},{1,3},{3,1},... | collective-permute-start | bytes 786440 | tf_op jit(solution)/shard_map/ppermute | solution.py:48
  8.8 1.4 %collective-permute-start.4 = (bf16[576,256]{1,0:T(8,128)(2,1)S(1)}, bf16[576,256]{1,0:T(8,128)(2,1)S(1)}, u32[]{:S(2)}, u32[]{:S(2)}) collective-permute-start(bf16[576,256]{1,0:T(8,128)(2,1)S(1)} %pad_maximum_fusion), channel_id=1, source_target_pairs={{8,12},{10,14},{4,0},{6,2},{9,13},{11,15},{5,1},{7,3},{24,28},{26,... | collective-permute-start | bytes 884744 | tf_op jit(solution)/shard_map/ppermute | solution.py:59
  10.2 3.2 %collective-permute-done.2.first = bf16[512,256]{1,0:T(8,128)(2,1)S(1)} collective-permute-done((bf16[512,256]{1,0:T(8,128)(2,1)}, bf16[512,256]{1,0:T(8,128)(2,1)S(1)}, u32[]{:S(2)}, u32[]{:S(2)}) %collective-permute-start.2) | collective-permute-done | bytes 262176 | tf_op jit(solution)/shard_map/ppermute | solution.py:59
  13.5 1.6 %collective-permute-start.3 = (bf16[512,256]{1,0:T(8,128)(2,1)S(1)}, bf16[512,256]{1,0:T(8,128)(2,1)S(1)}, u32[]{:S(2)}, u32[]{:S(2)}) collective-permute-start(bf16[512,256]{1,0:T(8,128)(2,1)S(1)} %broadcast_select_fusion), channel_id=1, source_target_pairs={{0,2},{2,0},{4,6},{6,4},{8,10},{10,8},{12,14},{14,12},{1,3},{3,1},... | collective-permute-start | bytes 786440 | tf_op jit(solution)/shard_map/ppermute | solution.py:48
  17.9 2.8 %collective-permute-done.3.cross = bf16[512,256]{1,0:T(8,128)(2,1)S(1)} collective-permute-done((bf16[512,256]{1,0:T(8,128)(2,1)S(1)}, bf16[512,256]{1,0:T(8,128)(2,1)S(1)}, u32[]{:S(2)}, u32[]{:S(2)}) %collective-permute-start.3) | collective-permute-done | bytes 262176 | tf_op jit(solution)/shard_map/ppermute | solution.py:48
  23.5 15.5 %attention.1 = (f32[2,256,512]{2,1,0:T(8,128)S(1)}, bf16[1024,256]{1,0:T(8,128)(2,1)S(1)}, f32[768,256]{1,0:T(8,128)S(1)}, bf16[512,256]{1,0:T(8,128)(2,1)S(1)},...) custom-call(s32[1]{0:T(128)S(6)} %copy.16.windows, bf16[2,512,256]{2,1,0:T(8,128)(2,1)S(1)} %get-tuple-element.43.slots, ...), custom_call_target="tpu_custom_call" | custom-call | flops 9663676416 | bytes 7864320 | tf_op jit(solution)/shard_map/attention/pallas_call | solution.py:70
  39.2 1.7 %collective-permute-done.9.got = bf16[1024,256]{1,0:T(8,128)(2,1)S(1)} collective-permute-done((bf16[1024,256]{1,0:T(8,128)(2,1)S(1)}, bf16[1024,256]{1,0:T(8,128)(2,1)S(1)}, u32[]{:S(2)}, u32[]{:S(2)}) %collective-permute-start.9) | collective-permute-done | bytes 524320 | tf_op jit(solution)/shard_map/ppermute | solution.py:48
  41.0 0.9 %spread.1 = (bf16[256,512]{1,0:T(8,128)(2,1)S(1)}, bf16[256,512]{1,0:T(8,128)(2,1)S(1)}, bf16[256,512]{1,0:T(8,128)(2,1)S(1)}, bf16[256,512]{1,0:T(8,128)(2,1)S(...) custom-call(s32[1,2]{1,0:T(1,128)S(1)} %copy-done.6, ...), custom_call_target="tpu_custom_call" | custom-call | flops 1572864 | bytes 3932160 | tf_op jit(solution)/shard_map/spread/pallas_call | solution.py:70
  41.9 1.6 %collective-permute-start.16 = (bf16[192,256]{1,0:T(8,128)(2,1)S(1)}, bf16[192,256]{1,0:T(8,128)(2,1)S(1)}, u32[]{:S(2)}, u32[]{:S(2)}) collective-permute-start(bf16[192,256]{1,0:T(8,128)(2,1)S(1)} %get-tuple-element.70), channel_id=1, source_target_pairs={{0,2},{2,0},{4,6},{6,4},{8,10},{10,8},{12,14},{14,12},{1,3},{3,1},... | collective-permute-start | bytes 294920 | tf_op jit(solution)/shard_map/ppermute | solution.py:48
  43.4 3.4 %collective-permute-start.17 = (bf16[192,256]{1,0:T(8,128)(2,1)S(1)}, bf16[192,256]{1,0:T(8,128)(2,1)S(1)}, u32[]{:S(2)}, u32[]{:S(2)}) collective-permute-start(bf16[192,256]{1,0:T(8,128)(2,1)S(1)} %get-tuple-element.71), channel_id=1, source_target_pairs={{0,4},{2,6},{4,0},{6,2},{8,12},{10,14},{12,8},{14,10},{1,5},{3,7},... | collective-permute-start | bytes 294920 | tf_op jit(solution)/shard_map/ppermute | solution.py:48
  46.8 0.9 %collective-permute-start.18 = (bf16[192,256]{1,0:T(8,128)(2,1)S(1)}, bf16[192,256]{1,0:T(8,128)(2,1)S(1)}, u32[]{:S(2)}, u32[]{:S(2)}) collective-permute-start(bf16[192,256]{1,0:T(8,128)(2,1)S(1)} %get-tuple-element.72), channel_id=1, source_target_pairs={{0,6},{2,4},{4,2},{6,0},{8,14},{10,12},{12,10},{14,8},{1,7},{3,5},... | collective-permute-start | bytes 294920 | tf_op jit(solution)/shard_map/ppermute | solution.py:48
  48.3 3.9 %collective-permute-start.11 = (bf16[256,512]{1,0:T(8,128)(2,1)S(1)}, bf16[256,512]{1,0:T(8,128)(2,1)S(1)}, u32[]{:S(2)}, u32[]{:S(2)}) collective-permute-start(bf16[256,512]{1,0:T(8,128)(2,1)S(1)} %get-tuple-element.60), channel_id=1, source_target_pairs={{0,4},{2,6},{12,8},{14,10},{1,5},{3,7},{13,9},{15,11},{16,20},{18,... | collective-permute-start | bytes 786440 | tf_op jit(solution)/shard_map/ppermute | solution.py:59
  53.0 2.7 %collective-permute-start.19 = (bf16[192,256]{1,0:T(8,128)(2,1)S(1)}, bf16[192,256]{1,0:T(8,128)(2,1)S(1)}, u32[]{:S(2)}, u32[]{:S(2)}) collective-permute-start(bf16[192,256]{1,0:T(8,128)(2,1)S(1)} %add_convert_fusion.1), channel_id=1, source_target_pairs={{0,8},{2,10},{4,12},{6,14},{8,0},{10,2},{12,4},{14,6},{1,9},{3,11}... | collective-permute-start | bytes 294920 | tf_op jit(solution)/shard_map/ppermute | solution.py:48
  55.7 1.2 %collective-permute-done.8.halo = bf16[64,256]{1,0:T(8,128)(2,1)S(1)} collective-permute-done((bf16[64,256]{1,0:T(8,128)(2,1)S(1)}, bf16[64,256]{1,0:T(8,128)(2,1)S(1)}, u32[]{:S(2)}, u32[]{:S(2)}) %collective-permute-start.8) | collective-permute-done | bytes 32800 | tf_op jit(solution)/shard_map/ppermute | solution.py:48
  56.9 0.9 %collective-permute-start.15 = (bf16[256,512]{1,0:T(8,128)(2,1)S(1)}, bf16[256,512]{1,0:T(8,128)(2,1)S(1)}, u32[]{:S(2)}, u32[]{:S(2)}) collective-permute-start(bf16[256,512]{1,0:T(8,128)(2,1)S(1)} %get-tuple-element.67), channel_id=1, source_target_pairs={{0,2},{2,0},{4,6},{6,4},{8,10},{10,8},{12,14},{14,12},{1,3},{3,1},... | collective-permute-start | bytes 786440 | tf_op jit(solution)/shard_map/ppermute | solution.py:48
  57.8 1.1 %context.1 = (bf16[512,256]{1,0:T(8,128)(2,1)}, f32[1,256]{1,0:T(1,128)S(1)}) custom-call(bf16[512,256]{1,0:T(8,128)(2,1)S(1)} %get-tuple-element.52.hidden, bf16[64,256]{1,0:T(8,128)(2,1)S(1)} %collective-permute-done.8.halo, f32[512,256]{1,0:T(8,128)S(1)} %get-tuple-element.53.residual, f32[1,256]{1,0:T(1,128)S(1)} %get-tuple-element.42._.gain, ...), custom_call_target="tpu_custom_call" | custom-call | flops 201326592 | bytes 1048576 | tf_op jit(solution)/shard_map/context/pallas_call | solution.py:70
  59.1 5.1 %collective-permute-start.13 = (bf16[256,512]{1,0:T(8,128)(2,1)S(1)}, bf16[256,512]{1,0:T(8,128)(2,1)S(1)}, u32[]{:S(2)}, u32[]{:S(2)}) collective-permute-start(bf16[256,512]{1,0:T(8,128)(2,1)S(1)} %get-tuple-element.65), channel_id=1, source_target_pairs={{0,4},{2,6},{8,12},{10,14},{4,0},{6,2},{12,8},{14,10},{1,5},{3,7},... | collective-permute-start | bytes 786440 | tf_op jit(solution)/shard_map/ppermute | solution.py:59
  64.9 3.8 %collective-permute-start.22 = (bf16[192,256]{1,0:T(8,128)(2,1)S(1)}, bf16[192,256]{1,0:T(8,128)(2,1)S(1)}, u32[]{:S(2)}, u32[]{:S(2)}) collective-permute-start(bf16[192,256]{1,0:T(8,128)(2,1)S(1)} %add_convert_fusion.own), channel_id=1, source_target_pairs={{0,6},{2,4},{4,2},{6,0},{8,14},{10,12},{12,10},{14,8},{1,7},{3,5},... | collective-permute-start | bytes 294920 | tf_op jit(solution)/shard_map/ppermute | solution.py:48
  69.4 1.3 %collective-permute-done.13.first = bf16[256,512]{1,0:T(8,128)(2,1)S(1)} collective-permute-done((bf16[256,512]{1,0:T(8,128)(2,1)S(1)}, bf16[256,512]{1,0:T(8,128)(2,1)S(1)}, u32[]{:S(2)}, u32[]{:S(2)}) %collective-permute-start.13) | collective-permute-done | bytes 262176 | tf_op jit(solution)/shard_map/ppermute | solution.py:59
  70.6 0.9 %latent_gradient.1 = (bf16[512,256]{1,0:T(8,128)(2,1)}, f32[16,128]{1,0:T(8,128)S(1)}) custom-call(f32[512,256]{1,0:T(8,128)S(1)} %get-tuple-element.55.base, bf16[256,512]{1,0:T(8,128)(2,1)S(1)} %collective-permute-done.13.first, bf16[256,512]{1,0:T(8,128)(2,1)S(1)} %collective-permute-done.14.second, bf16[256,512]{1,0:T(8,128)(2,1)S(1)} %collective-permute-done.15.pair), custom_call_target="tpu_custom_call" | custom-call | flops 524288 | bytes 1572864 | tf_op jit(solution)/shard_map/latent_gradient/pallas_call | solution.py:70
  72.2 1.2 %collective-permute-done.21.second = bf16[192,256]{1,0:T(8,128)(2,1)S(1)} collective-permute-done((bf16[192,256]{1,0:T(8,128)(2,1)S(1)}, bf16[192,256]{1,0:T(8,128)(2,1)S(1)}, u32[]{:S(2)}, u32[]{:S(2)}) %collective-permute-start.21) | collective-permute-done | bytes 98336 | tf_op jit(solution)/shard_map/ppermute | solution.py:48
  73.5 1.7 %collective-permute-done.23.other = bf16[768,256]{1,0:T(8,128)(2,1)S(1)} collective-permute-done((bf16[768,256]{1,0:T(8,128)(2,1)S(1)}, bf16[768,256]{1,0:T(8,128)(2,1)S(1)}, u32[]{:S(2)}, u32[]{:S(2)}) %collective-permute-start.23) | collective-permute-done | bytes 393248 | tf_op jit(solution)/shard_map/ppermute | solution.py:48
  75.2 1.2 %weight_gradients.1 = (f32[256,256]{1,0:T(8,128)}, f32[256,256]{1,0:T(8,128)}, f32[256,256]{1,0:T(8,128)}, f32[3,256,256]{2,1,0:T(8,128)}) custom-call(bf16[768,256]{1,0:T(8,128)(2,1)S(1)} %pieces.1.own, bf16[768,256]{1,0:T(8,128)(2,1)S(1)} %collective-permute-done.23.other), custom_call_target="tpu_custom_call" | custom-call | flops 393216 | bytes 2359296 | tf_op jit(solution)/shard_map/weight_gradients/pallas_call | solution.py:70
  (56 shorter events, 8.8 us)
Async XLA Ops:
  0.6 8.1 %collective-permute-start.1 = (bf16[512,256]{1,0:T(8,128)(2,1)}, bf16[512,256]{1,0:T(8,128)(2,1)S(1)}, u32[]{:S(2)}, u32[]{:S(2)}) collective-permute-start(bf16[512,256]{1,0:T(8,128)(2,1)} %bitcast.7), channel_id=1, source_target_pairs={{4,8},{6,10},{8,4},{10,6},{5,9},{7,11},{9,5},{11,7},{20,24},{22,26... | collective-permute-start | bytes 786440 | tf_op jit(solution)/shard_map/ppermute | solution.py:59
  1.3 12.1 %collective-permute-start.2 = (bf16[512,256]{1,0:T(8,128)(2,1)}, bf16[512,256]{1,0:T(8,128)(2,1)S(1)}, u32[]{:S(2)}, u32[]{:S(2)}) collective-permute-start(bf16[512,256]{1,0:T(8,128)(2,1)} %bitcast.8), channel_id=1, source_target_pairs={{0,4},{2,6},{8,12},{10,14},{4,0},{6,2},{12,8},{14,10},{1,5},{3,7},... | collective-permute-start | bytes 786440 | tf_op jit(solution)/shard_map/ppermute | solution.py:59
  7.2 10.7 %collective-permute-start = (bf16[512,256]{1,0:T(8,128)(2,1)}, bf16[512,256]{1,0:T(8,128)(2,1)S(1)}, u32[]{:S(2)}, u32[]{:S(2)}) collective-permute-start(bf16[512,256]{1,0:T(8,128)(2,1)} %bitcast.9), channel_id=1, source_target_pairs={{0,2},{2,0},{4,6},{6,4},{8,10},{10,8},{12,14},{14,12},{1,3},{3,1},... | collective-permute-start | bytes 786440 | tf_op jit(solution)/shard_map/ppermute | solution.py:48
  8.8 12.6 %collective-permute-start.4 = (bf16[576,256]{1,0:T(8,128)(2,1)S(1)}, bf16[576,256]{1,0:T(8,128)(2,1)S(1)}, u32[]{:S(2)}, u32[]{:S(2)}) collective-permute-start(bf16[576,256]{1,0:T(8,128)(2,1)S(1)} %pad_maximum_fusion), channel_id=1, source_target_pairs={{8,12},{10,14},{4,0},{6,2},{9,13},{11,15},{5,1},{7,3},{24,28},{26,... | collective-permute-start | bytes 884744 | tf_op jit(solution)/shard_map/ppermute | solution.py:59
  13.5 7.2 %collective-permute-start.3 = (bf16[512,256]{1,0:T(8,128)(2,1)S(1)}, bf16[512,256]{1,0:T(8,128)(2,1)S(1)}, u32[]{:S(2)}, u32[]{:S(2)}) collective-permute-start(bf16[512,256]{1,0:T(8,128)(2,1)S(1)} %broadcast_select_fusion), channel_id=1, source_target_pairs={{0,2},{2,0},{4,6},{6,4},{8,10},{10,8},{12,14},{14,12},{1,3},{3,1},... | collective-permute-start | bytes 786440 | tf_op jit(solution)/shard_map/ppermute | solution.py:48
  15.1 2.9 %collective-permute-start.5 = (bf16[512,256]{1,0:T(8,128)(2,1)S(1)}, bf16[512,256]{1,0:T(8,128)(2,1)S(1)}, u32[]{:S(2)}, u32[]{:S(2)}) collective-permute-start(bf16[512,256]{1,0:T(8,128)(2,1)S(1)} %collective-permute-done.2.first), channel_id=1, source_target_pairs={{4,8},{6,10},{8,4},{10,6},{5,9},{7,11},{9,5},{11,7},{20,24},{22,26... | collective-permute-start | bytes 786440 | tf_op jit(solution)/shard_map/ppermute | solution.py:59
  15.8 1.3 %collective-permute-start.6 = (bf16[64,256]{1,0:T(8,128)(2,1)S(1)}, bf16[64,256]{1,0:T(8,128)(2,1)S(1)}, u32[]{:S(2)}, u32[]{:S(2)}) collective-permute-start(bf16[64,256]{1,0:T(8,128)(2,1)S(1)} %select_bitcast_fusion), channel_id=1, source_target_pairs={{0,1},{1,0},{2,3},{3,2},{4,5},{5,4},{6,7},{7,6},{8,9},{9,8},{10,11... | collective-permute-start | bytes 98312 | tf_op jit(solution)/shard_map/ppermute | solution.py:48
  22.1 1.4 %collective-permute-start.7 = (bf16[2,128,256]{2,1,0:T(8,128)(2,1)S(1)}, bf16[2,128,256]{2,1,0:T(8,128)(2,1)S(1)}, u32[]{:S(2)}, u32[]{:S(2)}) collective-permute-start(bf16[2,128,256]{2,1,0:T(8,128)(2,1)S(1)} %get-tuple-element.44), channel_id=1, source_target_pairs={{0,1},{1,0},{2,3},{3,2},{4,5},{5,4},{6,7},{7,6},{8,9},{9,8},{10,11... | collective-permute-start | bytes 393224 | tf_op jit(solution)/shard_map/ppermute | solution.py:48
  39.0 2.0 %collective-permute-start.9 = (bf16[1024,256]{1,0:T(8,128)(2,1)S(1)}, bf16[1024,256]{1,0:T(8,128)(2,1)S(1)}, u32[]{:S(2)}, u32[]{:S(2)}) collective-permute-start(bf16[1024,256]{1,0:T(8,128)(2,1)S(1)} %get-tuple-element.58), channel_id=1, source_target_pairs={{0,1},{1,0},{2,3},{3,2},{4,5},{5,4},{6,7},{7,6},{8,9},{9,8},{10,11... | collective-permute-start | bytes 1572872 | tf_op jit(solution)/shard_map/ppermute | solution.py:48
  41.9 10.4 %collective-permute-start.16 = (bf16[192,256]{1,0:T(8,128)(2,1)S(1)}, bf16[192,256]{1,0:T(8,128)(2,1)S(1)}, u32[]{:S(2)}, u32[]{:S(2)}) collective-permute-start(bf16[192,256]{1,0:T(8,128)(2,1)S(1)} %get-tuple-element.70), channel_id=1, source_target_pairs={{0,2},{2,0},{4,6},{6,4},{8,10},{10,8},{12,14},{14,12},{1,3},{3,1},... | collective-permute-start | bytes 294920 | tf_op jit(solution)/shard_map/ppermute | solution.py:48
  43.4 9.5 %collective-permute-start.17 = (bf16[192,256]{1,0:T(8,128)(2,1)S(1)}, bf16[192,256]{1,0:T(8,128)(2,1)S(1)}, u32[]{:S(2)}, u32[]{:S(2)}) collective-permute-start(bf16[192,256]{1,0:T(8,128)(2,1)S(1)} %get-tuple-element.71), channel_id=1, source_target_pairs={{0,4},{2,6},{4,0},{6,2},{8,12},{10,14},{12,8},{14,10},{1,5},{3,7},... | collective-permute-start | bytes 294920 | tf_op jit(solution)/shard_map/ppermute | solution.py:48
  46.8 6.1 %collective-permute-start.18 = (bf16[192,256]{1,0:T(8,128)(2,1)S(1)}, bf16[192,256]{1,0:T(8,128)(2,1)S(1)}, u32[]{:S(2)}, u32[]{:S(2)}) collective-permute-start(bf16[192,256]{1,0:T(8,128)(2,1)S(1)} %get-tuple-element.72), channel_id=1, source_target_pairs={{0,6},{2,4},{4,2},{6,0},{8,14},{10,12},{12,10},{14,8},{1,7},{3,5},... | collective-permute-start | bytes 294920 | tf_op jit(solution)/shard_map/ppermute | solution.py:48
  47.7 11.2 %collective-permute-start.10 = (bf16[256,512]{1,0:T(8,128)(2,1)S(1)}, bf16[256,512]{1,0:T(8,128)(2,1)S(1)}, u32[]{:S(2)}, u32[]{:S(2)}) collective-permute-start(bf16[256,512]{1,0:T(8,128)(2,1)S(1)} %get-tuple-element.59), channel_id=1, source_target_pairs={{0,2},{2,0},{4,6},{6,4},{8,10},{10,8},{12,14},{14,12},{1,3},{3,1},... | collective-permute-start | bytes 786440 | tf_op jit(solution)/shard_map/ppermute | solution.py:48
  48.3 10.6 %collective-permute-start.11 = (bf16[256,512]{1,0:T(8,128)(2,1)S(1)}, bf16[256,512]{1,0:T(8,128)(2,1)S(1)}, u32[]{:S(2)}, u32[]{:S(2)}) collective-permute-start(bf16[256,512]{1,0:T(8,128)(2,1)S(1)} %get-tuple-element.60), channel_id=1, source_target_pairs={{0,4},{2,6},{12,8},{14,10},{1,5},{3,7},{13,9},{15,11},{16,20},{18,... | collective-permute-start | bytes 786440 | tf_op jit(solution)/shard_map/ppermute | solution.py:59
  52.2 6.7 %collective-permute-start.12 = (bf16[256,512]{1,0:T(8,128)(2,1)S(1)}, bf16[256,512]{1,0:T(8,128)(2,1)S(1)}, u32[]{:S(2)}, u32[]{:S(2)}) collective-permute-start(bf16[256,512]{1,0:T(8,128)(2,1)S(1)} %get-tuple-element.61), channel_id=1, source_target_pairs={{4,8},{6,10},{8,4},{10,6},{5,9},{7,11},{9,5},{11,7},{20,24},{22,26... | collective-permute-start | bytes 786440 | tf_op jit(solution)/shard_map/ppermute | solution.py:59
  53.0 11.9 %collective-permute-start.19 = (bf16[192,256]{1,0:T(8,128)(2,1)S(1)}, bf16[192,256]{1,0:T(8,128)(2,1)S(1)}, u32[]{:S(2)}, u32[]{:S(2)}) collective-permute-start(bf16[192,256]{1,0:T(8,128)(2,1)S(1)} %add_convert_fusion.1), channel_id=1, source_target_pairs={{0,8},{2,10},{4,12},{6,14},{8,0},{10,2},{12,4},{14,6},{1,9},{3,11}... | collective-permute-start | bytes 294920 | tf_op jit(solution)/shard_map/ppermute | solution.py:48
  55.7 1.2 %collective-permute-start.8 = (bf16[64,256]{1,0:T(8,128)(2,1)S(1)}, bf16[64,256]{1,0:T(8,128)(2,1)S(1)}, u32[]{:S(2)}, u32[]{:S(2)}) collective-permute-start(bf16[64,256]{1,0:T(8,128)(2,1)S(1)} %slice_select_fusion), channel_id=1, source_target_pairs={{0,1},{1,0},{2,3},{3,2},{4,5},{5,4},{6,7},{7,6},{8,9},{9,8},{10,11... | collective-permute-start | bytes 98312 | tf_op jit(solution)/shard_map/ppermute | solution.py:48
  56.9 11.8 %collective-permute-start.15 = (bf16[256,512]{1,0:T(8,128)(2,1)S(1)}, bf16[256,512]{1,0:T(8,128)(2,1)S(1)}, u32[]{:S(2)}, u32[]{:S(2)}) collective-permute-start(bf16[256,512]{1,0:T(8,128)(2,1)S(1)} %get-tuple-element.67), channel_id=1, source_target_pairs={{0,2},{2,0},{4,6},{6,4},{8,10},{10,8},{12,14},{14,12},{1,3},{3,1},... | collective-permute-start | bytes 786440 | tf_op jit(solution)/shard_map/ppermute | solution.py:48
  59.1 11.5 %collective-permute-start.13 = (bf16[256,512]{1,0:T(8,128)(2,1)S(1)}, bf16[256,512]{1,0:T(8,128)(2,1)S(1)}, u32[]{:S(2)}, u32[]{:S(2)}) collective-permute-start(bf16[256,512]{1,0:T(8,128)(2,1)S(1)} %get-tuple-element.65), channel_id=1, source_target_pairs={{0,4},{2,6},{8,12},{10,14},{4,0},{6,2},{12,8},{14,10},{1,5},{3,7},... | collective-permute-start | bytes 786440 | tf_op jit(solution)/shard_map/ppermute | solution.py:59
  64.2 6.5 %collective-permute-start.14 = (bf16[256,512]{1,0:T(8,128)(2,1)S(1)}, bf16[256,512]{1,0:T(8,128)(2,1)S(1)}, u32[]{:S(2)}, u32[]{:S(2)}) collective-permute-start(bf16[256,512]{1,0:T(8,128)(2,1)S(1)} %get-tuple-element.66), channel_id=1, source_target_pairs={{4,8},{6,10},{8,4},{10,6},{5,9},{7,11},{9,5},{11,7},{20,24},{22,26... | collective-permute-start | bytes 786440 | tf_op jit(solution)/shard_map/ppermute | solution.py:59
  64.9 7.3 %collective-permute-start.22 = (bf16[192,256]{1,0:T(8,128)(2,1)S(1)}, bf16[192,256]{1,0:T(8,128)(2,1)S(1)}, u32[]{:S(2)}, u32[]{:S(2)}) collective-permute-start(bf16[192,256]{1,0:T(8,128)(2,1)S(1)} %add_convert_fusion.own), channel_id=1, source_target_pairs={{0,6},{2,4},{4,2},{6,0},{8,14},{10,12},{12,10},{14,8},{1,7},{3,5},... | collective-permute-start | bytes 294920 | tf_op jit(solution)/shard_map/ppermute | solution.py:48
  68.7 4.6 %collective-permute-start.21 = (bf16[192,256]{1,0:T(8,128)(2,1)S(1)}, bf16[192,256]{1,0:T(8,128)(2,1)S(1)}, u32[]{:S(2)}, u32[]{:S(2)}) collective-permute-start(bf16[192,256]{1,0:T(8,128)(2,1)S(1)} %add_convert_fusion.own), channel_id=1, source_target_pairs={{0,4},{2,6},{4,0},{6,2},{8,12},{10,14},{12,8},{14,10},{1,5},{3,7},... | collective-permute-start | bytes 294920 | tf_op jit(solution)/shard_map/ppermute | solution.py:48
  68.7 4.6 %collective-permute-start.20 = (bf16[192,256]{1,0:T(8,128)(2,1)S(1)}, bf16[192,256]{1,0:T(8,128)(2,1)S(1)}, u32[]{:S(2)}, u32[]{:S(2)}) collective-permute-start(bf16[192,256]{1,0:T(8,128)(2,1)S(1)} %add_convert_fusion.own), channel_id=1, source_target_pairs={{0,2},{2,0},{4,6},{6,4},{8,10},{10,8},{12,14},{14,12},{1,3},{3,1},... | collective-permute-start | bytes 294920 | tf_op jit(solution)/shard_map/ppermute | solution.py:48
  73.4 1.8 %collective-permute-start.23 = (bf16[768,256]{1,0:T(8,128)(2,1)S(1)}, bf16[768,256]{1,0:T(8,128)(2,1)S(1)}, u32[]{:S(2)}, u32[]{:S(2)}) collective-permute-start(bf16[768,256]{1,0:T(8,128)(2,1)S(1)} %pieces.1.own), channel_id=1, source_target_pairs={{0,1},{1,0},{2,3},{3,2},{4,5},{5,4},{6,7},{7,6},{8,9},{9,8},{10,11... | collective-permute-start | bytes 1179656 | tf_op jit(solution)/shard_map/ppermute | solution.py:48
  (8 other events, 44.6 us)

commit v8 on v7

--- a/solution.py
+++ b/solution.py
@@ -514,7 +514,7 @@
     own = (own.astype(F32) + other.astype(F32)).astype(BF16)
 
     across = swapped(across, "frame", 1)
-    first = along(first, 0, passed_on=True)
+    first = along(first, 0)
     second = along(second, 2)
     coded, gain = whole_call(
         coded_kernel,

time: 76.6 us -> 76.6 us (level)
  starting transfers between devices: 37 us -> 34.3 us
  waiting for transfers between devices: 15.7 us -> 18.4 us
    ppermute x8, starting transfers between devices: 19 us -> 16.3 us  [along(): return lax.ppermute(array, 'frame', pairs)]
    ppermute x16, waiting for transfers between devices: 10.5 us -> 12.4 us  [swapped(): return lax.ppermute(array, axis, pairs)]
    ppermute x8, waiting for transfers between devices: 5.19 us -> 6.03 us  [along(): return lax.ppermute(array, 'frame', pairs)]
  transfers between devices with their start and end apart: 24 -> 24, of which waited for: 11 -> 12; matrix products, arithmetic and copies ran while one was open for 0% -> 0% of each run, Pallas kernels for 4% -> 4%
where the time goes in v8:
time: 76.6 us; the launch traced here: 76.4 us
  starting transfers between devices  34.3 us (45%)
  Pallas kernels  21.3 us (28%)
  waiting for transfers between devices  18.4 us (24%)
  between operations  2.19 us (3%)
    pallas_call x9, Pallas kernels, whole_call(): pl.pallas_call(body, out_shape=[jax.ShapeDtypeStruct(shape, dtype) for sh...  21.3 us
    ppermute x16, starting transfers between devices, swapped(): return lax.ppermute(array, axis, pairs)  18 us
    ppermute x8, starting transfers between devices, along(): return lax.ppermute(array, 'frame', pairs)  16.3 us
    ppermute x16, waiting for transfers between devices, swapped(): return lax.ppermute(array, axis, pairs)  12.4 us
    ppermute x8, waiting for transfers between devices, along(): return lax.ppermute(array, 'frame', pairs)  6.03 us
  transfers between devices with their start and end apart: 24, of which 12 were waited for; matrix products, arithmetic and copies ran while one was open for 0% of the time, Pallas kernels for 4%

profile of v8, /device:TPU:0, one launch (start us, length us, event | category | flops | bytes accessed | tf_op | source)
XLA Modules:
  0.0 76.4 jit_solution(6662629750540420571)
XLA Ops:
  1.3 5.9 %collective-permute-start.2 = (bf16[512,256]{1,0:T(8,128)(2,1)}, bf16[512,256]{1,0:T(8,128)(2,1)S(1)}, u32[]{:S(2)}, u32[]{:S(2)}) collective-permute-start(bf16[512,256]{1,0:T(8,128)(2,1)} %bitcast.8), channel_id=1, source_target_pairs={{0,4},{2,6},{8,12},{10,14},{4,0},{6,2},{12,8},{14,10},{1,5},{3,7},... | collective-permute-start | bytes 786440 | tf_op jit(solution)/shard_map/ppermute | solution.py:59
  7.2 1.5 %collective-permute-start = (bf16[512,256]{1,0:T(8,128)(2,1)}, bf16[512,256]{1,0:T(8,128)(2,1)S(1)}, u32[]{:S(2)}, u32[]{:S(2)}) collective-permute-start(bf16[512,256]{1,0:T(8,128)(2,1)} %bitcast.9), channel_id=1, source_target_pairs={{0,2},{2,0},{4,6},{6,4},{8,10},{10,8},{12,14},{14,12},{1,3},{3,1},... | collective-permute-start | bytes 786440 | tf_op jit(solution)/shard_map/ppermute | solution.py:48
  8.8 1.4 %collective-permute-start.4 = (bf16[576,256]{1,0:T(8,128)(2,1)S(1)}, bf16[576,256]{1,0:T(8,128)(2,1)S(1)}, u32[]{:S(2)}, u32[]{:S(2)}) collective-permute-start(bf16[576,256]{1,0:T(8,128)(2,1)S(1)} %pad_maximum_fusion), channel_id=1, source_target_pairs={{8,12},{10,14},{4,0},{6,2},{9,13},{11,15},{5,1},{7,3},{24,28},{26,... | collective-permute-start | bytes 884744 | tf_op jit(solution)/shard_map/ppermute | solution.py:59
  10.2 3.2 %collective-permute-done.2.first = bf16[512,256]{1,0:T(8,128)(2,1)S(1)} collective-permute-done((bf16[512,256]{1,0:T(8,128)(2,1)}, bf16[512,256]{1,0:T(8,128)(2,1)S(1)}, u32[]{:S(2)}, u32[]{:S(2)}) %collective-permute-start.2) | collective-permute-done | bytes 262176 | tf_op jit(solution)/shard_map/ppermute | solution.py:59
  13.5 1.6 %collective-permute-start.3 = (bf16[512,256]{1,0:T(8,128)(2,1)S(1)}, bf16[512,256]{1,0:T(8,128)(2,1)S(1)}, u32[]{:S(2)}, u32[]{:S(2)}) collective-permute-start(bf16[512,256]{1,0:T(8,128)(2,1)S(1)} %broadcast_select_fusion), channel_id=1, source_target_pairs={{0,2},{2,0},{4,6},{6,4},{8,10},{10,8},{12,14},{14,12},{1,3},{3,1},... | collective-permute-start | bytes 786440 | tf_op jit(solution)/shard_map/ppermute | solution.py:48
  17.9 2.8 %collective-permute-done.3.cross = bf16[512,256]{1,0:T(8,128)(2,1)S(1)} collective-permute-done((bf16[512,256]{1,0:T(8,128)(2,1)S(1)}, bf16[512,256]{1,0:T(8,128)(2,1)S(1)}, u32[]{:S(2)}, u32[]{:S(2)}) %collective-permute-start.3) | collective-permute-done | bytes 262176 | tf_op jit(solution)/shard_map/ppermute | solution.py:48
  23.5 15.5 %attention.1 = (f32[2,256,512]{2,1,0:T(8,128)S(1)}, bf16[1024,256]{1,0:T(8,128)(2,1)S(1)}, f32[768,256]{1,0:T(8,128)S(1)}, bf16[512,256]{1,0:T(8,128)(2,1)S(1)},...) custom-call(s32[1]{0:T(128)S(6)} %copy.16.windows, bf16[2,512,256]{2,1,0:T(8,128)(2,1)S(1)} %get-tuple-element.43.slots, ...), custom_call_target="tpu_custom_call" | custom-call | flops 9663676416 | bytes 7864320 | tf_op jit(solution)/shard_map/attention/pallas_call | solution.py:70
  39.2 1.7 %collective-permute-done.9.got = bf16[1024,256]{1,0:T(8,128)(2,1)S(1)} collective-permute-done((bf16[1024,256]{1,0:T(8,128)(2,1)S(1)}, bf16[1024,256]{1,0:T(8,128)(2,1)S(1)}, u32[]{:S(2)}, u32[]{:S(2)}) %collective-permute-start.9) | collective-permute-done | bytes 524320 | tf_op jit(solution)/shard_map/ppermute | solution.py:48
  41.0 0.9 %spread.1 = (bf16[256,512]{1,0:T(8,128)(2,1)S(1)}, bf16[256,512]{1,0:T(8,128)(2,1)S(1)}, bf16[256,512]{1,0:T(8,128)(2,1)S(1)}, bf16[256,512]{1,0:T(8,128)(2,1)S(...) custom-call(s32[1,2]{1,0:T(1,128)S(1)} %copy-done.6, ...), custom_call_target="tpu_custom_call" | custom-call | flops 1572864 | bytes 3932160 | tf_op jit(solution)/shard_map/spread/pallas_call | solution.py:70
  41.9 1.5 %collective-permute-start.16 = (bf16[192,256]{1,0:T(8,128)(2,1)S(1)}, bf16[192,256]{1,0:T(8,128)(2,1)S(1)}, u32[]{:S(2)}, u32[]{:S(2)}) collective-permute-start(bf16[192,256]{1,0:T(8,128)(2,1)S(1)} %get-tuple-element.70), channel_id=1, source_target_pairs={{0,2},{2,0},{4,6},{6,4},{8,10},{10,8},{12,14},{14,12},{1,3},{3,1},... | collective-permute-start | bytes 294920 | tf_op jit(solution)/shard_map/ppermute | solution.py:48
  43.4 3.4 %collective-permute-start.17 = (bf16[192,256]{1,0:T(8,128)(2,1)S(1)}, bf16[192,256]{1,0:T(8,128)(2,1)S(1)}, u32[]{:S(2)}, u32[]{:S(2)}) collective-permute-start(bf16[192,256]{1,0:T(8,128)(2,1)S(1)} %get-tuple-element.71), channel_id=1, source_target_pairs={{0,4},{2,6},{4,0},{6,2},{8,12},{10,14},{12,8},{14,10},{1,5},{3,7},... | collective-permute-start | bytes 294920 | tf_op jit(solution)/shard_map/ppermute | solution.py:48
  46.8 0.9 %collective-permute-start.18 = (bf16[192,256]{1,0:T(8,128)(2,1)S(1)}, bf16[192,256]{1,0:T(8,128)(2,1)S(1)}, u32[]{:S(2)}, u32[]{:S(2)}) collective-permute-start(bf16[192,256]{1,0:T(8,128)(2,1)S(1)} %get-tuple-element.72), channel_id=1, source_target_pairs={{0,6},{2,4},{4,2},{6,0},{8,14},{10,12},{12,10},{14,8},{1,7},{3,5},... | collective-permute-start | bytes 294920 | tf_op jit(solution)/shard_map/ppermute | solution.py:48
  48.3 2.0 %collective-permute-start.11 = (bf16[256,512]{1,0:T(8,128)(2,1)S(1)}, bf16[256,512]{1,0:T(8,128)(2,1)S(1)}, u32[]{:S(2)}, u32[]{:S(2)}) collective-permute-start(bf16[256,512]{1,0:T(8,128)(2,1)S(1)} %get-tuple-element.60), channel_id=1, source_target_pairs={{0,4},{2,6},{8,12},{10,14},{4,0},{6,2},{12,8},{14,10},{1,5},{3,7},... | collective-permute-start | bytes 786440 | tf_op jit(solution)/shard_map/ppermute | solution.py:59
  51.0 2.4 %collective-permute-done.18 = bf16[192,256]{1,0:T(8,128)(2,1)S(1)} collective-permute-done((bf16[192,256]{1,0:T(8,128)(2,1)S(1)}, bf16[192,256]{1,0:T(8,128)(2,1)S(1)}, u32[]{:S(2)}, u32[]{:S(2)}) %collective-permute-start.18) | collective-permute-done | bytes 98336 | tf_op jit(solution)/shard_map/ppermute | solution.py:48
  53.5 3.2 %collective-permute-start.19 = (bf16[192,256]{1,0:T(8,128)(2,1)S(1)}, bf16[192,256]{1,0:T(8,128)(2,1)S(1)}, u32[]{:S(2)}, u32[]{:S(2)}) collective-permute-start(bf16[192,256]{1,0:T(8,128)(2,1)S(1)} %add_convert_fusion.1), channel_id=1, source_target_pairs={{0,8},{2,10},{4,12},{6,14},{8,0},{10,2},{12,4},{14,6},{1,9},{3,11}... | collective-permute-start | bytes 294920 | tf_op jit(solution)/shard_map/ppermute | solution.py:48
  56.7 1.2 %collective-permute-done.8.halo = bf16[64,256]{1,0:T(8,128)(2,1)S(1)} collective-permute-done((bf16[64,256]{1,0:T(8,128)(2,1)S(1)}, bf16[64,256]{1,0:T(8,128)(2,1)S(1)}, u32[]{:S(2)}, u32[]{:S(2)}) %collective-permute-start.8) | collective-permute-done | bytes 32800 | tf_op jit(solution)/shard_map/ppermute | solution.py:48
  58.4 1.1 %context.1 = (bf16[512,256]{1,0:T(8,128)(2,1)}, f32[1,256]{1,0:T(1,128)S(1)}) custom-call(bf16[512,256]{1,0:T(8,128)(2,1)S(1)} %get-tuple-element.52.hidden, bf16[64,256]{1,0:T(8,128)(2,1)S(1)} %collective-permute-done.8.halo, f32[512,256]{1,0:T(8,128)S(1)} %get-tuple-element.53.residual, f32[1,256]{1,0:T(1,128)S(1)} %get-tuple-element.42._.gain, ...), custom_call_target="tpu_custom_call" | custom-call | flops 201326592 | bytes 1048576 | tf_op jit(solution)/shard_map/context/pallas_call | solution.py:70
  59.7 4.3 %collective-permute-start.13 = (bf16[256,512]{1,0:T(8,128)(2,1)S(1)}, bf16[256,512]{1,0:T(8,128)(2,1)S(1)}, u32[]{:S(2)}, u32[]{:S(2)}) collective-permute-start(bf16[256,512]{1,0:T(8,128)(2,1)S(1)} %get-tuple-element.65), channel_id=1, source_target_pairs={{0,4},{2,6},{8,12},{10,14},{4,0},{6,2},{12,8},{14,10},{1,5},{3,7},... | collective-permute-start | bytes 786440 | tf_op jit(solution)/shard_map/ppermute | solution.py:59
  64.7 2.9 %collective-permute-start.22 = (bf16[192,256]{1,0:T(8,128)(2,1)S(1)}, bf16[192,256]{1,0:T(8,128)(2,1)S(1)}, u32[]{:S(2)}, u32[]{:S(2)}) collective-permute-start(bf16[192,256]{1,0:T(8,128)(2,1)S(1)} %add_convert_fusion.own), channel_id=1, source_target_pairs={{0,6},{2,4},{4,2},{6,0},{8,14},{10,12},{12,10},{14,8},{1,7},{3,5},... | collective-permute-start | bytes 294920 | tf_op jit(solution)/shard_map/ppermute | solution.py:48
  67.7 1.4 %collective-permute-start.20 = (bf16[192,256]{1,0:T(8,128)(2,1)S(1)}, bf16[192,256]{1,0:T(8,128)(2,1)S(1)}, u32[]{:S(2)}, u32[]{:S(2)}) collective-permute-start(bf16[192,256]{1,0:T(8,128)(2,1)S(1)} %add_convert_fusion.own), channel_id=1, source_target_pairs={{0,2},{2,0},{4,6},{6,4},{8,10},{10,8},{12,14},{14,12},{1,3},{3,1},... | collective-permute-start | bytes 294920 | tf_op jit(solution)/shard_map/ppermute | solution.py:48
  69.1 2.1 %collective-permute-done.13.first = bf16[256,512]{1,0:T(8,128)(2,1)S(1)} collective-permute-done((bf16[256,512]{1,0:T(8,128)(2,1)S(1)}, bf16[256,512]{1,0:T(8,128)(2,1)S(1)}, u32[]{:S(2)}, u32[]{:S(2)}) %collective-permute-start.13) | collective-permute-done | bytes 262176 | tf_op jit(solution)/shard_map/ppermute | solution.py:59
  72.1 1.0 %collective-permute-done.22.third = bf16[192,256]{1,0:T(8,128)(2,1)S(1)} collective-permute-done((bf16[192,256]{1,0:T(8,128)(2,1)S(1)}, bf16[192,256]{1,0:T(8,128)(2,1)S(1)}, u32[]{:S(2)}, u32[]{:S(2)}) %collective-permute-start.22) | collective-permute-done | bytes 98336 | tf_op jit(solution)/shard_map/ppermute | solution.py:48
  73.5 1.7 %collective-permute-done.23.other = bf16[768,256]{1,0:T(8,128)(2,1)S(1)} collective-permute-done((bf16[768,256]{1,0:T(8,128)(2,1)S(1)}, bf16[768,256]{1,0:T(8,128)(2,1)S(1)}, u32[]{:S(2)}, u32[]{:S(2)}) %collective-permute-start.23) | collective-permute-done | bytes 393248 | tf_op jit(solution)/shard_map/ppermute | solution.py:48
  75.2 1.2 %weight_gradients.1 = (f32[256,256]{1,0:T(8,128)}, f32[256,256]{1,0:T(8,128)}, f32[256,256]{1,0:T(8,128)}, f32[3,256,256]{2,1,0:T(8,128)}) custom-call(bf16[768,256]{1,0:T(8,128)(2,1)S(1)} %pieces.1.own, bf16[768,256]{1,0:T(8,128)(2,1)S(1)} %collective-permute-done.23.other), custom_call_target="tpu_custom_call" | custom-call | flops 393216 | bytes 2359296 | tf_op jit(solution)/shard_map/weight_gradients/pallas_call | solution.py:70
  (56 shorter events, 9.3 us)
Async XLA Ops:
  0.6 8.1 %collective-permute-start.1 = (bf16[512,256]{1,0:T(8,128)(2,1)}, bf16[512,256]{1,0:T(8,128)(2,1)S(1)}, u32[]{:S(2)}, u32[]{:S(2)}) collective-permute-start(bf16[512,256]{1,0:T(8,128)(2,1)} %bitcast.7), channel_id=1, source_target_pairs={{4,8},{6,10},{8,4},{10,6},{5,9},{7,11},{9,5},{11,7},{20,24},{22,26... | collective-permute-start | bytes 786440 | tf_op jit(solution)/shard_map/ppermute | solution.py:59
  1.3 12.1 %collective-permute-start.2 = (bf16[512,256]{1,0:T(8,128)(2,1)}, bf16[512,256]{1,0:T(8,128)(2,1)S(1)}, u32[]{:S(2)}, u32[]{:S(2)}) collective-permute-start(bf16[512,256]{1,0:T(8,128)(2,1)} %bitcast.8), channel_id=1, source_target_pairs={{0,4},{2,6},{8,12},{10,14},{4,0},{6,2},{12,8},{14,10},{1,5},{3,7},... | collective-permute-start | bytes 786440 | tf_op jit(solution)/shard_map/ppermute | solution.py:59
  7.2 10.7 %collective-permute-start = (bf16[512,256]{1,0:T(8,128)(2,1)}, bf16[512,256]{1,0:T(8,128)(2,1)S(1)}, u32[]{:S(2)}, u32[]{:S(2)}) collective-permute-start(bf16[512,256]{1,0:T(8,128)(2,1)} %bitcast.9), channel_id=1, source_target_pairs={{0,2},{2,0},{4,6},{6,4},{8,10},{10,8},{12,14},{14,12},{1,3},{3,1},... | collective-permute-start | bytes 786440 | tf_op jit(solution)/shard_map/ppermute | solution.py:48
  8.8 12.6 %collective-permute-start.4 = (bf16[576,256]{1,0:T(8,128)(2,1)S(1)}, bf16[576,256]{1,0:T(8,128)(2,1)S(1)}, u32[]{:S(2)}, u32[]{:S(2)}) collective-permute-start(bf16[576,256]{1,0:T(8,128)(2,1)S(1)} %pad_maximum_fusion), channel_id=1, source_target_pairs={{8,12},{10,14},{4,0},{6,2},{9,13},{11,15},{5,1},{7,3},{24,28},{26,... | collective-permute-start | bytes 884744 | tf_op jit(solution)/shard_map/ppermute | solution.py:59
  13.5 7.2 %collective-permute-start.3 = (bf16[512,256]{1,0:T(8,128)(2,1)S(1)}, bf16[512,256]{1,0:T(8,128)(2,1)S(1)}, u32[]{:S(2)}, u32[]{:S(2)}) collective-permute-start(bf16[512,256]{1,0:T(8,128)(2,1)S(1)} %broadcast_select_fusion), channel_id=1, source_target_pairs={{0,2},{2,0},{4,6},{6,4},{8,10},{10,8},{12,14},{14,12},{1,3},{3,1},... | collective-permute-start | bytes 786440 | tf_op jit(solution)/shard_map/ppermute | solution.py:48
  15.1 2.9 %collective-permute-start.5 = (bf16[512,256]{1,0:T(8,128)(2,1)S(1)}, bf16[512,256]{1,0:T(8,128)(2,1)S(1)}, u32[]{:S(2)}, u32[]{:S(2)}) collective-permute-start(bf16[512,256]{1,0:T(8,128)(2,1)S(1)} %collective-permute-done.2.first), channel_id=1, source_target_pairs={{4,8},{6,10},{8,4},{10,6},{5,9},{7,11},{9,5},{11,7},{20,24},{22,26... | collective-permute-start | bytes 786440 | tf_op jit(solution)/shard_map/ppermute | solution.py:59
  15.8 1.3 %collective-permute-start.6 = (bf16[64,256]{1,0:T(8,128)(2,1)S(1)}, bf16[64,256]{1,0:T(8,128)(2,1)S(1)}, u32[]{:S(2)}, u32[]{:S(2)}) collective-permute-start(bf16[64,256]{1,0:T(8,128)(2,1)S(1)} %select_bitcast_fusion), channel_id=1, source_target_pairs={{0,1},{1,0},{2,3},{3,2},{4,5},{5,4},{6,7},{7,6},{8,9},{9,8},{10,11... | collective-permute-start | bytes 98312 | tf_op jit(solution)/shard_map/ppermute | solution.py:48
  22.1 1.4 %collective-permute-start.7 = (bf16[2,128,256]{2,1,0:T(8,128)(2,1)S(1)}, bf16[2,128,256]{2,1,0:T(8,128)(2,1)S(1)}, u32[]{:S(2)}, u32[]{:S(2)}) collective-permute-start(bf16[2,128,256]{2,1,0:T(8,128)(2,1)S(1)} %get-tuple-element.44), channel_id=1, source_target_pairs={{0,1},{1,0},{2,3},{3,2},{4,5},{5,4},{6,7},{7,6},{8,9},{9,8},{10,11... | collective-permute-start | bytes 393224 | tf_op jit(solution)/shard_map/ppermute | solution.py:48
  39.0 2.0 %collective-permute-start.9 = (bf16[1024,256]{1,0:T(8,128)(2,1)S(1)}, bf16[1024,256]{1,0:T(8,128)(2,1)S(1)}, u32[]{:S(2)}, u32[]{:S(2)}) collective-permute-start(bf16[1024,256]{1,0:T(8,128)(2,1)S(1)} %get-tuple-element.58), channel_id=1, source_target_pairs={{0,1},{1,0},{2,3},{3,2},{4,5},{5,4},{6,7},{7,6},{8,9},{9,8},{10,11... | collective-permute-start | bytes 1572872 | tf_op jit(solution)/shard_map/ppermute | solution.py:48
  41.9 8.4 %collective-permute-start.16 = (bf16[192,256]{1,0:T(8,128)(2,1)S(1)}, bf16[192,256]{1,0:T(8,128)(2,1)S(1)}, u32[]{:S(2)}, u32[]{:S(2)}) collective-permute-start(bf16[192,256]{1,0:T(8,128)(2,1)S(1)} %get-tuple-element.70), channel_id=1, source_target_pairs={{0,2},{2,0},{4,6},{6,4},{8,10},{10,8},{12,14},{14,12},{1,3},{3,1},... | collective-permute-start | bytes 294920 | tf_op jit(solution)/shard_map/ppermute | solution.py:48
  43.4 7.6 %collective-permute-start.17 = (bf16[192,256]{1,0:T(8,128)(2,1)S(1)}, bf16[192,256]{1,0:T(8,128)(2,1)S(1)}, u32[]{:S(2)}, u32[]{:S(2)}) collective-permute-start(bf16[192,256]{1,0:T(8,128)(2,1)S(1)} %get-tuple-element.71), channel_id=1, source_target_pairs={{0,4},{2,6},{4,0},{6,2},{8,12},{10,14},{12,8},{14,10},{1,5},{3,7},... | collective-permute-start | bytes 294920 | tf_op jit(solution)/shard_map/ppermute | solution.py:48
  46.8 6.6 %collective-permute-start.18 = (bf16[192,256]{1,0:T(8,128)(2,1)S(1)}, bf16[192,256]{1,0:T(8,128)(2,1)S(1)}, u32[]{:S(2)}, u32[]{:S(2)}) collective-permute-start(bf16[192,256]{1,0:T(8,128)(2,1)S(1)} %get-tuple-element.72), channel_id=1, source_target_pairs={{0,6},{2,4},{4,2},{6,0},{8,14},{10,12},{12,10},{14,8},{1,7},{3,5},... | collective-permute-start | bytes 294920 | tf_op jit(solution)/shard_map/ppermute | solution.py:48
  47.8 11.8 %collective-permute-start.10 = (bf16[256,512]{1,0:T(8,128)(2,1)S(1)}, bf16[256,512]{1,0:T(8,128)(2,1)S(1)}, u32[]{:S(2)}, u32[]{:S(2)}) collective-permute-start(bf16[256,512]{1,0:T(8,128)(2,1)S(1)} %get-tuple-element.59), channel_id=1, source_target_pairs={{0,2},{2,0},{4,6},{6,4},{8,10},{10,8},{12,14},{14,12},{1,3},{3,1},... | collective-permute-start | bytes 786440 | tf_op jit(solution)/shard_map/ppermute | solution.py:48
  48.3 11.2 %collective-permute-start.11 = (bf16[256,512]{1,0:T(8,128)(2,1)S(1)}, bf16[256,512]{1,0:T(8,128)(2,1)S(1)}, u32[]{:S(2)}, u32[]{:S(2)}) collective-permute-start(bf16[256,512]{1,0:T(8,128)(2,1)S(1)} %get-tuple-element.60), channel_id=1, source_target_pairs={{0,4},{2,6},{8,12},{10,14},{4,0},{6,2},{12,8},{14,10},{1,5},{3,7},... | collective-permute-start | bytes 786440 | tf_op jit(solution)/shard_map/ppermute | solution.py:59
  50.3 9.2 %collective-permute-start.12 = (bf16[256,512]{1,0:T(8,128)(2,1)S(1)}, bf16[256,512]{1,0:T(8,128)(2,1)S(1)}, u32[]{:S(2)}, u32[]{:S(2)}) collective-permute-start(bf16[256,512]{1,0:T(8,128)(2,1)S(1)} %get-tuple-element.61), channel_id=1, source_target_pairs={{4,8},{6,10},{8,4},{10,6},{5,9},{7,11},{9,5},{11,7},{20,24},{22,26... | collective-permute-start | bytes 786440 | tf_op jit(solution)/shard_map/ppermute | solution.py:59
  53.5 11.2 %collective-permute-start.19 = (bf16[192,256]{1,0:T(8,128)(2,1)S(1)}, bf16[192,256]{1,0:T(8,128)(2,1)S(1)}, u32[]{:S(2)}, u32[]{:S(2)}) collective-permute-start(bf16[192,256]{1,0:T(8,128)(2,1)S(1)} %add_convert_fusion.1), channel_id=1, source_target_pairs={{0,8},{2,10},{4,12},{6,14},{8,0},{10,2},{12,4},{14,6},{1,9},{3,11}... | collective-permute-start | bytes 294920 | tf_op jit(solution)/shard_map/ppermute | solution.py:48
  56.7 1.2 %collective-permute-start.8 = (bf16[64,256]{1,0:T(8,128)(2,1)S(1)}, bf16[64,256]{1,0:T(8,128)(2,1)S(1)}, u32[]{:S(2)}, u32[]{:S(2)}) collective-permute-start(bf16[64,256]{1,0:T(8,128)(2,1)S(1)} %slice_select_fusion), channel_id=1, source_target_pairs={{0,1},{1,0},{2,3},{3,2},{4,5},{5,4},{6,7},{7,6},{8,9},{9,8},{10,11... | collective-permute-start | bytes 98312 | tf_op jit(solution)/shard_map/ppermute | solution.py:48
  57.9 9.8 %collective-permute-start.15 = (bf16[256,512]{1,0:T(8,128)(2,1)S(1)}, bf16[256,512]{1,0:T(8,128)(2,1)S(1)}, u32[]{:S(2)}, u32[]{:S(2)}) collective-permute-start(bf16[256,512]{1,0:T(8,128)(2,1)S(1)} %get-tuple-element.67), channel_id=1, source_target_pairs={{0,2},{2,0},{4,6},{6,4},{8,10},{10,8},{12,14},{14,12},{1,3},{3,1},... | collective-permute-start | bytes 786440 | tf_op jit(solution)/shard_map/ppermute | solution.py:48
  59.7 11.5 %collective-permute-start.13 = (bf16[256,512]{1,0:T(8,128)(2,1)S(1)}, bf16[256,512]{1,0:T(8,128)(2,1)S(1)}, u32[]{:S(2)}, u32[]{:S(2)}) collective-permute-start(bf16[256,512]{1,0:T(8,128)(2,1)S(1)} %get-tuple-element.65), channel_id=1, source_target_pairs={{0,4},{2,6},{8,12},{10,14},{4,0},{6,2},{12,8},{14,10},{1,5},{3,7},... | collective-permute-start | bytes 786440 | tf_op jit(solution)/shard_map/ppermute | solution.py:59
  64.0 7.2 %collective-permute-start.14 = (bf16[256,512]{1,0:T(8,128)(2,1)S(1)}, bf16[256,512]{1,0:T(8,128)(2,1)S(1)}, u32[]{:S(2)}, u32[]{:S(2)}) collective-permute-start(bf16[256,512]{1,0:T(8,128)(2,1)S(1)} %get-tuple-element.66), channel_id=1, source_target_pairs={{4,8},{6,10},{8,4},{10,6},{5,9},{7,11},{9,5},{11,7},{20,24},{22,26... | collective-permute-start | bytes 786440 | tf_op jit(solution)/shard_map/ppermute | solution.py:59
  64.7 8.4 %collective-permute-start.22 = (bf16[192,256]{1,0:T(8,128)(2,1)S(1)}, bf16[192,256]{1,0:T(8,128)(2,1)S(1)}, u32[]{:S(2)}, u32[]{:S(2)}) collective-permute-start(bf16[192,256]{1,0:T(8,128)(2,1)S(1)} %add_convert_fusion.own), channel_id=1, source_target_pairs={{0,6},{2,4},{4,2},{6,0},{8,14},{10,12},{12,10},{14,8},{1,7},{3,5},... | collective-permute-start | bytes 294920 | tf_op jit(solution)/shard_map/ppermute | solution.py:48
  67.6 5.7 %collective-permute-start.21 = (bf16[192,256]{1,0:T(8,128)(2,1)S(1)}, bf16[192,256]{1,0:T(8,128)(2,1)S(1)}, u32[]{:S(2)}, u32[]{:S(2)}) collective-permute-start(bf16[192,256]{1,0:T(8,128)(2,1)S(1)} %add_convert_fusion.own), channel_id=1, source_target_pairs={{0,4},{2,6},{4,0},{6,2},{8,12},{10,14},{12,8},{14,10},{1,5},{3,7},... | collective-permute-start | bytes 294920 | tf_op jit(solution)/shard_map/ppermute | solution.py:48
  67.7 5.6 %collective-permute-start.20 = (bf16[192,256]{1,0:T(8,128)(2,1)S(1)}, bf16[192,256]{1,0:T(8,128)(2,1)S(1)}, u32[]{:S(2)}, u32[]{:S(2)}) collective-permute-start(bf16[192,256]{1,0:T(8,128)(2,1)S(1)} %add_convert_fusion.own), channel_id=1, source_target_pairs={{0,2},{2,0},{4,6},{6,4},{8,10},{10,8},{12,14},{14,12},{1,3},{3,1},... | collective-permute-start | bytes 294920 | tf_op jit(solution)/shard_map/ppermute | solution.py:48
  73.4 1.8 %collective-permute-start.23 = (bf16[768,256]{1,0:T(8,128)(2,1)S(1)}, bf16[768,256]{1,0:T(8,128)(2,1)S(1)}, u32[]{:S(2)}, u32[]{:S(2)}) collective-permute-start(bf16[768,256]{1,0:T(8,128)(2,1)S(1)} %pieces.1.own), channel_id=1, source_target_pairs={{0,1},{1,0},{2,3},{3,2},{4,5},{5,4},{6,7},{7,6},{8,9},{9,8},{10,11... | collective-permute-start | bytes 1179656 | tf_op jit(solution)/shard_map/ppermute | solution.py:48
  (8 other events, 44.6 us)

commit v9 on v7

--- a/solution.py
+++ b/solution.py
@@ -209,12 +209,12 @@
         value_t = jnp.zeros((width, width), F32)
         for slot in range(2):
             part = jnp.zeros((width, count + 2 * rim), F32)
+            part = part + dot(shared[...], dkt[slot].astype(BF16))
             for piece in halves_of(dkt[slot]):
-                part = part + dot(shared[...], piece)
                 rims = far_rim(piece)
                 shared_t += dot(piece[:, middle], slots[slot]) + dot(rims, halo[slot])
+            part = part + dot(value[...], dvt[slot].astype(BF16))
             for piece in halves_of(dvt[slot]):
-                part = part + dot(value[...], piece)
                 rims = far_rim(piece)
                 value_t += dot(piece[:, middle], slots[slot]) + dot(rims, halo[slot])
             mid_out[slot] = part[:, middle]

time: 76.6 us -> 76.2 us (level)
  no operation moved by 1% of the time
where the time goes in v9:
time: 76.2 us; the launch traced here: 76 us
  starting transfers between devices  36.9 us (48%)
  Pallas kernels  20.9 us (27%)
  waiting for transfers between devices  15.7 us (21%)
  between operations  2.21 us (3%)
    pallas_call x9, Pallas kernels, whole_call(): pl.pallas_call(body, out_shape=[jax.ShapeDtypeStruct(shape, dtype) for sh...  20.9 us
    ppermute x8, starting transfers between devices, along(): return lax.ppermute(array, 'frame', pairs)  19 us
    ppermute x16, starting transfers between devices, swapped(): return lax.ppermute(array, axis, pairs)  18 us
    ppermute x16, waiting for transfers between devices, swapped(): return lax.ppermute(array, axis, pairs)  10.5 us
    ppermute x8, waiting for transfers between devices, along(): return lax.ppermute(array, 'frame', pairs)  5.19 us
  transfers between devices with their start and end apart: 24, of which 11 were waited for; matrix products, arithmetic and copies ran while one was open for 0% of the time, Pallas kernels for 4%

profile of v9, /device:TPU:0, one launch (start us, length us, event | category | flops | bytes accessed | tf_op | source)
XLA Modules:
  0.0 76.0 jit_solution(10407114264066009221)
XLA Ops:
  1.3 5.9 %collective-permute-start.2 = (bf16[512,256]{1,0:T(8,128)(2,1)}, bf16[512,256]{1,0:T(8,128)(2,1)S(1)}, u32[]{:S(2)}, u32[]{:S(2)}) collective-permute-start(bf16[512,256]{1,0:T(8,128)(2,1)} %bitcast.8), channel_id=1, source_target_pairs={{0,4},{2,6},{8,12},{10,14},{4,0},{6,2},{12,8},{14,10},{1,5},{3,7},... | collective-permute-start | bytes 786440 | tf_op jit(solution)/shard_map/ppermute | solution.py:59
  7.2 1.5 %collective-permute-start = (bf16[512,256]{1,0:T(8,128)(2,1)}, bf16[512,256]{1,0:T(8,128)(2,1)S(1)}, u32[]{:S(2)}, u32[]{:S(2)}) collective-permute-start(bf16[512,256]{1,0:T(8,128)(2,1)} %bitcast.9), channel_id=1, source_target_pairs={{0,2},{2,0},{4,6},{6,4},{8,10},{10,8},{12,14},{14,12},{1,3},{3,1},... | collective-permute-start | bytes 786440 | tf_op jit(solution)/shard_map/ppermute | solution.py:48
  8.8 1.4 %collective-permute-start.4 = (bf16[576,256]{1,0:T(8,128)(2,1)S(1)}, bf16[576,256]{1,0:T(8,128)(2,1)S(1)}, u32[]{:S(2)}, u32[]{:S(2)}) collective-permute-start(bf16[576,256]{1,0:T(8,128)(2,1)S(1)} %pad_maximum_fusion), channel_id=1, source_target_pairs={{8,12},{10,14},{4,0},{6,2},{9,13},{11,15},{5,1},{7,3},{24,28},{26,... | collective-permute-start | bytes 884744 | tf_op jit(solution)/shard_map/ppermute | solution.py:59
  10.2 3.2 %collective-permute-done.2.first = bf16[512,256]{1,0:T(8,128)(2,1)S(1)} collective-permute-done((bf16[512,256]{1,0:T(8,128)(2,1)}, bf16[512,256]{1,0:T(8,128)(2,1)S(1)}, u32[]{:S(2)}, u32[]{:S(2)}) %collective-permute-start.2) | collective-permute-done | bytes 262176 | tf_op jit(solution)/shard_map/ppermute | solution.py:59
  13.5 1.6 %collective-permute-start.3 = (bf16[512,256]{1,0:T(8,128)(2,1)S(1)}, bf16[512,256]{1,0:T(8,128)(2,1)S(1)}, u32[]{:S(2)}, u32[]{:S(2)}) collective-permute-start(bf16[512,256]{1,0:T(8,128)(2,1)S(1)} %broadcast_select_fusion), channel_id=1, source_target_pairs={{0,2},{2,0},{4,6},{6,4},{8,10},{10,8},{12,14},{14,12},{1,3},{3,1},... | collective-permute-start | bytes 786440 | tf_op jit(solution)/shard_map/ppermute | solution.py:48
  17.9 2.8 %collective-permute-done.3.cross = bf16[512,256]{1,0:T(8,128)(2,1)S(1)} collective-permute-done((bf16[512,256]{1,0:T(8,128)(2,1)S(1)}, bf16[512,256]{1,0:T(8,128)(2,1)S(1)}, u32[]{:S(2)}, u32[]{:S(2)}) %collective-permute-start.3) | collective-permute-done | bytes 262176 | tf_op jit(solution)/shard_map/ppermute | solution.py:48
  23.5 15.1 %attention.1 = (f32[2,256,512]{2,1,0:T(8,128)S(1)}, bf16[1024,256]{1,0:T(8,128)(2,1)S(1)}, f32[768,256]{1,0:T(8,128)S(1)}, bf16[512,256]{1,0:T(8,128)(2,1)S(1)},...) custom-call(s32[1]{0:T(128)S(6)} %copy.16.windows, bf16[2,512,256]{2,1,0:T(8,128)(2,1)S(1)} %get-tuple-element.43.slots, ...), custom_call_target="tpu_custom_call" | custom-call | flops 9663676416 | bytes 7864320 | tf_op jit(solution)/shard_map/attention/pallas_call | solution.py:70
  38.8 1.7 %collective-permute-done.9.got = bf16[1024,256]{1,0:T(8,128)(2,1)S(1)} collective-permute-done((bf16[1024,256]{1,0:T(8,128)(2,1)S(1)}, bf16[1024,256]{1,0:T(8,128)(2,1)S(1)}, u32[]{:S(2)}, u32[]{:S(2)}) %collective-permute-start.9) | collective-permute-done | bytes 524320 | tf_op jit(solution)/shard_map/ppermute | solution.py:48
  40.6 0.9 %spread.1 = (bf16[256,512]{1,0:T(8,128)(2,1)S(1)}, bf16[256,512]{1,0:T(8,128)(2,1)S(1)}, bf16[256,512]{1,0:T(8,128)(2,1)S(1)}, bf16[256,512]{1,0:T(8,128)(2,1)S(...) custom-call(s32[1,2]{1,0:T(1,128)S(1)} %copy-done.6, ...), custom_call_target="tpu_custom_call" | custom-call | flops 1572864 | bytes 3932160 | tf_op jit(solution)/shard_map/spread/pallas_call | solution.py:70
  41.5 1.5 %collective-permute-start.16 = (bf16[192,256]{1,0:T(8,128)(2,1)S(1)}, bf16[192,256]{1,0:T(8,128)(2,1)S(1)}, u32[]{:S(2)}, u32[]{:S(2)}) collective-permute-start(bf16[192,256]{1,0:T(8,128)(2,1)S(1)} %get-tuple-element.70), channel_id=1, source_target_pairs={{0,2},{2,0},{4,6},{6,4},{8,10},{10,8},{12,14},{14,12},{1,3},{3,1},... | collective-permute-start | bytes 294920 | tf_op jit(solution)/shard_map/ppermute | solution.py:48
  43.0 3.4 %collective-permute-start.17 = (bf16[192,256]{1,0:T(8,128)(2,1)S(1)}, bf16[192,256]{1,0:T(8,128)(2,1)S(1)}, u32[]{:S(2)}, u32[]{:S(2)}) collective-permute-start(bf16[192,256]{1,0:T(8,128)(2,1)S(1)} %get-tuple-element.71), channel_id=1, source_target_pairs={{0,4},{2,6},{4,0},{6,2},{8,12},{10,14},{12,8},{14,10},{1,5},{3,7},... | collective-permute-start | bytes 294920 | tf_op jit(solution)/shard_map/ppermute | solution.py:48
  46.4 0.9 %collective-permute-start.18 = (bf16[192,256]{1,0:T(8,128)(2,1)S(1)}, bf16[192,256]{1,0:T(8,128)(2,1)S(1)}, u32[]{:S(2)}, u32[]{:S(2)}) collective-permute-start(bf16[192,256]{1,0:T(8,128)(2,1)S(1)} %get-tuple-element.72), channel_id=1, source_target_pairs={{0,6},{2,4},{4,2},{6,0},{8,14},{10,12},{12,10},{14,8},{1,7},{3,5},... | collective-permute-start | bytes 294920 | tf_op jit(solution)/shard_map/ppermute | solution.py:48
  47.9 3.9 %collective-permute-start.11 = (bf16[256,512]{1,0:T(8,128)(2,1)S(1)}, bf16[256,512]{1,0:T(8,128)(2,1)S(1)}, u32[]{:S(2)}, u32[]{:S(2)}) collective-permute-start(bf16[256,512]{1,0:T(8,128)(2,1)S(1)} %get-tuple-element.60), channel_id=1, source_target_pairs={{0,4},{2,6},{12,8},{14,10},{1,5},{3,7},{13,9},{15,11},{16,20},{18,... | collective-permute-start | bytes 786440 | tf_op jit(solution)/shard_map/ppermute | solution.py:59
  52.6 2.7 %collective-permute-start.19 = (bf16[192,256]{1,0:T(8,128)(2,1)S(1)}, bf16[192,256]{1,0:T(8,128)(2,1)S(1)}, u32[]{:S(2)}, u32[]{:S(2)}) collective-permute-start(bf16[192,256]{1,0:T(8,128)(2,1)S(1)} %add_convert_fusion.1), channel_id=1, source_target_pairs={{0,8},{2,10},{4,12},{6,14},{8,0},{10,2},{12,4},{14,6},{1,9},{3,11}... | collective-permute-start | bytes 294920 | tf_op jit(solution)/shard_map/ppermute | solution.py:48
  55.3 1.2 %collective-permute-done.8.halo = bf16[64,256]{1,0:T(8,128)(2,1)S(1)} collective-permute-done((bf16[64,256]{1,0:T(8,128)(2,1)S(1)}, bf16[64,256]{1,0:T(8,128)(2,1)S(1)}, u32[]{:S(2)}, u32[]{:S(2)}) %collective-permute-start.8) | collective-permute-done | bytes 32800 | tf_op jit(solution)/shard_map/ppermute | solution.py:48
  56.5 0.9 %collective-permute-start.15 = (bf16[256,512]{1,0:T(8,128)(2,1)S(1)}, bf16[256,512]{1,0:T(8,128)(2,1)S(1)}, u32[]{:S(2)}, u32[]{:S(2)}) collective-permute-start(bf16[256,512]{1,0:T(8,128)(2,1)S(1)} %get-tuple-element.67), channel_id=1, source_target_pairs={{0,2},{2,0},{4,6},{6,4},{8,10},{10,8},{12,14},{14,12},{1,3},{3,1},... | collective-permute-start | bytes 786440 | tf_op jit(solution)/shard_map/ppermute | solution.py:48
  57.4 1.1 %context.1 = (bf16[512,256]{1,0:T(8,128)(2,1)}, f32[1,256]{1,0:T(1,128)S(1)}) custom-call(bf16[512,256]{1,0:T(8,128)(2,1)S(1)} %get-tuple-element.52.hidden, bf16[64,256]{1,0:T(8,128)(2,1)S(1)} %collective-permute-done.8.halo, f32[512,256]{1,0:T(8,128)S(1)} %get-tuple-element.53.residual, f32[1,256]{1,0:T(1,128)S(1)} %get-tuple-element.42._.gain, ...), custom_call_target="tpu_custom_call" | custom-call | flops 201326592 | bytes 1048576 | tf_op jit(solution)/shard_map/context/pallas_call | solution.py:70
  58.7 5.1 %collective-permute-start.13 = (bf16[256,512]{1,0:T(8,128)(2,1)S(1)}, bf16[256,512]{1,0:T(8,128)(2,1)S(1)}, u32[]{:S(2)}, u32[]{:S(2)}) collective-permute-start(bf16[256,512]{1,0:T(8,128)(2,1)S(1)} %get-tuple-element.65), channel_id=1, source_target_pairs={{0,4},{2,6},{8,12},{10,14},{4,0},{6,2},{12,8},{14,10},{1,5},{3,7},... | collective-permute-start | bytes 786440 | tf_op jit(solution)/shard_map/ppermute | solution.py:59
  64.5 3.8 %collective-permute-start.22 = (bf16[192,256]{1,0:T(8,128)(2,1)S(1)}, bf16[192,256]{1,0:T(8,128)(2,1)S(1)}, u32[]{:S(2)}, u32[]{:S(2)}) collective-permute-start(bf16[192,256]{1,0:T(8,128)(2,1)S(1)} %add_convert_fusion.own), channel_id=1, source_target_pairs={{0,6},{2,4},{4,2},{6,0},{8,14},{10,12},{12,10},{14,8},{1,7},{3,5},... | collective-permute-start | bytes 294920 | tf_op jit(solution)/shard_map/ppermute | solution.py:48
  69.0 1.3 %collective-permute-done.13.first = bf16[256,512]{1,0:T(8,128)(2,1)S(1)} collective-permute-done((bf16[256,512]{1,0:T(8,128)(2,1)S(1)}, bf16[256,512]{1,0:T(8,128)(2,1)S(1)}, u32[]{:S(2)}, u32[]{:S(2)}) %collective-permute-start.13) | collective-permute-done | bytes 262176 | tf_op jit(solution)/shard_map/ppermute | solution.py:59
  70.2 0.9 %latent_gradient.1 = (bf16[512,256]{1,0:T(8,128)(2,1)}, f32[16,128]{1,0:T(8,128)S(1)}) custom-call(f32[512,256]{1,0:T(8,128)S(1)} %get-tuple-element.55.base, bf16[256,512]{1,0:T(8,128)(2,1)S(1)} %collective-permute-done.13.first, bf16[256,512]{1,0:T(8,128)(2,1)S(1)} %collective-permute-done.14.second, bf16[256,512]{1,0:T(8,128)(2,1)S(1)} %collective-permute-done.15.pair), custom_call_target="tpu_custom_call" | custom-call | flops 524288 | bytes 1572864 | tf_op jit(solution)/shard_map/latent_gradient/pallas_call | solution.py:70
  71.8 1.2 %collective-permute-done.21.second = bf16[192,256]{1,0:T(8,128)(2,1)S(1)} collective-permute-done((bf16[192,256]{1,0:T(8,128)(2,1)S(1)}, bf16[192,256]{1,0:T(8,128)(2,1)S(1)}, u32[]{:S(2)}, u32[]{:S(2)}) %collective-permute-start.21) | collective-permute-done | bytes 98336 | tf_op jit(solution)/shard_map/ppermute | solution.py:48
  73.1 1.7 %collective-permute-done.23.other = bf16[768,256]{1,0:T(8,128)(2,1)S(1)} collective-permute-done((bf16[768,256]{1,0:T(8,128)(2,1)S(1)}, bf16[768,256]{1,0:T(8,128)(2,1)S(1)}, u32[]{:S(2)}, u32[]{:S(2)}) %collective-permute-start.23) | collective-permute-done | bytes 393248 | tf_op jit(solution)/shard_map/ppermute | solution.py:48
  74.8 1.2 %weight_gradients.1 = (f32[256,256]{1,0:T(8,128)}, f32[256,256]{1,0:T(8,128)}, f32[256,256]{1,0:T(8,128)}, f32[3,256,256]{2,1,0:T(8,128)}) custom-call(bf16[768,256]{1,0:T(8,128)(2,1)S(1)} %pieces.1.own, bf16[768,256]{1,0:T(8,128)(2,1)S(1)} %collective-permute-done.23.other), custom_call_target="tpu_custom_call" | custom-call | flops 393216 | bytes 2359296 | tf_op jit(solution)/shard_map/weight_gradients/pallas_call | solution.py:70
  (56 shorter events, 8.8 us)
Async XLA Ops:
  0.6 8.1 %collective-permute-start.1 = (bf16[512,256]{1,0:T(8,128)(2,1)}, bf16[512,256]{1,0:T(8,128)(2,1)S(1)}, u32[]{:S(2)}, u32[]{:S(2)}) collective-permute-start(bf16[512,256]{1,0:T(8,128)(2,1)} %bitcast.7), channel_id=1, source_target_pairs={{4,8},{6,10},{8,4},{10,6},{5,9},{7,11},{9,5},{11,7},{20,24},{22,26... | collective-permute-start | bytes 786440 | tf_op jit(solution)/shard_map/ppermute | solution.py:59
  1.3 12.1 %collective-permute-start.2 = (bf16[512,256]{1,0:T(8,128)(2,1)}, bf16[512,256]{1,0:T(8,128)(2,1)S(1)}, u32[]{:S(2)}, u32[]{:S(2)}) collective-permute-start(bf16[512,256]{1,0:T(8,128)(2,1)} %bitcast.8), channel_id=1, source_target_pairs={{0,4},{2,6},{8,12},{10,14},{4,0},{6,2},{12,8},{14,10},{1,5},{3,7},... | collective-permute-start | bytes 786440 | tf_op jit(solution)/shard_map/ppermute | solution.py:59
  7.2 10.7 %collective-permute-start = (bf16[512,256]{1,0:T(8,128)(2,1)}, bf16[512,256]{1,0:T(8,128)(2,1)S(1)}, u32[]{:S(2)}, u32[]{:S(2)}) collective-permute-start(bf16[512,256]{1,0:T(8,128)(2,1)} %bitcast.9), channel_id=1, source_target_pairs={{0,2},{2,0},{4,6},{6,4},{8,10},{10,8},{12,14},{14,12},{1,3},{3,1},... | collective-permute-start | bytes 786440 | tf_op jit(solution)/shard_map/ppermute | solution.py:48
  8.8 12.6 %collective-permute-start.4 = (bf16[576,256]{1,0:T(8,128)(2,1)S(1)}, bf16[576,256]{1,0:T(8,128)(2,1)S(1)}, u32[]{:S(2)}, u32[]{:S(2)}) collective-permute-start(bf16[576,256]{1,0:T(8,128)(2,1)S(1)} %pad_maximum_fusion), channel_id=1, source_target_pairs={{8,12},{10,14},{4,0},{6,2},{9,13},{11,15},{5,1},{7,3},{24,28},{26,... | collective-permute-start | bytes 884744 | tf_op jit(solution)/shard_map/ppermute | solution.py:59
  13.5 7.2 %collective-permute-start.3 = (bf16[512,256]{1,0:T(8,128)(2,1)S(1)}, bf16[512,256]{1,0:T(8,128)(2,1)S(1)}, u32[]{:S(2)}, u32[]{:S(2)}) collective-permute-start(bf16[512,256]{1,0:T(8,128)(2,1)S(1)} %broadcast_select_fusion), channel_id=1, source_target_pairs={{0,2},{2,0},{4,6},{6,4},{8,10},{10,8},{12,14},{14,12},{1,3},{3,1},... | collective-permute-start | bytes 786440 | tf_op jit(solution)/shard_map/ppermute | solution.py:48
  15.1 2.9 %collective-permute-start.5 = (bf16[512,256]{1,0:T(8,128)(2,1)S(1)}, bf16[512,256]{1,0:T(8,128)(2,1)S(1)}, u32[]{:S(2)}, u32[]{:S(2)}) collective-permute-start(bf16[512,256]{1,0:T(8,128)(2,1)S(1)} %collective-permute-done.2.first), channel_id=1, source_target_pairs={{4,8},{6,10},{8,4},{10,6},{5,9},{7,11},{9,5},{11,7},{20,24},{22,26... | collective-permute-start | bytes 786440 | tf_op jit(solution)/shard_map/ppermute | solution.py:59
  15.8 1.3 %collective-permute-start.6 = (bf16[64,256]{1,0:T(8,128)(2,1)S(1)}, bf16[64,256]{1,0:T(8,128)(2,1)S(1)}, u32[]{:S(2)}, u32[]{:S(2)}) collective-permute-start(bf16[64,256]{1,0:T(8,128)(2,1)S(1)} %select_bitcast_fusion), channel_id=1, source_target_pairs={{0,1},{1,0},{2,3},{3,2},{4,5},{5,4},{6,7},{7,6},{8,9},{9,8},{10,11... | collective-permute-start | bytes 98312 | tf_op jit(solution)/shard_map/ppermute | solution.py:48
  22.1 1.4 %collective-permute-start.7 = (bf16[2,128,256]{2,1,0:T(8,128)(2,1)S(1)}, bf16[2,128,256]{2,1,0:T(8,128)(2,1)S(1)}, u32[]{:S(2)}, u32[]{:S(2)}) collective-permute-start(bf16[2,128,256]{2,1,0:T(8,128)(2,1)S(1)} %get-tuple-element.44), channel_id=1, source_target_pairs={{0,1},{1,0},{2,3},{3,2},{4,5},{5,4},{6,7},{7,6},{8,9},{9,8},{10,11... | collective-permute-start | bytes 393224 | tf_op jit(solution)/shard_map/ppermute | solution.py:48
  38.6 2.0 %collective-permute-start.9 = (bf16[1024,256]{1,0:T(8,128)(2,1)S(1)}, bf16[1024,256]{1,0:T(8,128)(2,1)S(1)}, u32[]{:S(2)}, u32[]{:S(2)}) collective-permute-start(bf16[1024,256]{1,0:T(8,128)(2,1)S(1)} %get-tuple-element.58), channel_id=1, source_target_pairs={{0,1},{1,0},{2,3},{3,2},{4,5},{5,4},{6,7},{7,6},{8,9},{9,8},{10,11... | collective-permute-start | bytes 1572872 | tf_op jit(solution)/shard_map/ppermute | solution.py:48
  41.5 10.3 %collective-permute-start.16 = (bf16[192,256]{1,0:T(8,128)(2,1)S(1)}, bf16[192,256]{1,0:T(8,128)(2,1)S(1)}, u32[]{:S(2)}, u32[]{:S(2)}) collective-permute-start(bf16[192,256]{1,0:T(8,128)(2,1)S(1)} %get-tuple-element.70), channel_id=1, source_target_pairs={{0,2},{2,0},{4,6},{6,4},{8,10},{10,8},{12,14},{14,12},{1,3},{3,1},... | collective-permute-start | bytes 294920 | tf_op jit(solution)/shard_map/ppermute | solution.py:48
  43.0 9.5 %collective-permute-start.17 = (bf16[192,256]{1,0:T(8,128)(2,1)S(1)}, bf16[192,256]{1,0:T(8,128)(2,1)S(1)}, u32[]{:S(2)}, u32[]{:S(2)}) collective-permute-start(bf16[192,256]{1,0:T(8,128)(2,1)S(1)} %get-tuple-element.71), channel_id=1, source_target_pairs={{0,4},{2,6},{4,0},{6,2},{8,12},{10,14},{12,8},{14,10},{1,5},{3,7},... | collective-permute-start | bytes 294920 | tf_op jit(solution)/shard_map/ppermute | solution.py:48
  46.4 6.1 %collective-permute-start.18 = (bf16[192,256]{1,0:T(8,128)(2,1)S(1)}, bf16[192,256]{1,0:T(8,128)(2,1)S(1)}, u32[]{:S(2)}, u32[]{:S(2)}) collective-permute-start(bf16[192,256]{1,0:T(8,128)(2,1)S(1)} %get-tuple-element.72), channel_id=1, source_target_pairs={{0,6},{2,4},{4,2},{6,0},{8,14},{10,12},{12,10},{14,8},{1,7},{3,5},... | collective-permute-start | bytes 294920 | tf_op jit(solution)/shard_map/ppermute | solution.py:48
  47.3 11.2 %collective-permute-start.10 = (bf16[256,512]{1,0:T(8,128)(2,1)S(1)}, bf16[256,512]{1,0:T(8,128)(2,1)S(1)}, u32[]{:S(2)}, u32[]{:S(2)}) collective-permute-start(bf16[256,512]{1,0:T(8,128)(2,1)S(1)} %get-tuple-element.59), channel_id=1, source_target_pairs={{0,2},{2,0},{4,6},{6,4},{8,10},{10,8},{12,14},{14,12},{1,3},{3,1},... | collective-permute-start | bytes 786440 | tf_op jit(solution)/shard_map/ppermute | solution.py:48
  47.9 10.6 %collective-permute-start.11 = (bf16[256,512]{1,0:T(8,128)(2,1)S(1)}, bf16[256,512]{1,0:T(8,128)(2,1)S(1)}, u32[]{:S(2)}, u32[]{:S(2)}) collective-permute-start(bf16[256,512]{1,0:T(8,128)(2,1)S(1)} %get-tuple-element.60), channel_id=1, source_target_pairs={{0,4},{2,6},{12,8},{14,10},{1,5},{3,7},{13,9},{15,11},{16,20},{18,... | collective-permute-start | bytes 786440 | tf_op jit(solution)/shard_map/ppermute | solution.py:59
  51.8 6.7 %collective-permute-start.12 = (bf16[256,512]{1,0:T(8,128)(2,1)S(1)}, bf16[256,512]{1,0:T(8,128)(2,1)S(1)}, u32[]{:S(2)}, u32[]{:S(2)}) collective-permute-start(bf16[256,512]{1,0:T(8,128)(2,1)S(1)} %get-tuple-element.61), channel_id=1, source_target_pairs={{4,8},{6,10},{8,4},{10,6},{5,9},{7,11},{9,5},{11,7},{20,24},{22,26... | collective-permute-start | bytes 786440 | tf_op jit(solution)/shard_map/ppermute | solution.py:59
  52.6 11.9 %collective-permute-start.19 = (bf16[192,256]{1,0:T(8,128)(2,1)S(1)}, bf16[192,256]{1,0:T(8,128)(2,1)S(1)}, u32[]{:S(2)}, u32[]{:S(2)}) collective-permute-start(bf16[192,256]{1,0:T(8,128)(2,1)S(1)} %add_convert_fusion.1), channel_id=1, source_target_pairs={{0,8},{2,10},{4,12},{6,14},{8,0},{10,2},{12,4},{14,6},{1,9},{3,11}... | collective-permute-start | bytes 294920 | tf_op jit(solution)/shard_map/ppermute | solution.py:48
  55.3 1.2 %collective-permute-start.8 = (bf16[64,256]{1,0:T(8,128)(2,1)S(1)}, bf16[64,256]{1,0:T(8,128)(2,1)S(1)}, u32[]{:S(2)}, u32[]{:S(2)}) collective-permute-start(bf16[64,256]{1,0:T(8,128)(2,1)S(1)} %slice_select_fusion), channel_id=1, source_target_pairs={{0,1},{1,0},{2,3},{3,2},{4,5},{5,4},{6,7},{7,6},{8,9},{9,8},{10,11... | collective-permute-start | bytes 98312 | tf_op jit(solution)/shard_map/ppermute | solution.py:48
  56.5 11.8 %collective-permute-start.15 = (bf16[256,512]{1,0:T(8,128)(2,1)S(1)}, bf16[256,512]{1,0:T(8,128)(2,1)S(1)}, u32[]{:S(2)}, u32[]{:S(2)}) collective-permute-start(bf16[256,512]{1,0:T(8,128)(2,1)S(1)} %get-tuple-element.67), channel_id=1, source_target_pairs={{0,2},{2,0},{4,6},{6,4},{8,10},{10,8},{12,14},{14,12},{1,3},{3,1},... | collective-permute-start | bytes 786440 | tf_op jit(solution)/shard_map/ppermute | solution.py:48
  58.7 11.5 %collective-permute-start.13 = (bf16[256,512]{1,0:T(8,128)(2,1)S(1)}, bf16[256,512]{1,0:T(8,128)(2,1)S(1)}, u32[]{:S(2)}, u32[]{:S(2)}) collective-permute-start(bf16[256,512]{1,0:T(8,128)(2,1)S(1)} %get-tuple-element.65), channel_id=1, source_target_pairs={{0,4},{2,6},{8,12},{10,14},{4,0},{6,2},{12,8},{14,10},{1,5},{3,7},... | collective-permute-start | bytes 786440 | tf_op jit(solution)/shard_map/ppermute | solution.py:59
  63.8 6.5 %collective-permute-start.14 = (bf16[256,512]{1,0:T(8,128)(2,1)S(1)}, bf16[256,512]{1,0:T(8,128)(2,1)S(1)}, u32[]{:S(2)}, u32[]{:S(2)}) collective-permute-start(bf16[256,512]{1,0:T(8,128)(2,1)S(1)} %get-tuple-element.66), channel_id=1, source_target_pairs={{4,8},{6,10},{8,4},{10,6},{5,9},{7,11},{9,5},{11,7},{20,24},{22,26... | collective-permute-start | bytes 786440 | tf_op jit(solution)/shard_map/ppermute | solution.py:59
  64.5 7.3 %collective-permute-start.22 = (bf16[192,256]{1,0:T(8,128)(2,1)S(1)}, bf16[192,256]{1,0:T(8,128)(2,1)S(1)}, u32[]{:S(2)}, u32[]{:S(2)}) collective-permute-start(bf16[192,256]{1,0:T(8,128)(2,1)S(1)} %add_convert_fusion.own), channel_id=1, source_target_pairs={{0,6},{2,4},{4,2},{6,0},{8,14},{10,12},{12,10},{14,8},{1,7},{3,5},... | collective-permute-start | bytes 294920 | tf_op jit(solution)/shard_map/ppermute | solution.py:48
  68.3 4.6 %collective-permute-start.21 = (bf16[192,256]{1,0:T(8,128)(2,1)S(1)}, bf16[192,256]{1,0:T(8,128)(2,1)S(1)}, u32[]{:S(2)}, u32[]{:S(2)}) collective-permute-start(bf16[192,256]{1,0:T(8,128)(2,1)S(1)} %add_convert_fusion.own), channel_id=1, source_target_pairs={{0,4},{2,6},{4,0},{6,2},{8,12},{10,14},{12,8},{14,10},{1,5},{3,7},... | collective-permute-start | bytes 294920 | tf_op jit(solution)/shard_map/ppermute | solution.py:48
  68.3 4.6 %collective-permute-start.20 = (bf16[192,256]{1,0:T(8,128)(2,1)S(1)}, bf16[192,256]{1,0:T(8,128)(2,1)S(1)}, u32[]{:S(2)}, u32[]{:S(2)}) collective-permute-start(bf16[192,256]{1,0:T(8,128)(2,1)S(1)} %add_convert_fusion.own), channel_id=1, source_target_pairs={{0,2},{2,0},{4,6},{6,4},{8,10},{10,8},{12,14},{14,12},{1,3},{3,1},... | collective-permute-start | bytes 294920 | tf_op jit(solution)/shard_map/ppermute | solution.py:48
  73.0 1.8 %collective-permute-start.23 = (bf16[768,256]{1,0:T(8,128)(2,1)S(1)}, bf16[768,256]{1,0:T(8,128)(2,1)S(1)}, u32[]{:S(2)}, u32[]{:S(2)}) collective-permute-start(bf16[768,256]{1,0:T(8,128)(2,1)S(1)} %pieces.1.own), channel_id=1, source_target_pairs={{0,1},{1,0},{2,3},{3,2},{4,5},{5,4},{6,7},{7,6},{8,9},{9,8},{10,11... | collective-permute-start | bytes 1179656 | tf_op jit(solution)/shard_map/ppermute | solution.py:48
  (8 other events, 44.6 us)
